TPU v7x, 256 devices: a whole 4x4x8 slice. The times are simulated.
256 devices in a mesh: dp: 64 (over z_hi, y, x, core), tensor: 4 (over z_lo).
Axes of the slice: x: 4, y: 4, z: 8 (z_hi: 2, z_lo: 4; z = z_hi * 4 + z_lo), core: 2. Of those that a mesh axis runs over, the one named last changes fastest.
Arguments:
- projection_input: bfloat16 [32768, 8192], P(('dp', 'tensor')), may hold values from -24 to 24
- rank_activations: bfloat16 [32768, 256], P('dp'), may hold values from -16 to 16
- projection_output_gradient: bfloat16 [32768, 8192], P('dp', 'tensor'), may hold values from -6 to 6
- down_factor: bfloat16 [8192, 256], replicated, may hold values from -0.375 to 0.375
- up_factor: bfloat16 [256, 8192], P(None, 'tensor'), may hold values from -0.0625 to 0.0625
- sparse_block_values: bfloat16 [4, 64, 64, 64], P('tensor'), may hold values from -0.75 to 0.75
- slot_block_rows: int32 [4, 64], P('tensor'), may hold values from 0 to 127, as said below
- slot_block_columns: int32 [4, 64], P('tensor'), may hold values from 0 to 31, as said below
- shard_block_count: int32 [4], P('tensor'), may hold values from 16 to 64, as said below
Outputs:
- grad_down: float32 [8192, 256], P('dp')
- up_factor_gradient: float32 [256, 8192], P('dp', 'tensor')
- grad_delta: float32 [4, 64, 64, 64], P('tensor')
- grad_input: bfloat16 [32768, 8192], P(('dp', 'tensor'))
Inputs may be any that keep to these rules, and one draw needn't show every extreme that they name: `slot_block_rows`: within a shard no two slots name the same block (same row and column). `slot_block_columns`: columns count blocks inside the shard's own 8192 / 4 outputs. `shard_block_count`: some shard uses all 64 slots in every draw.
All inputs are finite; a program needn't handle non-finite values.
Results may differ from a plain program's by a relative error of at most 0.017.
Values may be sent and summed in bfloat16 or wider, within the bound.
No kernel may reach another device: no remote copies, remote signals or barrier semaphores. Data moves between devices by JAX's collectives and lax.ppermute only.
A program may use at most 128 MiB of HBM per device.

v0:
```python
import jax
import jax.numpy as jnp
from jax import lax
from jax.sharding import PartitionSpec as P


def place_rows(spread, pick_table, form):
    high_part = spread.astype(jnp.bfloat16)
    low_part = (spread - high_part.astype(jnp.float32)).astype(jnp.bfloat16)
    placed = jnp.einsum(form, high_part, pick_table, preferred_element_type=jnp.float32)
    return placed + jnp.einsum(form, low_part, pick_table, preferred_element_type=jnp.float32)


def per_device(
    projection_input,
    rank_activations,
    projection_output_gradient,
    down_factor,
    up_factor,
    sparse_block_values,
    slot_block_rows,
    slot_block_columns,
    shard_block_count,
):
    full_rows = lax.all_gather(projection_input, "tensor", axis=0, tiled=True)
    tok_count = full_rows.shape[0]
    feat_width = full_rows.shape[1]
    block_size = sparse_block_values.shape[2]
    slot_count = sparse_block_values.shape[1]
    row_blocks = feat_width // block_size
    col_blocks = projection_output_gradient.shape[1] // block_size
    own_rows = projection_input.shape[0]
    part_low = lax.dot_general(
        projection_output_gradient,
        up_factor,
        (((1,), (1,)), ((), ())),
        preferred_element_type=jnp.float32,
    )
    low_all = lax.psum(part_low.astype(jnp.bfloat16), "tensor")
    rank_local_part = lax.dynamic_slice_in_dim(
        low_all, lax.axis_index("tensor") * own_rows, own_rows, 0
    )
    grad_down = lax.psum_scatter(
        lax.dot_general(
            full_rows, low_all, (((0,), (0,)), ((), ())), preferred_element_type=jnp.float32
        ),
        "dp",
        scatter_dimension=0,
        tiled=True,
    )
    up_factor_gradient = lax.psum_scatter(
        lax.dot_general(
            rank_activations,
            projection_output_gradient,
            (((0,), (0,)), ((), ())),
            preferred_element_type=jnp.float32,
        ),
        "dp",
        scatter_dimension=0,
        tiled=True,
    )
    rows_here = slot_block_rows[0]
    cols_here = slot_block_columns[0]
    live_mask = (jnp.arange(slot_count) < shard_block_count[0]).astype(jnp.float32)
    pick_rows = (rows_here[:, None] == jnp.arange(row_blocks)[None, :]).astype(jnp.bfloat16)
    pick_cols = (cols_here[:, None] == jnp.arange(col_blocks)[None, :]).astype(jnp.bfloat16)
    input_pick = jnp.einsum(
        "nrk,sr->snk",
        full_rows.reshape(tok_count, row_blocks, block_size),
        pick_rows,
        preferred_element_type=jnp.float32,
    ).astype(jnp.bfloat16)
    grad_pick = jnp.einsum(
        "ncj,sc->snj",
        projection_output_gradient.reshape(tok_count, col_blocks, block_size),
        pick_cols,
        preferred_element_type=jnp.float32,
    ).astype(jnp.bfloat16)
    local_delta = (
        jnp.einsum("snk,snj->skj", input_pick, grad_pick, preferred_element_type=jnp.float32)
        * live_mask[:, None, None]
    )
    grad_delta = lax.psum(local_delta, "dp")[None]
    spread = (
        jnp.einsum(
            "snj,skj->snk", grad_pick, sparse_block_values[0], preferred_element_type=jnp.float32
        )
        * live_mask[:, None, None]
    )
    dense_part = lax.dot_general(
        rank_local_part, down_factor, (((1,), (1,)), ((), ())), preferred_element_type=jnp.float32
    )
    partial_value = place_rows(spread, pick_rows, "snk,sr->nrk").reshape(tok_count, feat_width)
    summed = lax.psum_scatter(
        partial_value.astype(jnp.bfloat16), "tensor", scatter_dimension=0, tiled=True
    ).astype(jnp.float32)
    grad_input = (dense_part + summed).astype(jnp.bfloat16)
    return (grad_down, up_factor_gradient, grad_delta, grad_input)


def solution(mesh):
    return jax.shard_map(
        per_device,
        mesh=mesh,
        in_specs=(
            P(("dp", "tensor"), None),
            P("dp", None),
            P("dp", "tensor"),
            P(),
            P(None, "tensor"),
            P("tensor", None, None, None),
            P("tensor", None),
            P("tensor", None),
            P("tensor"),
        ),
        out_specs=(
            P("dp", None),
            P("dp", "tensor"),
            P("tensor", None, None, None),
            P(("dp", "tensor"), None),
        ),
        check_vma=False,
    )
```

profile of v0, /device:TPU:1, one launch (start us, length us, event | category | flops | bytes accessed | tf_op | source)
XLA Modules:
  0.0 1602.2 jit_solution(12746619665061689151)
XLA Ops:
  7.2 0.0 all-gather.2.cloned.1.call-start
  7.2 4.2 copy.30
  11.5 0.0 all-gather.2.cloned.1.call-update
  11.5 0.0 all-reduce.5.cloned.1.call-start
  11.6 2.7 convolution_convert_fusion.1
  14.3 0.0 all-reduce.5.cloned.1.call-update
  14.3 0.0 all-reduce.7.cloned.1.call-start
  14.3 2.9 copy.32
  17.2 3.6 fusion.33
  21.6 3.7 convolution_convert_fusion
  25.2 145.2 %all-gather.2.cloned.1.call-done = bf16[512,8192]{0,1:T(8,128)(2,1)} async-done(((bf16[128,8192]{0,1:T(8,128)(2,1)}), bf16[512,8192]{0,1:T(8,128)(2,1)}) %all-gather.2.cloned.1.call-update) | async-done | bytes 8388624 | tf_op jit(solution)/shard_map/all_gather | solution.py:25
  170.4 13.4 fusion.12
  183.8 6.2 multiply_bitcast_fusion
  190.1 0.0 all-reduce.7.cloned.1.call-update
  190.1 0.0 reduce-scatter.5.cloned.1.call-start
  190.2 7.9 subtract_convert_fusion
  198.1 12.0 fusion.5
  210.2 12.9 fusion.3
  223.1 11.4 copy.39
  234.4 11.5 copy.40
  246.0 0.3 reduce-scatter.3.cloned.1.call-start
  246.2 0.0 all-reduce.5.cloned.1.call-done
  246.2 9.2 convolution_bitcast_fusion
  255.5 0.6 copy-done.8
  256.1 0.6 dynamic-slice
  257.3 760.4 %all-reduce.7.cloned.1.call-done = (f32[256,2048]{1,0:T(8,128)}, f32[1,64,64,64]{3,2,1,0:T(8,128)}) async-done(((f32[256,2048]{1,0:T(8,128)}, f32[1,64,64,64]{3,2,1,0:T(8,128)}), (f32[256,2048]{1,0:T(8,128)}, f32[1,64,64,64]{3,2,1,0:T(8,128)})) %all-reduce.7.cloned.1.call-update) | async-done | bytes 3145744
  1017.8 1.5 constant_dynamic-slice_fusion
  1019.2 151.2 %reduce-scatter.5.cloned.1.call-done = bf16[128,8192]{1,0:T(8,128)(2,1)} async-done(((bf16[512,8192]{1,0:T(8,128)(2,1)}), bf16[128,8192]{1,0:T(8,128)(2,1)}) %reduce-scatter.5.cloned.1.call-update) | async-done | bytes 2097168 | tf_op jit(solution)/shard_map/reduce_scatter | solution.py:94
  1170.4 5.8 fusion
  1176.2 416.2 %reduce-scatter.3.cloned.1.call-done = f32[128,256]{0,1:T(8,128)} async-done(((f32[8192,256]{0,1:T(8,128)}), f32[128,256]{0,1:T(8,128)}) %reduce-scatter.3.cloned.1.call-update) | async-done | bytes 131088 | tf_op jit(solution)/shard_map/reduce_scatter | solution.py:43
  1592.4 1.7 copy.41
  1594.1 1.3 copy.68
  (20 shorter events, 0.1 us)
Async XLA Ops:
  7.2 183.0 %copy-start = (bf16[1,64,64,64]{3,2,1,0:T(8,128)(2,1)S(1)}, bf16[1,64,64,64]{3,2,1,0:T(8,128)(2,1)}, u32[]{:S(2)}) copy-start(bf16[1,64,64,64]{3,2,1,0:T(8,128)(2,1)} %param.14) | copy-start | bytes 1572868
  7.2 4.4 copy-start.3
  7.2 163.2 %all-gather.2.cloned.1.call-start = ((), (), s32[]{:S(2)}) async-start(), calls=%async_computation.3 | async-start | bytes 10485760 | tf_op jit(solution)/shard_map/all_gather | solution.py:25
  11.5 5.7 copy-start.5
  11.5 234.7 %all-reduce.5.cloned.1.call-start = ((), (), s32[]{:S(2)}) async-start(), calls=%async_computation.2 | async-start | bytes 524288 | tf_op jit(solution)/shard_map/psum | solution.py:39
  14.3 7.3 copy-start.7
  14.3 1003.5 %all-reduce.7.cloned.1.call-start = ((), (), s32[]{:S(2)}) async-start(), calls=%async_computation.6 | async-start | bytes 8388608
  20.9 149.6 %copy-start.6 = (s32[1,64]{1,0:T(1,128)S(1)}, s32[1,64]{1,0:T(1,128)}, u32[]{:S(2)}) copy-start(s32[1,64]{1,0:T(1,128)} %param.15) | copy-start | bytes 772
  170.4 13.4 copy-start.2
  190.1 980.3 %reduce-scatter.5.cloned.1.call-start = ((), (), s32[]{:S(2)}) async-start(), calls=%async_computation.5 | async-start | bytes 10485760 | tf_op jit(solution)/shard_map/reduce_scatter | solution.py:94
  246.0 1346.5 %reduce-scatter.3.cloned.1.call-start = ((), (), s32[]{:S(2)}) async-start(), calls=%async_computation.4 | async-start | bytes 8519680 | tf_op jit(solution)/shard_map/reduce_scatter | solution.py:43
  255.4 0.7 copy-start.8
  1019.2 574.8 %copy-start.4 = (f32[1,64,64,64]{3,2,1,0:T(8,128)S(1)}, f32[1,64,64,64]{3,2,1,0:T(8,128)}, u32[]{:S(2)}) copy-start(f32[1,64,64,64]{3,2,1,0:T(8,128)} %get-tuple-element.22) | copy-start | bytes 3145732
  1170.4 425.0 %copy-start.1 = (bf16[1,64,64,64]{3,2,1,0:T(8,128)(2,1)S(1)}, bf16[1,64,64,64]{3,2,1,0:T(8,128)(2,1)}, u32[]{:S(2)}) copy-start(bf16[1,64,64,64]{3,2,1,0:T(8,128)(2,1)} %param.14) | copy-start | bytes 1572868
Sparse Core Ops, SparseCore 0:
  11.6 158.7 all-gather.1
  173.1 44.9 all-reduce.4
  221.5 796.2 all-reduce.6
  1020.2 150.1 reduce-scatter.4
  1172.8 419.5 reduce-scatter.2
where the time goes:
time: 1620 us; the launch traced here: 1600 us
  waiting for transfers between devices  1470 us (91%)
  matrix products  77.5 us (5%)
  local copies, waits for them, and re-layouts  35.7 us (2%)
    unnamed x6, waiting for transfers between devices  761 us
    reduce_scatter x1, waiting for transfers between devices, per_device(): lax.psum_scatter(lax.dot_general(full_rows, low_all, (((0,), (0,)), ((),...  416 us
    reduce_scatter x1, waiting for transfers between devices, per_device(): lax.psum_scatter(partial_value.astype(jnp.bfloat16), 'tensor', scatter_di...  151 us
    all_gather x1, waiting for transfers between devices, per_device(): full_rows = lax.all_gather(projection_input, 'tensor', axis=0, tiled=True)  145 us
  transfers between devices with their start and end apart: 5, of which 4 were waited for; matrix products, arithmetic and copies ran while one was open for 7% of the time, Pallas kernels for 0%

commit v1 on v0

v1 whole, which is shorter than its diff:
```python
import functools

import jax
import jax.numpy as jnp
from jax import lax
from jax.experimental import pallas as pl
from jax.experimental.pallas import tpu as pltpu
from jax.sharding import Mesh, PartitionSpec as P

F32 = jnp.float32
BF16 = jnp.bfloat16
ZH, Y, X, C, T = 2, 4, 4, 2, 4
XY = Y * X
DP = ("zh", "y", "x", "c")
ALL = DP + ("t",)
BLK = 64
TOK = 128
PAIRS = 32
VMEM_LIMIT = 48 * 1024 * 1024


def block_rows(ref, index):
    return ref[pl.ds(pl.multiple_of(index * BLK, BLK), BLK), :]


def delta_kernel(rows, cols, cnt, x_ref, g_ref, out_ref, gt_ref, xt_ref):
    def turn(i, carry):
        at = pl.multiple_of(i * 128, 128)
        xt_ref[pl.ds(at, 128), :] = x_ref[:, pl.ds(at, 128)].T
        return carry

    lax.fori_loop(0, x_ref.shape[1] // 128, turn, 0, unroll=4)
    width = g_ref.shape[2]
    for t in range(T):

        def turn_g(i, carry):
            at = pl.multiple_of(i * 128, 128)
            gt_ref[pl.ds(t * width + at, 128), :] = g_ref[t, :, pl.ds(at, 128)].T
            return carry

        lax.fori_loop(0, width // 128, turn_g, 0, unroll=4)

    lane = lax.broadcasted_iota(jnp.int32, (BLK, 2 * BLK), 1)
    per_shard = width // BLK

    def pair(p, carry):
        for t in range(T):
            s0, s1 = p, p + PAIRS
            xt = jnp.concatenate(
                [block_rows(xt_ref, rows[t, s0]), block_rows(xt_ref, rows[t, s1])], axis=0
            )
            gt = jnp.concatenate(
                [
                    block_rows(gt_ref, cols[t, s0] + t * per_shard),
                    block_rows(gt_ref, cols[t, s1] + t * per_shard),
                ],
                axis=0,
            )
            full = lax.dot_general(xt, gt, (((1,), (1,)), ((), ())), preferred_element_type=F32)
            live = jnp.where(lane < BLK, s0, s1) < cnt[t, 0]
            both = jnp.where(lane < BLK, full[:BLK], full[BLK:])
            out_ref[p, t] = jnp.where(live, both, 0.0).astype(BF16)
        return carry

    lax.fori_loop(0, PAIRS, pair, 0, unroll=2)


def input_kernel(rows, cols, cnt, low_ref, down_ref, gt_ref, v_ref, out_ref, acc_ref):
    low = low_ref[...]
    step = 512

    def dense(i, carry):
        at = pl.multiple_of(i * step, step)
        acc_ref[pl.ds(at, step), :] = lax.dot_general(
            down_ref[pl.ds(at, step), :], low, (((1,), (1,)), ((), ())), preferred_element_type=F32
        )
        return carry

    lax.fori_loop(0, acc_ref.shape[0] // step, dense, 0, unroll=2)
    lane = lax.broadcasted_iota(jnp.int32, (BLK, 2 * BLK), 1)
    per_shard = gt_ref.shape[0] // T // BLK

    def pair(p, carry):
        s0, s1 = p, p + PAIRS
        parts = []
        for t in range(T):
            v = v_ref[t, p]
            zero = jnp.zeros_like(v)
            top = jnp.where((lane < BLK) & (s0 < cnt[t, 0]), v, zero)
            bottom = jnp.where((lane >= BLK) & (s1 < cnt[t, 0]), v, zero)
            gt = jnp.concatenate(
                [
                    block_rows(gt_ref, cols[t, s0] + t * per_shard),
                    block_rows(gt_ref, cols[t, s1] + t * per_shard),
                ],
                axis=0,
            )
            parts.append(
                jnp.dot(
                    jnp.concatenate([top, bottom], axis=0), gt, preferred_element_type=F32
                )
            )
        for t in range(T):
            for s, part in ((s0, parts[t][:BLK]), (s1, parts[t][BLK:])):
                at = pl.ds(pl.multiple_of(rows[t, s] * BLK, BLK), BLK)
                acc_ref[at, :] = acc_ref[at, :] + part
        return carry

    lax.fori_loop(0, PAIRS, pair, 0, unroll=2)

    def turn(i, carry):
        at = pl.multiple_of(i * 128, 128)
        out_ref[:, pl.ds(at, 128)] = acc_ref[pl.ds(at, 128), :].T.astype(BF16)
        return carry

    lax.fori_loop(0, acc_ref.shape[0] // 128, turn, 0, unroll=4)


def whole():
    return pl.BlockSpec(memory_space=pltpu.VMEM)


def scalars():
    return pl.BlockSpec(memory_space=pltpu.SMEM)


def ring(shift_of_core):
    def place(z, c):
        return (z // T * C + c) * T + z % T

    n = ZH * T
    return [
        (place(z, c), place((z + shift_of_core[c]) % n, c)) for z in range(n) for c in range(C)
    ]


def swap(array):
    return lax.ppermute(array, "c", [(0, 1), (1, 0)])


def per_device(x_own, acts, grad, down, up, values, slot_rows, slot_cols, count):
    c = lax.axis_index("c")
    t = lax.axis_index("t")
    feat = x_own.shape[1]
    width = grad.shape[1]
    rank = up.shape[0]

    grad_own = lax.all_to_all(grad.reshape(T, TOK, width), "t", 0, 0, tiled=True)

    table = jnp.concatenate(
        [slot_rows, slot_cols, jnp.broadcast_to(count[:, None], (1, 128))], axis=1
    )
    tables = lax.all_gather(table, "t", axis=0, tiled=True)
    rows4, cols4, cnt4 = tables[:, :64], tables[:, 64:128], tables[:, 128:]

    packed = jnp.concatenate([values[0, :PAIRS], values[0, PAIRS:]], axis=2)
    half = lax.dynamic_slice_in_dim(packed, c * (PAIRS // C), PAIRS // C, 0)
    axes = ("zh", "c", "t")
    from_prev = lax.ppermute(half, axes, ring((1, 1)))
    from_next = lax.ppermute(half, axes, ring((-1, -1)))
    from_far = lax.ppermute(half, axes, ring((2, -2)))
    got = jnp.stack([from_prev, from_far, from_next])
    got_too = swap(got)
    others = jnp.where(c == 0, jnp.concatenate([got, got_too], 1), jnp.concatenate([got_too, got], 1))
    ordered = jnp.concatenate([packed[None], others], 0)
    values4 = jnp.take(ordered, (t - jnp.arange(T)) % T, axis=0)

    x_view = x_own.reshape(TOK, ZH, Y, X, C, 128)
    x_keep = lax.dynamic_index_in_dim(x_view, c, 4, keepdims=False)
    x_give = lax.dynamic_index_in_dim(x_view, 1 - c, 4, keepdims=False)
    x_got = swap(x_give)

    low_part = lax.dot_general(grad, up, (((1,), (1,)), ((), ())), preferred_element_type=F32)
    low_parts = lax.all_to_all(
        low_part.astype(BF16).reshape(T, TOK, rank), "t", 0, 0, tiled=True
    )
    low = jnp.sum(low_parts.astype(F32), axis=0).astype(BF16)
    low_got = swap(low)

    acts_view = acts.reshape(acts.shape[0], ZH, XY, C, 4).transpose(0, 3, 2, 1, 4)
    up_part = lax.dot_general(
        acts_view.reshape(acts.shape[0], rank), grad, (((0,), (0,)), ((), ())),
        preferred_element_type=F32,
    ).astype(BF16).reshape(C, XY, ZH * 4, width)
    up_keep = lax.dynamic_index_in_dim(up_part, c, 0, keepdims=False)
    up_got = swap(lax.dynamic_index_in_dim(up_part, 1 - c, 0, keepdims=False))
    up_half = (up_keep.astype(F32) + up_got.astype(F32)).astype(BF16)
    up_sum = jnp.sum(
        lax.all_to_all(up_half, ("y", "x"), 0, 0, tiled=True).astype(F32), axis=0
    ).reshape(ZH, 4, width)
    zh = lax.axis_index("zh")
    up_far = lax.ppermute(
        lax.dynamic_index_in_dim(up_sum, 1 - zh, 0, keepdims=False), "zh", [(0, 1), (1, 0)]
    )
    up_grad = lax.dynamic_index_in_dim(up_sum, zh, 0, keepdims=False) + up_far

    form = "nzyxk,nr->yxzkr"
    down_part = jnp.einsum(form, x_keep, low, preferred_element_type=F32) + jnp.einsum(
        form, x_got, low_got, preferred_element_type=F32
    )
    down_part = down_part.astype(BF16).reshape(XY, ZH * 128, rank)
    down_sum = jnp.sum(
        lax.all_to_all(down_part, ("y", "x"), 0, 0, tiled=True).astype(F32), axis=0
    ).astype(BF16).reshape(ZH, 1, 128, rank)
    down_all = lax.all_to_all(
        jnp.broadcast_to(down_sum, (ZH, T, 128, rank)).reshape(ZH * T, 128, rank),
        ("zh", "t"), 0, 0, tiled=True,
    )
    down_grad = jnp.sum(down_all.astype(F32), axis=0)

    params = pltpu.CompilerParams(vmem_limit_bytes=VMEM_LIMIT)
    delta_part, grad_t = pl.pallas_call(
        delta_kernel,
        out_shape=(
            jax.ShapeDtypeStruct((PAIRS, T, BLK, 2 * BLK), BF16),
            jax.ShapeDtypeStruct((T * width, TOK), BF16),
        ),
        in_specs=[scalars()] * 3 + [whole()] * 2,
        out_specs=(whole(), whole()),
        scratch_shapes=[pltpu.VMEM((feat, TOK), BF16)],
        compiler_params=params,
        cost_estimate=pl.CostEstimate(flops=4 << 30, bytes_accessed=8 << 20, transcendentals=0),
        name="delta",
    )(rows4, cols4, cnt4, x_own, grad_own)
    delta_view = delta_part.reshape(XY, C, T * BLK, 2 * BLK)
    delta_keep = lax.dynamic_index_in_dim(delta_view, c, 1, keepdims=False)
    delta_got = swap(lax.dynamic_index_in_dim(delta_view, 1 - c, 1, keepdims=False))
    delta_half = (delta_keep.astype(F32) + delta_got.astype(F32)).astype(BF16)
    delta_sum = jnp.sum(
        lax.all_to_all(delta_half, ("y", "x"), 0, 0, tiled=True).astype(F32), axis=0
    ).astype(BF16).reshape(1, T, BLK, 2 * BLK)
    delta_all = lax.all_to_all(
        jnp.broadcast_to(delta_sum, (ZH, T, BLK, 2 * BLK)).reshape(ZH * T, BLK, 2 * BLK),
        ("zh", "t"), 0, 0, tiled=True,
    )
    delta_one = jnp.sum(delta_all.astype(F32), axis=0, keepdims=True).astype(BF16)
    delta_full = lax.all_gather(delta_one, ("y", "x", "c"), axis=0, tiled=True).astype(F32)
    grad_delta = jnp.concatenate([delta_full[:, :, :BLK], delta_full[:, :, BLK:]], 0)[None]

    grad_input = pl.pallas_call(
        input_kernel,
        out_shape=jax.ShapeDtypeStruct((TOK, feat), BF16),
        in_specs=[scalars()] * 3 + [whole()] * 4,
        out_specs=whole(),
        scratch_shapes=[pltpu.VMEM((feat, TOK), F32)],
        compiler_params=params,
        cost_estimate=pl.CostEstimate(flops=5 << 30, bytes_accessed=12 << 20, transcendentals=0),
        name="grad_input",
    )(rows4, cols4, cnt4, low, down, grad_t, values4)
    return down_grad, up_grad, grad_delta, grad_input


def solution(mesh):
    fine = Mesh(mesh.devices.reshape(ZH, Y, X, C, T), ALL)
    return jax.shard_map(
        per_device,
        mesh=fine,
        in_specs=(
            P(ALL, None),
            P(DP, None),
            P(DP, "t"),
            P(),
            P(None, "t"),
            P("t", None, None, None),
            P("t", None),
            P("t", None),
            P("t"),
        ),
        out_specs=(
            P(DP, None),
            P(DP, "t"),
            P("t", None, None, None),
            P(ALL, None),
        ),
        check_vma=False,
    )
```

time: 1620 us -> 235 us (0.15); the launches traced: 1600 us -> 234 us
  waiting for transfers between devices: 1470 us -> 38.5 us
  matrix products: 77.5 us -> 7.92 us
  starting transfers between devices: 0.42 us -> 57.5 us
  blocking collectives: 0 us -> 53 us
  Pallas kernels: 0 us -> 22 us
  other arithmetic: 0.01 us -> 21.5 us
    unnamed x6 -> x0, waiting for transfers between devices: 761 us -> none
    reduce_scatter x2 -> x0, waiting for transfers between devices: 567 us -> none  [the longest x1 416 us: per_device(): lax.psum_scatter(lax.dot_general(full_rows, low_all, (((0,), (0,)), ((),...]
    all_gather x1 -> x0, waiting for transfers between devices: 145 us -> none  [per_device(): full_rows = lax.all_gather(projection_input, 'tensor', axis=0, tiled=True)]
    dot_general x10 -> x2, matrix products: 77.5 us -> 5.34 us  [the longest x1 3.04 us: per_device(): lax.dot_general(grad, up, (((1,), (1,)), ((), ())), preferred_element_typ...]
    all_gather x0 -> x2, blocking collectives: none -> 37 us  [the longest x1 24.2 us: per_device(): lax.all_gather(delta_one, ('y', 'x', 'c'), axis=0, tiled=True).astype(F32)]
    ppermute x0 -> x9, starting transfers between devices: none -> 30.5 us  [the longest x5 14.8 us: swap(): return lax.ppermute(array, 'c', [(0, 1), (1, 0)])]
    all_to_all x0 -> x6, starting transfers between devices: none -> 27.1 us  [the longest x1 6.61 us: per_device(): lax.all_to_all(delta_half, ('y', 'x'), 0, 0, tiled=True).astype(F32)]
    all_to_all x0 -> x6, waiting for transfers between devices: none -> 27 us  [the longest x1 9.32 us: per_device(): lax.all_to_all(jnp.broadcast_to(down_sum, (ZH, T, 128, rank)).reshape(ZH...]
  transfers between devices with their start and end apart: 5 -> 15, of which waited for: 4 -> 8; matrix products, arithmetic and copies ran while one was open for 7% -> 22% of each run, Pallas kernels for 0% -> 9%
where the time goes in v1:
time: 235 us; the launch traced here: 234 us
  starting transfers between devices  57.5 us (24%)
  blocking collectives  53 us (23%)
  waiting for transfers between devices  38.5 us (16%)
  local copies, waits for them, and re-layouts  31.7 us (13%)
  Pallas kernels  22 us (9%)
  other arithmetic  21.5 us (9%)
  matrix products  7.92 us (3%)
    all_gather x1, blocking collectives, per_device(): lax.all_gather(delta_one, ('y', 'x', 'c'), axis=0, tiled=True).astype(F32)  24.2 us
    all_to_all x1, blocking collectives, per_device(): lax.all_to_all(up_half, ('y', 'x'), 0, 0, tiled=True).astype(F32)  15.9 us
    ppermute x5, starting transfers between devices, swap(): return lax.ppermute(array, 'c', [(0, 1), (1, 0)])  14.8 us
    all_gather x1, blocking collectives, per_device(): tables = lax.all_gather(table, 't', axis=0, tiled=True)  12.9 us
    unnamed x28, local copies, waits for them, and re-layouts  12.3 us
    pallas_call x1, Pallas kernels, per_device(): pl.pallas_call(input_kernel, out_shape=jax.ShapeDtypeStruct((TOK, feat),...  11.8 us
    ppermute x1, starting transfers between devices, per_device(): from_next = lax.ppermute(half, axes, ring((-1, -1)))  11.7 us
    pallas_call x1, Pallas kernels, per_device(): pl.pallas_call(delta_kernel, out_shape=(jax.ShapeDtypeStruct((PAIRS, T, B...  10.2 us
  transfers between devices with their start and end apart: 15, of which 8 were waited for; matrix products, arithmetic and copies ran while one was open for 22% of the time, Pallas kernels for 9%

profile of v1, /device:TPU:1, one launch (start us, length us, event | category | flops | bytes accessed | tf_op | source)
XLA Modules:
  0.0 233.7 jit_solution(10066507306800102138)
XLA Ops:
  2.1 2.3 convolution_convert_fusion
  4.4 3.3 %collective-permute-start.2 = (bf16[16,8,2048]{2,1,0:T(8,128)(2,1)S(1)}, bf16[16,8,2048]{2,1,0:T(8,128)(2,1)S(1)}, u32[]{:S(2)}, u32[]{:S(2)}) collective-permute-start(bf16[16,8,2048]{2,1,0:T(8,128)(2,1)S(1)} %dynamic-slice_bitcast_fusion.1), channel_id=1, source_target_pairs={{0,4},{4,0},{1,5},{5,1},{2,6},{6,2},{3,7},{7,3},{8,12},{12,8},{9,1... | collective-permute-start | bytes 1572872 | tf_op jit(solution)/shard_map/ppermute | solution.py:138
  7.8 3.0 %convolution_convert_fusion.1 = bf16[512,256]{1,0:T(8,128)(2,1)} fusion(bf16[512,2048]{1,0:T(8,128)(2,1)} %param.11, bf16[256,2048]{1,0:T(8,128)(2,1)S(1)} %copy-done), kind=kOutput, calls=%fused_computation.10 | convolution fusion | flops 537001984 | bytes 3407872 | tf_op jit(solution)/shard_map/dot_general | solution.py:173
  10.8 3.9 %all-to-all-start = ((bf16[4,128,256]{2,1,0:T(8,128)(2,1)}), bf16[4,128,256]{2,1,0:T(8,128)(2,1)S(1)}, u32[]{:S(2)}, u32[]{:S(2)}) async-start(bf16[4,128,256]{2,1,0:T(8,128)(2,1)} %bitcast.81), calls=%async_computation | async-start | bytes 524288 | tf_op jit(solution)/shard_map/all_to_all | solution.py:174
  14.8 7.4 %all-to-all-done = bf16[4,128,256]{2,1,0:T(8,128)(2,1)S(1)} async-done(((bf16[4,128,256]{2,1,0:T(8,128)(2,1)}), bf16[4,128,256]{2,1,0:T(8,128)(2,1)S(1)}, u32[]{:S(2)}, u32[]{:S(2)}) %all-to-all-start) | async-done | bytes 262176 | tf_op jit(solution)/shard_map/all_to_all | solution.py:174
  22.2 15.9 %all_to_all.35 = bf16[16,8,2048]{2,1,0:T(8,128)(2,1)} all-to-all(bf16[16,8,2048]{2,1,0:T(8,128)(2,1)S(1)} %fusion.2), channel_id=1, replica_groups=mesh['zh'=2,'y'=4,'x'=4,'c'=2,'t'=4] {'y','x'}, dimensions={0} | all-to-all | bytes 1048576 | tf_op jit(solution)/shard_map/all_to_all | solution.py:189
  38.1 4.4 %all-to-all-start.4 = ((bf16[4,128,2048]{2,1,0:T(8,128)(2,1)}), bf16[4,128,2048]{2,1,0:T(8,128)(2,1)}, u32[]{:S(2)}, u32[]{:S(2)}) async-start(bf16[4,128,2048]{2,1,0:T(8,128)(2,1)} %bitcast.19), calls=%async_computation.4 | async-start | bytes 4194304 | tf_op jit(solution)/shard_map/all_to_all | solution.py:148
  42.6 3.2 %reshape.116 = bf16[128,2,4,4,2,128]{5,4,3,2,1,0:T(2,128)(2,1)S(1)} reshape(bf16[128,8192]{1,0:T(8,128)(2,1)} %x_ref.1) | data formatting | bytes 4194304 | tf_op jit(solution)/shard_map/reshape | solution.py:168
  45.8 7.3 %constant_dynamic-slice_fusion = (bf16[128,2,4,4,1,128]{5,4,3,2,1,0:T(2,128)(2,1)}, bf16[128,2,4,4,1,128]{5,4,3,2,1,0:T(2,128)(2,1)}) fusion(bf16[128,2,4,4,2,128]{5,4,3,2,1,0:T(2,128)(2,1)S(1)} %reshape.116, s32[]{:T(128)S(6)} %select_n.70, s32[]{:T(128)S(6)} %select_n.69), kind=kLoop, calls=%fused_computation.30 | loop fusion | bytes 4194312 | tf_op jit(solution)/shard_map/jit(dynamic_index_in_dim)/dynamic_slice | solution.py:170
  53.2 6.0 %copy.32 = bf16[128,2,4,4,1,128]{0,5,3,2,1,4:T(8,128)(2,1)} copy(bf16[128,2,4,4,1,128]{5,4,3,2,1,0:T(2,128)(2,1)} %get-tuple-element.8) | data formatting | bytes 2097152
  59.2 3.4 %collective-permute-start.1 = (bf16[128,2,4,4,128]{0,4,3,2,1:T(8,128)(2,1)}, bf16[128,2,4,4,128]{0,4,3,2,1:T(8,128)(2,1)}, u32[]{:S(2)}, u32[]{:S(2)}) collective-permute-start(bf16[128,2,4,4,128]{0,4,3,2,1:T(8,128)(2,1)} %bitcast.4), channel_id=1, source_target_pairs={{0,4},{4,0},{1,5},{5,1},{2,6},{6,2},{3,7},{7,3},{8,12},{12,8},{9,1... | collective-permute-start | bytes 3145736 | tf_op jit(solution)/shard_map/ppermute | solution.py:138
  65.3 12.9 %all-gather.1 = s32[4,1,256]{2,1,0:T(1,128)S(1)} all-gather(s32[1,1,256]{2,1,0:T(1,128)S(1)} %add_bitcast_fusion), channel_id=1, replica_groups=mesh['zh'=2,'y'=4,'x'=4,'c'=2,'t'=4] {'t'}, dimensions={0}, use_global_device_ids=true | all-gather | bytes 5120 | tf_op jit(solution)/shard_map/all_gather | solution.py:153
  78.2 5.2 %collective-permute-start = (bf16[128,256]{1,0:T(8,128)(2,1)S(1)}, bf16[128,256]{1,0:T(8,128)(2,1)S(1)}, u32[]{:S(2)}, u32[]{:S(2)}) collective-permute-start(bf16[128,256]{1,0:T(8,128)(2,1)S(1)} %reduce_sum.66.low_ref), channel_id=1, source_target_pairs={{0,4},{4,0},{1,5},{5,1},{2,6},{6,2},{3,7},{7,3},{8,12},{12,8},{9,1... | collective-permute-start | bytes 196616 | tf_op jit(solution)/shard_map/ppermute | solution.py:138
  84.3 1.9 fusion.10
  90.4 4.6 %all-to-all-start.1 = ((bf16[16,256,256]{2,1,0:T(8,128)(2,1)}), bf16[16,256,256]{2,1,0:T(8,128)(2,1)}, u32[]{:S(2)}, u32[]{:S(2)}) async-start(bf16[16,256,256]{2,1,0:T(8,128)(2,1)} %bitcast.8), calls=%async_computation.1 | async-start | bytes 4194304 | tf_op jit(solution)/shard_map/all_to_all | solution.py:203
  95.1 10.2 %delta.1 = (bf16[32,4,64,128]{3,2,1,0:T(8,128)(2,1)S(1)}, bf16[8192,128]{1,0:T(8,128)(2,1)S(1)}) custom-call(s32[4,64]{1,0:T(4,128)S(1)} %get-tuple-element.15.rows, s32[4,64]{1,0:T(4,128)S(1)} %get-tuple-element.14.cols, s32[4,128]{1,0:T(4,128)S(1)} %slice.32.cnt, bf16[128,8192]{1,0:T(8,128)(2,1)} %x_ref.1, bf16[4,128,2048]{2,1,0:T(8,128)(2,1)} %all-to-all-done.4.g_ref), custom_call_target="tpu_custom_call" | custom-call | flops 4294967296 | bytes 8388608 | tf_op jit(solution)/shard_map/delta/pallas_call | solution.py:212
  111.3 11.7 %collective-permute-start.7 = (bf16[16,64,128]{2,1,0:T(8,128)(2,1)}, bf16[16,64,128]{2,1,0:T(8,128)(2,1)S(1)}, u32[]{:S(2)}, u32[]{:S(2)}) collective-permute-start(bf16[16,64,128]{2,1,0:T(8,128)(2,1)} %fusion.3), channel_id=1, source_target_pairs={{0,131},{4,135},{1,0},{5,4},{2,1},{6,5},{3,2},{7,6},{128,3},{132,7... | collective-permute-start | bytes 786440 | tf_op jit(solution)/shard_map/ppermute | solution.py:160
  125.2 6.3 %collective-permute-done.7 = bf16[16,64,128]{2,1,0:T(8,128)(2,1)S(1)} collective-permute-done((bf16[16,64,128]{2,1,0:T(8,128)(2,1)}, bf16[16,64,128]{2,1,0:T(8,128)(2,1)S(1)}, u32[]{:S(2)}, u32[]{:S(2)}) %collective-permute-start.7) | collective-permute-done | bytes 262176 | tf_op jit(solution)/shard_map/ppermute | solution.py:160
  131.5 3.5 %collective-permute-done.6 = bf16[16,64,128]{2,1,0:T(8,128)(2,1)} collective-permute-done((bf16[16,64,128]{2,1,0:T(8,128)(2,1)}, bf16[16,64,128]{2,1,0:T(8,128)(2,1)}, u32[]{:S(2)}, u32[]{:S(2)}) %collective-permute-start.6) | collective-permute-done | bytes 262176 | tf_op jit(solution)/shard_map/ppermute | solution.py:161
  136.4 2.0 pad_maximum_fusion.1
  139.9 2.5 %fusion.1 = bf16[16,256,128]{2,1,0:T(8,128)(2,1)} fusion(bf16[16,256,128]{2,1,0:T(8,128)(2,1)} %collective-permute-done.4, bf16[16,2,256,128]{3,2,1,0:T(8,128)(2,1)S(1)} %bitcast.69, s32[]{:T(128)S(6)} %select_n.69), kind=kLoop, calls=%fused_computation.7 | loop fusion | flops 2097152 | bytes 3145732 | tf_op jit(solution)/shard_map/convert_element_type | solution.py:228
  142.4 6.6 %all-to-all-start.5 = ((bf16[16,256,128]{2,1,0:T(8,128)(2,1)}), bf16[16,256,128]{2,1,0:T(8,128)(2,1)S(1)}, u32[]{:S(2)}, u32[]{:S(2)}) async-start(bf16[16,256,128]{2,1,0:T(8,128)(2,1)} %fusion.1), calls=%async_computation.5 | async-start | bytes 2097152 | tf_op jit(solution)/shard_map/all_to_all | solution.py:230
  153.1 2.8 %maximum_select_fusion = bf16[3,32,64,128]{3,2,1,0:T(8,128)(2,1)} fusion(bf16[3,16,64,128]{3,2,1,0:T(8,128)(2,1)} %collective-permute-done.8, bf16[1,16,64,128]{3,2,1,0:T(8,128)(2,1)S(1)} %bitcast.78, bf16[1,16,64,128]{3,2,1,0:T(8,128)(2,1)} %bitcast.32, bf16[1,16,64,128]{3,2,1,0:T(8,128)(2,1)} %bitcast.31, pred[]{:T(512)S(6)} %eq.5), kind=kLoop, calls=%fused_computation.9 | loop fusion | flops 5505024 | bytes 3145729 | tf_op jit(solution)/shard_map/jit(_where)/select_n | solution.py:164
  155.9 1.9 reduce_sum.67
  157.8 8.7 %all-to-all-done.5 = bf16[16,256,128]{2,1,0:T(8,128)(2,1)S(1)} async-done(((bf16[16,256,128]{2,1,0:T(8,128)(2,1)}), bf16[16,256,128]{2,1,0:T(8,128)(2,1)S(1)}, u32[]{:S(2)}, u32[]{:S(2)}) %all-to-all-start.5) | async-done | bytes 1048608 | tf_op jit(solution)/shard_map/all_to_all | solution.py:230
  167.7 4.1 %all-to-all-start.2 = ((bf16[8,128,256]{2,1,0:T(8,128)(2,1)}), bf16[8,128,256]{2,1,0:T(8,128)(2,1)}, u32[]{:S(2)}, u32[]{:S(2)}) async-start(bf16[8,128,256]{2,1,0:T(8,128)(2,1)} %bitcast.10), calls=%async_computation.2 | async-start | bytes 1048576 | tf_op jit(solution)/shard_map/all_to_all | solution.py:205
  173.5 2.1 gather_fusion
  175.6 1.9 broadcast_select_fusion.v_ref
  179.1 9.3 %all-to-all-done.2 = bf16[8,128,256]{2,1,0:T(8,128)(2,1)} async-done(((bf16[8,128,256]{2,1,0:T(8,128)(2,1)}), bf16[8,128,256]{2,1,0:T(8,128)(2,1)}, u32[]{:S(2)}, u32[]{:S(2)}) %all-to-all-start.2) | async-done | bytes 524320 | tf_op jit(solution)/shard_map/all_to_all | solution.py:205
  189.1 3.4 %all-to-all-start.6 = ((bf16[8,64,128]{2,1,0:T(8,128)(2,1)}), bf16[8,64,128]{2,1,0:T(8,128)(2,1)S(1)}, u32[]{:S(2)}, u32[]{:S(2)}) async-start(bf16[8,64,128]{2,1,0:T(8,128)(2,1)} %bitcast.24), calls=%async_computation.6 | async-start | bytes 262144 | tf_op jit(solution)/shard_map/all_to_all | solution.py:232
  194.0 11.8 %grad_input.1 = bf16[128,8192]{1,0:T(8,128)(2,1)} custom-call(s32[4,64]{1,0:T(4,128)S(1)} %get-tuple-element.15.rows, s32[4,64]{1,0:T(4,128)S(1)} %get-tuple-element.14.cols, s32[4,128]{1,0:T(4,128)S(1)} %slice.32.cnt, bf16[128,256]{1,0:T(8,128)(2,1)S(1)} %reduce_sum.66.low_ref, bf16[8192,256]{1,0:T(8,128)(2,1)} %down_ref.1, ...), custom_call_target="tpu_custom_call" | custom-call | flops 5368709120 | bytes 12582912 | tf_op jit(solution)/shard_map/grad_input/pallas_call | solution.py:240
  207.7 24.2 %all-gather = bf16[2048,128]{1,0:T(8,128)(2,1)S(1)} all-gather(bf16[64,128]{1,0:T(8,128)(2,1)S(1)} %reduce_sum.71), channel_id=2, replica_groups=mesh['zh'=2,'y'=4,'x'=4,'c'=2,'t'=4] {'y','x','c'}, dimensions={0}, use_global_device_ids=true | all-gather | bytes 540672 | tf_op jit(solution)/shard_map/all_gather | solution.py:237
  (75 shorter events, 34.0 us)
Async XLA Ops:
  0.6 7.1 %copy-start = (bf16[256,2048]{1,0:T(8,128)(2,1)S(1)}, bf16[256,2048]{1,0:T(8,128)(2,1)}, u32[]{:S(2)}) copy-start(bf16[256,2048]{1,0:T(8,128)(2,1)} %param.13) | copy-start | bytes 3145732
  4.4 10.2 %collective-permute-start.2 = (bf16[16,8,2048]{2,1,0:T(8,128)(2,1)S(1)}, bf16[16,8,2048]{2,1,0:T(8,128)(2,1)S(1)}, u32[]{:S(2)}, u32[]{:S(2)}) collective-permute-start(bf16[16,8,2048]{2,1,0:T(8,128)(2,1)S(1)} %dynamic-slice_bitcast_fusion.1), channel_id=1, source_target_pairs={{0,4},{4,0},{1,5},{5,1},{2,6},{6,2},{3,7},{7,3},{8,12},{12,8},{9,1... | collective-permute-start | bytes 1572872 | tf_op jit(solution)/shard_map/ppermute | solution.py:138
  10.8 11.4 %all-to-all-start = ((bf16[4,128,256]{2,1,0:T(8,128)(2,1)}), bf16[4,128,256]{2,1,0:T(8,128)(2,1)S(1)}, u32[]{:S(2)}, u32[]{:S(2)}) async-start(bf16[4,128,256]{2,1,0:T(8,128)(2,1)} %bitcast.81), calls=%async_computation | async-start | bytes 524288 | tf_op jit(solution)/shard_map/all_to_all | solution.py:174
  38.1 52.2 %all-to-all-start.4 = ((bf16[4,128,2048]{2,1,0:T(8,128)(2,1)}), bf16[4,128,2048]{2,1,0:T(8,128)(2,1)}, u32[]{:S(2)}, u32[]{:S(2)}) async-start(bf16[4,128,2048]{2,1,0:T(8,128)(2,1)} %bitcast.19), calls=%async_computation.4 | async-start | bytes 4194304 | tf_op jit(solution)/shard_map/all_to_all | solution.py:148
  53.2 9.5 %copy-start.4 = (bf16[128,2,4,4,1,128]{5,4,3,2,1,0:T(2,128)(2,1)S(1)}, bf16[128,2,4,4,1,128]{5,4,3,2,1,0:T(2,128)(2,1)}, u32[]{:S(2)}) copy-start(bf16[128,2,4,4,1,128]{5,4,3,2,1,0:T(2,128)(2,1)} %get-tuple-element.9) | copy-start | bytes 3145732
  59.2 6.0 %copy-start.10 = (s32[1,64]{1,0:T(1,128)S(1)}, s32[1,64]{1,0:T(1,128)}, u32[]{:S(2)}) copy-start(s32[1,64]{1,0:T(1,128)} %param.16) | copy-start | bytes 772
  59.2 6.0 %copy-start.11 = (s32[1,64]{1,0:T(1,128)S(1)}, s32[1,64]{1,0:T(1,128)}, u32[]{:S(2)}) copy-start(s32[1,64]{1,0:T(1,128)} %param.15) | copy-start | bytes 772
  59.2 25.1 %collective-permute-start.1 = (bf16[128,2,4,4,128]{0,4,3,2,1:T(8,128)(2,1)}, bf16[128,2,4,4,128]{0,4,3,2,1:T(8,128)(2,1)}, u32[]{:S(2)}, u32[]{:S(2)}) collective-permute-start(bf16[128,2,4,4,128]{0,4,3,2,1:T(8,128)(2,1)} %bitcast.4), channel_id=1, source_target_pairs={{0,4},{4,0},{1,5},{5,1},{2,6},{6,2},{3,7},{7,3},{8,12},{12,8},{9,1... | collective-permute-start | bytes 3145736 | tf_op jit(solution)/shard_map/ppermute | solution.py:138
  78.2 6.1 %collective-permute-start = (bf16[128,256]{1,0:T(8,128)(2,1)S(1)}, bf16[128,256]{1,0:T(8,128)(2,1)S(1)}, u32[]{:S(2)}, u32[]{:S(2)}) collective-permute-start(bf16[128,256]{1,0:T(8,128)(2,1)S(1)} %reduce_sum.66.low_ref), channel_id=1, source_target_pairs={{0,4},{4,0},{1,5},{5,1},{2,6},{6,2},{3,7},{7,3},{8,12},{12,8},{9,1... | collective-permute-start | bytes 196616 | tf_op jit(solution)/shard_map/ppermute | solution.py:138
  90.4 52.0 %all-to-all-start.1 = ((bf16[16,256,256]{2,1,0:T(8,128)(2,1)}), bf16[16,256,256]{2,1,0:T(8,128)(2,1)}, u32[]{:S(2)}, u32[]{:S(2)}) async-start(bf16[16,256,256]{2,1,0:T(8,128)(2,1)} %bitcast.8), calls=%async_computation.1 | async-start | bytes 4194304 | tf_op jit(solution)/shard_map/all_to_all | solution.py:203
  105.3 1.3 copy-start.2
  107.6 32.2 %collective-permute-start.4 = (bf16[16,256,128]{2,1,0:T(8,128)(2,1)}, bf16[16,256,128]{2,1,0:T(8,128)(2,1)}, u32[]{:S(2)}, u32[]{:S(2)}) collective-permute-start(bf16[16,256,128]{2,1,0:T(8,128)(2,1)} %dynamic-slice_bitcast_fusion), channel_id=1, source_target_pairs={{0,4},{4,0},{1,5},{5,1},{2,6},{6,2},{3,7},{7,3},{8,12},{12,8},{9,1... | collective-permute-start | bytes 3145736 | tf_op jit(solution)/shard_map/ppermute | solution.py:138
  111.3 20.2 %collective-permute-start.7 = (bf16[16,64,128]{2,1,0:T(8,128)(2,1)}, bf16[16,64,128]{2,1,0:T(8,128)(2,1)S(1)}, u32[]{:S(2)}, u32[]{:S(2)}) collective-permute-start(bf16[16,64,128]{2,1,0:T(8,128)(2,1)} %fusion.3), channel_id=1, source_target_pairs={{0,131},{4,135},{1,0},{5,4},{2,1},{6,5},{3,2},{7,6},{128,3},{132,7... | collective-permute-start | bytes 786440 | tf_op jit(solution)/shard_map/ppermute | solution.py:160
  123.0 12.1 %collective-permute-start.6 = (bf16[16,64,128]{2,1,0:T(8,128)(2,1)}, bf16[16,64,128]{2,1,0:T(8,128)(2,1)}, u32[]{:S(2)}, u32[]{:S(2)}) collective-permute-start(bf16[16,64,128]{2,1,0:T(8,128)(2,1)} %fusion.3), channel_id=1, source_target_pairs={{0,2},{4,134},{1,3},{5,135},{2,128},{6,4},{3,129},{7,5},{128,130},... | collective-permute-start | bytes 786440 | tf_op jit(solution)/shard_map/ppermute | solution.py:161
  123.7 12.7 %collective-permute-start.5 = (bf16[16,64,128]{2,1,0:T(8,128)(2,1)}, bf16[16,64,128]{2,1,0:T(8,128)(2,1)}, u32[]{:S(2)}, u32[]{:S(2)}) collective-permute-start(bf16[16,64,128]{2,1,0:T(8,128)(2,1)} %fusion.3), channel_id=1, source_target_pairs={{0,1},{4,5},{1,2},{5,6},{2,3},{6,7},{3,128},{7,132},{128,129},{132... | collective-permute-start | bytes 786440 | tf_op jit(solution)/shard_map/ppermute | solution.py:159
  138.5 14.6 %collective-permute-start.8 = (bf16[3,16,64,128]{3,2,1,0:T(8,128)(2,1)}, bf16[3,16,64,128]{3,2,1,0:T(8,128)(2,1)}, u32[]{:S(2)}, u32[]{:S(2)}) collective-permute-start(bf16[3,16,64,128]{3,2,1,0:T(8,128)(2,1)} %pad_maximum_fusion.1), channel_id=1, source_target_pairs={{0,4},{4,0},{1,5},{5,1},{2,6},{6,2},{3,7},{7,3},{8,12},{12,8},{9,1... | collective-permute-start | bytes 2359304 | tf_op jit(solution)/shard_map/ppermute | solution.py:138
  142.3 8.2 %copy-start.7 = (bf16[16,8,2048]{2,1,0:T(8,128)(2,1)S(1)}, bf16[16,8,2048]{2,1,0:T(8,128)(2,1)}, u32[]{:S(2)}) copy-start(bf16[16,8,2048]{2,1,0:T(8,128)(2,1)} %all_to_all.35) | copy-start | bytes 1572868
  142.4 24.2 %all-to-all-start.5 = ((bf16[16,256,128]{2,1,0:T(8,128)(2,1)}), bf16[16,256,128]{2,1,0:T(8,128)(2,1)S(1)}, u32[]{:S(2)}, u32[]{:S(2)}) async-start(bf16[16,256,128]{2,1,0:T(8,128)(2,1)} %fusion.1), calls=%async_computation.5 | async-start | bytes 2097152 | tf_op jit(solution)/shard_map/all_to_all | solution.py:230
  151.3 26.2 %collective-permute-start.3 = (f32[4,2048]{1,0:T(4,128)}, f32[4,2048]{1,0:T(4,128)}, u32[]{:S(2)}, u32[]{:S(2)}) collective-permute-start(f32[4,2048]{1,0:T(4,128)} %dynamic-slice_bitcast_fusion.2), channel_id=1, source_target_pairs={{0,128},{128,0},{1,129},{129,1},{2,130},{130,2},{3,131},{131,3},{4... | collective-permute-start | bytes 98312 | tf_op jit(solution)/shard_map/ppermute | solution.py:192
  155.9 16.0 %copy-start.8 = (bf16[1,32,64,128]{3,2,1,0:T(8,128)(2,1)S(1)}, bf16[1,32,64,128]{3,2,1,0:T(8,128)(2,1)}, u32[]{:S(2)}) copy-start(bf16[1,32,64,128]{3,2,1,0:T(8,128)(2,1)} %maximum_bitcast_fusion.1) | copy-start | bytes 1572868
  166.5 1.2 copy-start.5
  167.7 20.7 %all-to-all-start.2 = ((bf16[8,128,256]{2,1,0:T(8,128)(2,1)}), bf16[8,128,256]{2,1,0:T(8,128)(2,1)}, u32[]{:S(2)}, u32[]{:S(2)}) async-start(bf16[8,128,256]{2,1,0:T(8,128)(2,1)} %bitcast.10), calls=%async_computation.2 | async-start | bytes 1048576 | tf_op jit(solution)/shard_map/all_to_all | solution.py:205
  173.4 2.1 copy-start.9
  175.6 3.3 %copy-start.6 = (bf16[16,256,128]{2,1,0:T(8,128)(2,1)S(1)}, bf16[16,256,128]{2,1,0:T(8,128)(2,1)}, u32[]{:S(2)}) copy-start(bf16[16,256,128]{2,1,0:T(8,128)(2,1)} %copy-done.5) | copy-start | bytes 3145732
  189.1 18.6 %all-to-all-start.6 = ((bf16[8,64,128]{2,1,0:T(8,128)(2,1)}), bf16[8,64,128]{2,1,0:T(8,128)(2,1)S(1)}, u32[]{:S(2)}, u32[]{:S(2)}) async-start(bf16[8,64,128]{2,1,0:T(8,128)(2,1)} %bitcast.24), calls=%async_computation.6 | async-start | bytes 262144 | tf_op jit(solution)/shard_map/all_to_all | solution.py:232
  192.4 1.6 copy-start.3
  232.1 1.5 copy-start.1

commit v2 on v0

v2 whole, which is shorter than its diff:
```python
import functools

import jax
import jax.numpy as jnp
from jax import lax
from jax.experimental import pallas as pl
from jax.experimental.pallas import tpu as pltpu
from jax.sharding import Mesh, PartitionSpec as P

F32 = jnp.float32
BF16 = jnp.bfloat16
ZH, Y, X, C, T = 2, 4, 4, 2, 4
XY = Y * X
DP = ("zh", "y", "x", "c")
ALL = DP + ("t",)
BLK = 64
TOK = 128
SLOTS = 64
PAIRS = SLOTS // 2
LANES_OVER = (((1,), (1,)), ((), ()))
MIB = 1024 * 1024


GUESS = {"delta_last": 8.0, "delta_most": 0.0, "low": 10.0, "grad_input": 0.0, "stage": 0.0, "pack": 0.0, "values": 0.0}


def whole():
    return pl.BlockSpec(memory_space=pltpu.VMEM)


def scalars():
    return pl.BlockSpec(memory_space=pltpu.SMEM)


def anywhere():
    return pl.BlockSpec(memory_space=pl.ANY)


def aligned(index, size):
    return pl.ds(pl.multiple_of(index * size, size), size)


def turn_kernel(x_hbm, after_ref, out_ref, x_ref, sems):
    step = x_ref.shape[1] // 8
    copies = []
    for i in range(8):
        at = pl.ds(i * step, step)
        copies.append(pltpu.make_async_copy(x_hbm.at[:, at], x_ref.at[:, at], sems.at[i]))
    for copy in copies:
        copy.start()
    for i in range(8):
        copies[i].wait()
        for j in range(i * step, i * step + step, 128):
            out_ref[j : j + 128, :] = x_ref[:, j : j + 128].T


def front_kernel(place, count, *refs):
    from_hbm, lows, pieces = refs[:4], refs[4 : 4 + T], refs[4 + T : 4 + 2 * T]
    grad_ref, up_ref, rows_ref, cols_ref, low_ref, sems = refs[4 + 2 * T :]
    copies = [
        pltpu.make_async_copy(there, here, sems.at[i])
        for i, (there, here) in enumerate(zip(from_hbm, (grad_ref, up_ref, rows_ref, cols_ref)))
    ]
    for copy in copies:
        copy.start()
    copies[0].wait()
    gives = []
    for k in range(T):
        at = pl.ds(pl.multiple_of((place[4] ^ k) * TOK, TOK), TOK)
        gives.append(pltpu.make_async_copy(grad_ref.at[at], pieces[k], sems.at[4 + k]))
    for give in gives:
        give.start()
    for copy in copies[1:]:
        copy.wait()
    low_ref[...] = lax.dot_general(
        grad_ref[...], up_ref[...], LANES_OVER, preferred_element_type=F32
    ).astype(BF16)
    line = jnp.concatenate(
        [rows_ref[...], cols_ref[...], jnp.full((1, 2 * SLOTS), count[0], jnp.int32)], axis=1
    ).astype(F32)
    line = jnp.broadcast_to(line, (16, line.shape[1])).astype(BF16)
    for k in range(T):
        lows[k][:TOK] = low_ref[aligned(place[4] ^ k, TOK), :]
        lows[k][TOK:] = line
    for give in gives:
        give.wait()


def up_kernel(grad_hbm, acts_hbm, out_ref, grad_ref, acts_ref, sems):
    copies = [
        pltpu.make_async_copy(acts_hbm, acts_ref, sems.at[0]),
        pltpu.make_async_copy(grad_hbm, grad_ref, sems.at[1]),
    ]
    for copy in copies:
        copy.start()
    copies[0].wait()
    rank = acts_ref.shape[1]
    here = lax.broadcasted_iota(jnp.int32, (rank, rank), 1)
    chunk, zh = here >> 3, (here >> 2) & 1
    order = lax.broadcasted_iota(jnp.int32, (rank, rank), 0) == (
        ((zh * (XY * C) + chunk) << 2) + (here & 3)
    )
    order = jnp.where(order, 1.0, 0.0).astype(BF16)
    acts = jnp.dot(acts_ref[...], order, preferred_element_type=F32).astype(BF16)
    copies[1].wait()
    step = 512

    def columns(i, carry):
        out_ref[:, aligned(i, step)] = lax.dot_general(
            acts, grad_ref[:, aligned(i, step)], (((0,), (0,)), ((), ())),
            preferred_element_type=F32,
        ).astype(BF16)
        return carry

    lax.fori_loop(0, grad_ref.shape[1] // step, columns, 0, unroll=2)


def low_kernel(*refs):
    low_ref, table_ref = refs[-2:]
    total = refs[0][:TOK].astype(F32)
    for piece in refs[1:T]:
        total += piece[:TOK].astype(F32)
    low_ref[...] = total.astype(BF16)
    for k in range(T):
        table_ref[k * 8 : k * 8 + 8] = refs[k][TOK:].astype(F32).astype(jnp.int32)[:8]


def pass_kernel(*refs):
    pass


def pack_kernel(values_ref, after_ref, out_ref):
    def one(p, carry):
        out_ref[p] = jnp.concatenate([values_ref[p], values_ref[p + PAIRS]], axis=1)
        return carry

    lax.fori_loop(0, PAIRS, one, 0, unroll=4)


def down_sum_kernel(place, down_ref, keep_ref, give_ref):
    rows = down_ref.shape[1] // ZH
    for mine in range(2):
        zh = place[5] ^ (1 - mine)
        at = aligned(zh, rows)
        total = down_ref[0, at, :].astype(F32)
        for i in range(1, XY):
            total += down_ref[i, at, :].astype(F32)
        if mine:
            keep_ref[...] = total
        else:
            give_ref[...] = total.astype(BF16)


def down_half_kernel(keep_ref, far_ref, out_ref):
    out_ref[...] = (keep_ref[...] + far_ref[...].astype(F32)).astype(BF16)


def down_last_kernel(*refs):
    total = refs[0][...].astype(F32)
    for part in refs[1:T]:
        total += part[...].astype(F32)
    refs[-1][...] = total


def stage_kernel(place, delta_ref, after_ref, out_ref, sum_ref):
    for k in range(T):
        total = delta_ref[0, k].astype(F32)
        for i in range(1, XY):
            total += delta_ref[i, k].astype(F32)
        sum_ref[k] = total
    for t in range(T):
        part = sum_ref[place[4] ^ t].astype(BF16)
        for zh in range(ZH):
            out_ref[zh * T + t] = part


def last_kernel(parts_ref, after_ref, after_too_ref, delta_ref):
    total = parts_ref[0].astype(F32)
    for i in range(1, ZH * T):
        total += parts_ref[i].astype(F32)
    delta = total.astype(BF16)
    for p in range(PAIRS):
        delta_ref[p] = delta


def unpack_kernel(pairs_ref, out_ref):
    def one(p, carry):
        pair = pairs_ref[p].astype(F32)
        out_ref[p] = pair[:, :BLK]
        out_ref[p + PAIRS] = pair[:, BLK:]
        return carry

    lax.fori_loop(0, PAIRS, one, 0, unroll=4)


def down_kernel(place, xt_ref, xt_far_ref, low_ref, low_far_ref, *refs):
    out_ref = refs[-1]
    low, low_far = low_ref[...], low_far_ref[...]
    core = place[0]

    def block(i, carry):
        for zh in range(ZH):
            at = aligned((zh * XY + i) * C + core, 128)
            total = jnp.dot(xt_ref[at, :], low, preferred_element_type=F32)
            total += jnp.dot(xt_far_ref[at, :], low_far, preferred_element_type=F32)
            out_ref[i, zh * 128 : (zh + 1) * 128] = total.astype(BF16)
        return carry

    lax.fori_loop(0, XY, block, 0, unroll=4)


def delta_kernel(pieces, place, table, xt_ref, xt_far_ref, *refs):
    n = len(pieces)
    near, far = refs[:n], refs[n : 2 * n]
    all_ref, grad_ref, out_ref, gt_ref, both_ref, sems = refs[-6:]
    width = near[0].shape[1]
    core = place[0]
    for j in range(n):

        def turn(i, carry, j=j):
            at = pl.ds(pl.multiple_of(i * 128, 128), 128)
            own = near[j][:, at].T
            both_ref[at, j * 256 : j * 256 + 128] = own
            both_ref[at, j * 256 + 128 : j * 256 + 256] = far[j][:, at].T
            gt_ref[pl.ds(pl.multiple_of(j * width + i * 128, 128), 128), :] = own
            return carry

        lax.fori_loop(0, width // 128, turn, 0, unroll=4)
    keep = pltpu.make_async_copy(gt_ref, grad_ref, sems.at[0])
    keep.start()

    lane = lax.broadcasted_iota(jnp.int32, (BLK, 2 * BLK), 1)

    def rows_of(index):
        return jnp.concatenate(
            [xt_ref[aligned(index, BLK), :], xt_far_ref[aligned(index, BLK), :]], axis=1
        )

    def pair(i, carry):
        s0 = i * C + core
        s1 = s0 + PAIRS
        for j, k in enumerate(pieces):
            xt = jnp.concatenate([rows_of(table[8 * k, s0]), rows_of(table[8 * k, s1])], axis=0)
            gt = jnp.concatenate(
                [
                    both_ref[aligned(table[8 * k, SLOTS + s], BLK), j * 256 : j * 256 + 256]
                    for s in (s0, s1)
                ],
                axis=0,
            )
            full = lax.dot_general(xt, gt, LANES_OVER, preferred_element_type=F32)
            live = jnp.where(lane < BLK, s0, s1) < table[8 * k, 2 * SLOTS]
            both = jnp.where(lane < BLK, full[:BLK], full[BLK:])
            out_ref[i, j] = jnp.where(live, both, 0.0).astype(BF16)
        return carry

    lax.fori_loop(0, XY, pair, 0, unroll=4)
    give = pltpu.make_async_copy(out_ref, all_ref.at[:, pieces[0] : pieces[0] + n], sems.at[1])
    give.start()
    keep.wait()
    give.wait()


def input_kernel(place, table, low_ref, *refs):
    from_hbm = refs[:7]
    out_ref, acc_ref, down_ref, gt_ref, values, sems = refs[7:]
    most = from_hbm[1].shape[0]
    to_vmem = (
        down_ref, gt_ref.at[:most], gt_ref.at[most:], values.at[0], values.at[1], values.at[2], values.at[3],
    )
    copies = [
        pltpu.make_async_copy(there, here, sems.at[n])
        for n, (there, here) in enumerate(zip(from_hbm, to_vmem))
    ]
    for copy in copies:
        copy.start()
    low = low_ref[...]
    step = 512
    width = gt_ref.shape[0] // T

    def dense(i, carry):
        acc_ref[aligned(i, step), :] = lax.dot_general(
            down_ref[aligned(i, step), :], low, LANES_OVER, preferred_element_type=F32
        )
        return carry

    copies[0].wait()
    lax.fori_loop(0, acc_ref.shape[0] // step, dense, 0, unroll=2)
    for copy in copies[1:]:
        copy.wait()
    lane = lax.broadcasted_iota(jnp.int32, (BLK, 2 * BLK), 1)

    def product(v, k, s0, s1):
        zero = jnp.zeros_like(v)
        live = table[8 * k, 2 * SLOTS]
        top = jnp.where((lane < BLK) & (s0 < live), v, zero)
        bottom = jnp.where((lane >= BLK) & (s1 < live), v, zero)
        gt = jnp.concatenate(
            [
                gt_ref[aligned(table[8 * k, SLOTS + s] + k * (width // BLK), BLK), :]
                for s in (s0, s1)
            ],
            axis=0,
        )
        return jnp.dot(jnp.concatenate([top, bottom], axis=0), gt, preferred_element_type=F32)

    def pair(i, carry):
        done = []
        for s0 in (2 * i, 2 * i + 1):
            s1 = s0 + PAIRS
            for m in range(T):
                k = 0 if m == 0 else place[m]
                done.append((k, s0, s1, product(values[m, s0], k, s0, s1)))
        for k, s0, s1, part in done:
            for s, add in ((s0, part[:BLK]), (s1, part[BLK:])):
                at = aligned(table[8 * k, s], BLK)
                acc_ref[at, :] = acc_ref[at, :] + add
        return carry

    lax.fori_loop(0, PAIRS // 2, pair, 0)

    def turn(i, carry):
        out_ref[:, aligned(i, 128)] = acc_ref[aligned(i, 128), :].T.astype(BF16)
        return carry

    lax.fori_loop(0, acc_ref.shape[0] // 128, turn, 0, unroll=4)


def ring(shift_of_core):
    def place(z, c):
        return (z // T * C + c) * T + z % T

    n = ZH * T
    return [
        (place(z, c), place((z + shift_of_core[c]) % n, c)) for z in range(n) for c in range(C)
    ]


def swap(array, axis="c"):
    return lax.ppermute(array, axis, [(0, 1), (1, 0)])


def cross(array, k):
    return lax.ppermute(array, "t", [(i, i ^ k) for i in range(T)])


def call(kernel, name, outs, in_specs, *args, out_specs=None, scratch=(), room=16, **grid):
    return pl.pallas_call(
        kernel,
        out_shape=outs,
        in_specs=in_specs,
        out_specs=out_specs if out_specs is not None else jax.tree.map(lambda _: whole(), outs),
        scratch_shapes=scratch,
        compiler_params=pltpu.CompilerParams(vmem_limit_bytes=room * MIB),
        cost_estimate=pl.CostEstimate(
            flops=int(GUESS.get(name, 0) * 1000000000) + 1024, bytes_accessed=1024, transcendentals=0
        ),
        name=name,
        **grid,
    )(*args)


def per_device(x_own, acts, grad, down, up, values, slot_rows, slot_cols, count):
    zh, c, t = lax.axis_index("zh"), lax.axis_index("c"), lax.axis_index("t")
    feat, width, rank = x_own.shape[1], grad.shape[1], up.shape[0]
    place = jnp.stack(
        [c, t ^ ((t - 1) % T), t ^ ((t + 1) % T), 2 + 0 * t, t, zh]
    ).astype(jnp.int32)
    rows = TOK + 16
    shape = jax.ShapeDtypeStruct

    given = call(
        front_kernel, "front",
        (shape((rows, rank), BF16),) * T + (shape((TOK, width), BF16),) * T,
        [scalars()] * 2 + [anywhere()] * 4, place, count, grad, up, slot_rows, slot_cols,
        out_specs=(whole(),) * T + (anywhere(),) * T, room=56,
        scratch=[
            pltpu.VMEM(grad.shape, BF16),
            pltpu.VMEM(up.shape, BF16),
            pltpu.VMEM((1, SLOTS), jnp.int32),
            pltpu.VMEM((1, SLOTS), jnp.int32),
            pltpu.VMEM((T * TOK, rank), BF16),
            pltpu.SemaphoreType.DMA((4 + T,)),
        ],
    )
    parts, near = given[:T], given[T:]
    parts = [parts[0]] + [cross(parts[k], k) for k in (1, 2, 3)]
    near = [near[0]] + [cross(near[k], k) for k in (1, 2, 3)]

    xt = call(
        turn_kernel, "turn_input", shape((feat, TOK), BF16),
        [anywhere()] * 2, x_own, given[0],
        scratch=[pltpu.VMEM(x_own.shape, BF16), pltpu.SemaphoreType.DMA((8,))],
    )
    xt_far = swap(xt)

    up_part = call(
        up_kernel, "up_part", shape((rank, width), BF16), [anywhere()] * 2, grad, acts,
        scratch=[
            pltpu.VMEM(grad.shape, BF16),
            pltpu.VMEM(acts.shape, BF16),
            pltpu.SemaphoreType.DMA((2,)),
        ],
    )

    low, table = call(
        low_kernel, "low", (shape((TOK, rank), BF16), shape((8 * T, rank), jnp.int32)),
        [whole()] * T + [anywhere()], *parts, up_part,
    )
    low_far = swap(low)

    up_all = lax.all_to_all(
        up_part.reshape(XY * C, ZH * 4, width), ("y", "x", "c"), 0, 0, tiled=True
    )
    up_sum = jnp.sum(up_all.astype(F32), axis=0).reshape(ZH, 4, width)
    up_far = swap(lax.dynamic_index_in_dim(up_sum, 1 - zh, 0, keepdims=False), "zh")
    up_grad = lax.dynamic_index_in_dim(up_sum, zh, 0, keepdims=False) + up_far

    down_part = call(
        down_kernel, "down_part", shape((XY, ZH * 128, rank), BF16),
        [scalars()] + [whole()] * 4 + [anywhere()], place, xt, xt_far, low, low_far,
        up_all,
    )
    down_all = lax.all_to_all(down_part, ("y", "x"), 0, 0, tiled=True)
    down_keep, down_give = call(
        down_sum_kernel, "down_sum", (shape((128, rank), F32), shape((128, rank), BF16)),
        [scalars(), whole()], place, down_all,
    )
    down_half = call(
        down_half_kernel, "down_half", shape((128, rank), BF16), [whole()] * 2,
        down_keep, swap(down_give, "zh"),
    )
    down_grad = call(
        down_last_kernel, "down_last", shape((128, rank), F32), [whole()] * T,
        down_half, *[cross(down_half, k) for k in (1, 2, 3)],
    )

    def delta_call(pieces, *before):
        n = len(pieces)
        return call(
            functools.partial(delta_kernel, pieces), "delta_last" if before else "delta_most",
            (shape((XY, T, BLK, 2 * BLK), BF16), shape((n * width, TOK), BF16)),
            [scalars()] * 2 + [whole()] * (2 + 2 * n) + [anywhere()] * len(before),
            place, table, xt, xt_far, *[near[k] for k in pieces], *[far[k] for k in pieces],
            *before,
            out_specs=(anywhere(), anywhere()), room=24,
            scratch=[
                pltpu.VMEM((XY, n, BLK, 2 * BLK), BF16),
                pltpu.VMEM((n * width, TOK), BF16),
                pltpu.VMEM((width, 256 * n), BF16),
                pltpu.SemaphoreType.DMA((2,)),
            ],
            input_output_aliases={4 + 2 * n: 0} if before else {},
        )

    far = [swap(near[k]) for k in (0, 1, 2)]
    delta_most, grad_most = delta_call((0, 1, 2))
    near[3] = call(
        pass_kernel, "gate", shape((TOK, width), BF16), [anywhere()] * 2, near[3], delta_most,
        out_specs=anywhere(), input_output_aliases={0: 0},
    )
    far.append(swap(near[3]))
    delta_full, grad_last = delta_call((3,), delta_most)
    delta_part = call(
        pass_kernel, "join", shape((XY, T, BLK, 2 * BLK), BF16), [anywhere()] * 2,
        delta_full, down_all,
        out_specs=anywhere(), input_output_aliases={0: 0},
    )
    delta_all = lax.all_to_all(delta_part, ("y", "x"), 0, 0, tiled=True)

    packed = call(
        pack_kernel, "pack", shape((PAIRS, BLK, 2 * BLK), BF16), [whole(), anywhere()],
        values[0], near[3],
    )
    axes = ("zh", "t")
    got = [
        lax.ppermute(packed, axes, [(i, (i + 1) % (ZH * T)) for i in range(ZH * T)]),
        lax.ppermute(packed, axes, [(i, (i - 1) % (ZH * T)) for i in range(ZH * T)]),
        lax.ppermute(packed, ("zh", "c", "t"), ring((2, -2))),
    ]
    got = call(
        pass_kernel, "values", (shape(packed.shape, BF16),) * 3, [anywhere()] * 3, *got,
        out_specs=(anywhere(),) * 3, input_output_aliases={0: 0, 1: 1, 2: 2},
    )
    grad_input = call(
        input_kernel, "grad_input", shape((TOK, feat), BF16),
        [scalars()] * 2 + [whole()] + [anywhere()] * 7,
        place, table, low, down, grad_most, grad_last, packed, *got, room=56,
        scratch=[
            pltpu.VMEM((feat, TOK), F32),
            pltpu.VMEM(down.shape, BF16),
            pltpu.VMEM((T * width, TOK), BF16),
            pltpu.VMEM((T, PAIRS, BLK, 2 * BLK), BF16),
            pltpu.SemaphoreType.DMA((7,)),
        ],
    )

    stage = call(
        stage_kernel, "stage", shape((ZH * T, BLK, 128), BF16),
        [scalars(), whole(), anywhere()], place, delta_all, down_give,
        scratch=[pltpu.VMEM((T, BLK, 2 * BLK), F32)],
    )
    stage_all = lax.all_to_all(stage, ("zh", "t"), 0, 0, tiled=True)
    delta_one = call(
        last_kernel, "last", shape((PAIRS, BLK, 2 * BLK), BF16), [whole()] + [anywhere()] * 2,
        stage_all, grad_input, down_half,
    )
    delta_full = lax.all_to_all(delta_one, ("y", "x", "c"), 0, 0, tiled=True)
    grad_delta = call(
        unpack_kernel, "unpack", shape((SLOTS, BLK, BLK), F32), [whole()], delta_full
    )[None]
    return down_grad, up_grad, grad_delta, grad_input


def solution(mesh):
    fine = Mesh(mesh.devices.reshape(ZH, Y, X, C, T), ALL)
    return jax.shard_map(
        per_device,
        mesh=fine,
        in_specs=(
            P(ALL, None),
            P(DP, None),
            P(DP, "t"),
            P(),
            P(None, "t"),
            P("t", None, None, None),
            P("t", None),
            P("t", None),
            P("t"),
        ),
        out_specs=(
            P(DP, None),
            P(DP, "t"),
            P("t", None, None, None),
            P(ALL, None),
        ),
        check_vma=False,
    )
```

time: 1620 us -> 164 us (0.10); the launches traced: 1600 us -> 163 us
  waiting for transfers between devices: 1470 us -> 30 us
  matrix products: 77.5 us -> 0 us
  starting transfers between devices: 0.42 us -> 74.9 us
  Pallas kernels: 0 us -> 41.1 us
  local copies, waits for them, and re-layouts: 35.7 us -> 14.6 us
    unnamed x6 -> x0, waiting for transfers between devices: 761 us -> none
    reduce_scatter x2 -> x0, waiting for transfers between devices: 567 us -> none  [the longest x1 416 us: per_device(): lax.psum_scatter(lax.dot_general(full_rows, low_all, (((0,), (0,)), ((),...]
    all_gather x1 -> x0, waiting for transfers between devices: 145 us -> none  [per_device(): full_rows = lax.all_gather(projection_input, 'tensor', axis=0, tiled=True)]
    dot_general x10 -> x0, matrix products: 77.5 us -> none  [the longest x1 13.4 us: per_device(): jnp.einsum('nrk,sr->snk', full_rows.reshape(tok_count, row_blocks, block_...]
    pallas_call x0 -> x18, Pallas kernels: none -> 41.1 us  [call(): pl.pallas_call(kernel, out_shape=outs, in_specs=in_specs, out_specs=out_s...]
    ppermute x0 -> x20, starting transfers between devices: none -> 38.5 us  [the longest x8 15.8 us: swap(): return lax.ppermute(array, axis, [(0, 1), (1, 0)])]
    all_to_all x0 -> x5, starting transfers between devices: none -> 36.5 us  [the longest x1 11.2 us: per_device(): delta_full = lax.all_to_all(delta_one, ('y', 'x', 'c'), 0, 0, tiled=True)]
    convert_element_type x2 -> x0, local copies, waits for them, and re-layouts: 22.9 us -> none  [per_device(): partial_value.astype(jnp.bfloat16)]
  transfers between devices with their start and end apart: 5 -> 25, of which waited for: 4 -> 10; matrix products, arithmetic and copies ran while one was open for 7% -> 0% of each run, Pallas kernels for 0% -> 20%
where the time goes in v2:
time: 164 us; the launch traced here: 163 us
  starting transfers between devices  74.9 us (46%)
  Pallas kernels  41.1 us (25%)
  waiting for transfers between devices  30 us (18%)
  local copies, waits for them, and re-layouts  14.6 us (9%)
    pallas_call x18, Pallas kernels, call(): pl.pallas_call(kernel, out_shape=outs, in_specs=in_specs, out_specs=out_s...  41.1 us
    ppermute x8, starting transfers between devices, swap(): return lax.ppermute(array, axis, [(0, 1), (1, 0)])  15.8 us
    unnamed x48, local copies, waits for them, and re-layouts  14 us
    ppermute x9, starting transfers between devices, cross(): return lax.ppermute(array, 't', [(i, i ^ k) for i in range(T)])  13.6 us
    all_to_all x1, starting transfers between devices, per_device(): delta_full = lax.all_to_all(delta_one, ('y', 'x', 'c'), 0, 0, tiled=True)  11.2 us
    all_to_all x1, starting transfers between devices, per_device(): stage_all = lax.all_to_all(stage, ('zh', 't'), 0, 0, tiled=True)  10.1 us
    all_to_all x1, waiting for transfers between devices, per_device(): lax.all_to_all(up_part.reshape(XY * C, ZH * 4, width), ('y', 'x', 'c'), 0...  8.67 us
    ppermute x9, waiting for transfers between devices, cross(): return lax.ppermute(array, 't', [(i, i ^ k) for i in range(T)])  8.53 us
  transfers between devices with their start and end apart: 25, of which 10 were waited for; matrix products, arithmetic and copies ran while one was open for 0% of the time, Pallas kernels for 20%

profile of v2, /device:TPU:1, one launch (start us, length us, event | category | flops | bytes accessed | tf_op | source)
XLA Modules:
  0.0 163.0 jit_solution(6389872922315382410)
XLA Ops:
  1.9 4.5 %front.1 = (bf16[144,256]{1,0:T(8,128)(2,1)}, bf16[144,256]{1,0:T(8,128)(2,1)}, bf16[144,256]{1,0:T(8,128)(2,1)}, bf16[144,256]{1,0:T(8,128)(2,1)}, bf16[128,204...) custom-call(s32[6]{0:T(128)} %stack.23.place, ...), custom_call_target="tpu_custom_call" | custom-call | flops 1024 | bytes 1024 | tf_op jit(solution)/shard_map/front/pallas_call | solution.py:348
  8.5 3.3 %collective-permute-start = (bf16[8192,128]{1,0:T(8,128)(2,1)S(1)}, bf16[8192,128]{1,0:T(8,128)(2,1)}, u32[]{:S(2)}, u32[]{:S(2)}) collective-permute-start(bf16[8192,128]{1,0:T(8,128)(2,1)S(1)} %turn_input.1.xt_ref), channel_id=1, source_target_pairs={{0,4},{4,0},{1,5},{5,1},{2,6},{6,2},{3,7},{7,3},{8,12},{12,8},{9,1... | collective-permute-start | bytes 6291464 | tf_op jit(solution)/shard_map/ppermute | solution.py:340
  11.8 2.9 %collective-permute-start.2 = (bf16[144,256]{1,0:T(8,128)(2,1)}, bf16[144,256]{1,0:T(8,128)(2,1)S(1)}, u32[]{:S(2)}, u32[]{:S(2)}) collective-permute-start(bf16[144,256]{1,0:T(8,128)(2,1)} %get-tuple-element.25), channel_id=1, source_target_pairs={{0,2},{1,3},{2,0},{3,1},{4,6},{5,7},{6,4},{7,5},{8,10},{9,11},{10,... | collective-permute-start | bytes 221192 | tf_op jit(solution)/shard_map/ppermute | solution.py:344
  15.4 1.3 up_part.1.refs_4_
  17.7 7.1 %all-to-all-start = ((bf16[32,8,2048]{2,1,0:T(8,128)(2,1)}), bf16[32,8,2048]{2,1,0:T(8,128)(2,1)S(1)}, u32[]{:S(2)}, u32[]{:S(2)}) async-start(bf16[32,8,2048]{2,1,0:T(8,128)(2,1)} %bitcast.12), calls=%async_computation | async-start | bytes 2097152 | tf_op jit(solution)/shard_map/all_to_all | solution.py:412
  25.3 3.5 %collective-permute-start.12 = (bf16[128,2048]{1,0:T(8,128)(2,1)}, bf16[128,2048]{1,0:T(8,128)(2,1)}, u32[]{:S(2)}, u32[]{:S(2)}) collective-permute-start(bf16[128,2048]{1,0:T(8,128)(2,1)} %get-tuple-element.34), channel_id=1, source_target_pairs={{0,2},{1,3},{2,0},{3,1},{4,6},{5,7},{6,4},{7,5},{8,10},{9,11},{10,... | collective-permute-start | bytes 1572872 | tf_op jit(solution)/shard_map/ppermute | solution.py:344
  33.3 8.7 %all-to-all-done.refs_0_ = bf16[32,8,2048]{2,1,0:T(8,128)(2,1)S(1)} async-done(((bf16[32,8,2048]{2,1,0:T(8,128)(2,1)}), bf16[32,8,2048]{2,1,0:T(8,128)(2,1)S(1)}, u32[]{:S(2)}, u32[]{:S(2)}) %all-to-all-start) | async-done | bytes 1048608 | tf_op jit(solution)/shard_map/all_to_all | solution.py:412
  42.0 3.3 %down_part.1 = bf16[16,256,256]{2,1,0:T(8,128)(2,1)S(1)} custom-call(s32[6]{0:T(128)S(1)} %copy-done.20, bf16[8192,128]{1,0:T(8,128)(2,1)S(1)} %turn_input.1.xt_ref, bf16[8192,128]{1,0:T(8,128)(2,1)} %collective-permute-done.xt_far_ref, bf16[128,256]{1,0:T(8,128)(2,1)S(1)} %get-tuple-element.27.low_ref, ...), custom_call_target="tpu_custom_call" | custom-call | flops 1024 | bytes 1024 | tf_op jit(solution)/shard_map/down_part/pallas_call | solution.py:348
  46.7 3.7 %all-to-all-start.1 = ((bf16[16,256,256]{2,1,0:T(8,128)(2,1)}), bf16[16,256,256]{2,1,0:T(8,128)(2,1)S(1)}, u32[]{:S(2)}, u32[]{:S(2)}) async-start(bf16[16,256,256]{2,1,0:T(8,128)(2,1)} %copy-done.5), calls=%async_computation.1 | async-start | bytes 4194304 | tf_op jit(solution)/shard_map/all_to_all | solution.py:424
  51.0 2.2 %collective-permute-start.15 = (bf16[128,2048]{1,0:T(8,128)(2,1)}, bf16[128,2048]{1,0:T(8,128)(2,1)S(1)}, u32[]{:S(2)}, u32[]{:S(2)}) collective-permute-start(bf16[128,2048]{1,0:T(8,128)(2,1)} %collective-permute-done.12.refs_2_), channel_id=1, source_target_pairs={{0,4},{4,0},{1,5},{5,1},{2,6},{6,2},{3,7},{7,3},{8,12},{12,8},{9,1... | collective-permute-start | bytes 1572872 | tf_op jit(solution)/shard_map/ppermute | solution.py:340
  53.2 2.2 %collective-permute-start.10 = (bf16[128,2048]{1,0:T(8,128)(2,1)}, bf16[128,2048]{1,0:T(8,128)(2,1)S(1)}, u32[]{:S(2)}, u32[]{:S(2)}) collective-permute-start(bf16[128,2048]{1,0:T(8,128)(2,1)} %get-tuple-element.31), channel_id=1, source_target_pairs={{0,3},{1,2},{2,1},{3,0},{4,7},{5,6},{6,5},{7,4},{8,11},{9,10},{10,... | collective-permute-start | bytes 1572872 | tf_op jit(solution)/shard_map/ppermute | solution.py:344
  55.4 1.6 copy-done.1
  58.1 5.9 %delta_most.1 = (bf16[16,4,64,128]{3,2,1,0:T(8,128)(2,1)}, bf16[6144,128]{1,0:T(8,128)(2,1)S(1)}) custom-call(s32[6]{0:T(128)S(1)} %copy-done.20, s32[32,256]{1,0:T(8,128)S(1)} %get-tuple-element.30.table, bf16[8192,128]{1,0:T(8,128)(2,1)S(1)} %copy-done.1, bf16[8192,128]{1,0:T(8,128)(2,1)} %collective-permute-done.xt_far_ref, ...), custom_call_target="tpu_custom_call" | custom-call | flops 1024 | bytes 1024 | tf_op jit(solution)/shard_map/delta_most/pallas_call | solution.py:348
  64.0 4.8 %collective-permute-done.10.refs_0_ = bf16[128,2048]{1,0:T(8,128)(2,1)S(1)} collective-permute-done((bf16[128,2048]{1,0:T(8,128)(2,1)}, bf16[128,2048]{1,0:T(8,128)(2,1)S(1)}, u32[]{:S(2)}, u32[]{:S(2)}) %collective-permute-start.10) | collective-permute-done | bytes 524320 | tf_op jit(solution)/shard_map/ppermute | solution.py:344
  69.7 1.5 collective-permute-done.16.refs_1_
  71.2 3.8 %delta_last.1 = (bf16[16,4,64,128]{3,2,1,0:T(8,128)(2,1)}, bf16[2048,128]{1,0:T(8,128)(2,1)S(1)}) custom-call(s32[6]{0:T(128)S(1)} %copy-done.20, s32[32,256]{1,0:T(8,128)S(1)} %get-tuple-element.30.table, bf16[8192,128]{1,0:T(8,128)(2,1)S(1)} %copy-done.2, bf16[8192,128]{1,0:T(8,128)(2,1)} %collective-permute-done.xt_far_ref, ...), custom_call_target="tpu_custom_call", output_to_operand_aliasing={{0}: (6, {})} | custom-call | flops 8000001024 | bytes 1024 | tf_op jit(solution)/shard_map/delta_last/pallas_call | solution.py:348
  76.7 6.7 %all-to-all-done.1.down_ref.refs_1_ = bf16[16,256,256]{2,1,0:T(8,128)(2,1)S(1)} async-done(((bf16[16,256,256]{2,1,0:T(8,128)(2,1)}), bf16[16,256,256]{2,1,0:T(8,128)(2,1)S(1)}, u32[]{:S(2)}, u32[]{:S(2)}) %all-to-all-start.1) | async-done | bytes 2097184 | tf_op jit(solution)/shard_map/all_to_all | solution.py:424
  83.4 4.4 %all-to-all-start.2 = ((bf16[16,4,64,128]{3,2,1,0:T(8,128)(2,1)}), bf16[16,4,64,128]{3,2,1,0:T(8,128)(2,1)}, u32[]{:S(2)}, u32[]{:S(2)}) async-start(bf16[16,4,64,128]{3,2,1,0:T(8,128)(2,1)} %join.1), calls=%async_computation.2 | async-start | bytes 2097152 | tf_op jit(solution)/shard_map/all_to_all | solution.py:469
  90.0 1.5 pack.1.refs_3_
  91.5 5.1 %collective-permute-start.17 = (bf16[32,64,128]{2,1,0:T(8,128)(2,1)}, bf16[32,64,128]{2,1,0:T(8,128)(2,1)}, u32[]{:S(2)}, u32[]{:S(2)}) collective-permute-start(bf16[32,64,128]{2,1,0:T(8,128)(2,1)} %pack.1.refs_3_), channel_id=1, source_target_pairs={{0,1},{1,2},{2,3},{3,128},{128,129},{129,130},{130,131},{131,0},{4... | collective-permute-start | bytes 1572872 | tf_op jit(solution)/shard_map/ppermute | solution.py:477
  96.6 4.0 %collective-permute-start.19 = (bf16[32,64,128]{2,1,0:T(8,128)(2,1)}, bf16[32,64,128]{2,1,0:T(8,128)(2,1)}, u32[]{:S(2)}, u32[]{:S(2)}) collective-permute-start(bf16[32,64,128]{2,1,0:T(8,128)(2,1)} %pack.1.refs_3_), channel_id=1, source_target_pairs={{0,2},{4,134},{1,3},{5,135},{2,128},{6,4},{3,129},{7,5},{128,130},... | collective-permute-start | bytes 1572872 | tf_op jit(solution)/shard_map/ppermute | solution.py:479
  101.4 2.0 %all-to-all-done.2.delta_ref = bf16[16,4,64,128]{3,2,1,0:T(8,128)(2,1)} async-done(((bf16[16,4,64,128]{3,2,1,0:T(8,128)(2,1)}), bf16[16,4,64,128]{3,2,1,0:T(8,128)(2,1)}, u32[]{:S(2)}, u32[]{:S(2)}) %all-to-all-start.2) | async-done | bytes 1048608 | tf_op jit(solution)/shard_map/all_to_all | solution.py:469
  103.4 2.0 %stage.1 = bf16[8,64,128]{2,1,0:T(8,128)(2,1)} custom-call(s32[6]{0:T(128)S(1)} %copy-done.20, bf16[16,4,64,128]{3,2,1,0:T(8,128)(2,1)} %all-to-all-done.2.delta_ref, bf16[128,256]{1,0:T(8,128)(2,1)S(1)} %get-tuple-element.29.after_ref), custom_call_target="tpu_custom_call" | custom-call | flops 1024 | bytes 1024 | tf_op jit(solution)/shard_map/stage/pallas_call | solution.py:348
  105.5 10.1 %all-to-all-start.3 = ((bf16[8,64,128]{2,1,0:T(8,128)(2,1)}), bf16[8,64,128]{2,1,0:T(8,128)(2,1)S(1)}, u32[]{:S(2)}, u32[]{:S(2)}) async-start(bf16[8,64,128]{2,1,0:T(8,128)(2,1)} %stage.1), calls=%async_computation.3 | async-start | bytes 262144 | tf_op jit(solution)/shard_map/all_to_all | solution.py:503
  115.5 5.4 %collective-permute-start.5 = (bf16[128,256]{1,0:T(8,128)(2,1)S(1)}, bf16[128,256]{1,0:T(8,128)(2,1)S(1)}, u32[]{:S(2)}, u32[]{:S(2)}) collective-permute-start(bf16[128,256]{1,0:T(8,128)(2,1)S(1)} %get-tuple-element.29.after_ref), channel_id=1, source_target_pairs={{0,128},{128,0},{1,129},{129,1},{2,130},{130,2},{3,131},{131,3},{4... | collective-permute-start | bytes 196616 | tf_op jit(solution)/shard_map/ppermute | solution.py:340
  122.3 13.0 %grad_input.1.after_ref = bf16[128,8192]{1,0:T(8,128)(2,1)} custom-call(s32[6]{0:T(128)} %stack.23.place, s32[32,256]{1,0:T(8,128)} %copy-done.17, bf16[128,256]{1,0:T(8,128)(2,1)} %copy-done.15, bf16[8192,256]{1,0:T(8,128)(2,1)} %refs_0_.3, bf16[6144,128]{1,0:T(8,128)(2,1)} %copy-done.11, bf16[2048,128]{1,0:T(8,128)(2,1)} %copy-done.14, ...), custom_call_target="tpu_custom_call" | custom-call | flops 1024 | bytes 1024 | tf_op jit(solution)/shard_map/grad_input/pallas_call | solution.py:348
  135.4 1.6 copy-done.4
  137.8 11.2 %all-to-all-start.4 = ((bf16[32,64,128]{2,1,0:T(8,128)(2,1)}), bf16[32,64,128]{2,1,0:T(8,128)(2,1)S(1)}, u32[]{:S(2)}, u32[]{:S(2)}) async-start(bf16[32,64,128]{2,1,0:T(8,128)(2,1)} %last.1), calls=%async_computation.4 | async-start | bytes 1048576 | tf_op jit(solution)/shard_map/all_to_all | solution.py:508
  149.1 2.5 %collective-permute-start.9 = (f32[4,2048]{1,0:T(4,128)S(1)}, f32[4,2048]{1,0:T(4,128)S(1)}, u32[]{:S(2)}, u32[]{:S(2)}) collective-permute-start(f32[4,2048]{1,0:T(4,128)S(1)} %dynamic-slice_bitcast_fusion), channel_id=1, source_target_pairs={{0,128},{128,0},{1,129},{129,1},{2,130},{130,2},{3,131},{131,3},{4... | collective-permute-start | bytes 98312 | tf_op jit(solution)/shard_map/ppermute | solution.py:340
  152.6 1.7 %collective-permute-start.7 = (bf16[128,256]{1,0:T(8,128)(2,1)S(1)}, bf16[128,256]{1,0:T(8,128)(2,1)S(1)}, u32[]{:S(2)}, u32[]{:S(2)}) collective-permute-start(bf16[128,256]{1,0:T(8,128)(2,1)S(1)} %down_half.1.refs_0_.after_too_ref), channel_id=1, source_target_pairs={{0,2},{1,3},{2,0},{3,1},{4,6},{5,7},{6,4},{7,5},{8,10},{9,11},{10,... | collective-permute-start | bytes 196616 | tf_op jit(solution)/shard_map/ppermute | solution.py:344
  156.9 3.3 %collective-permute-done.8.refs_3_ = bf16[128,256]{1,0:T(8,128)(2,1)S(1)} collective-permute-done((bf16[128,256]{1,0:T(8,128)(2,1)S(1)}, bf16[128,256]{1,0:T(8,128)(2,1)S(1)}, u32[]{:S(2)}, u32[]{:S(2)}) %collective-permute-start.8) | collective-permute-done | bytes 65568 | tf_op jit(solution)/shard_map/ppermute | solution.py:344
  160.9 2.0 %unpack.1 = f32[64,64,64]{2,1,0:T(8,128)} custom-call(bf16[32,64,128]{2,1,0:T(8,128)(2,1)S(1)} %all-to-all-done.4.pairs_ref), custom_call_target="tpu_custom_call" | custom-call | flops 1024 | bytes 1024 | tf_op jit(solution)/shard_map/unpack/pallas_call | solution.py:348
  (89 shorter events, 24.4 us)
Async XLA Ops:
  7.3 8.1 %copy-start.3 = (bf16[512,2048]{1,0:T(8,128)(2,1)S(1)}, bf16[512,2048]{1,0:T(8,128)(2,1)}, u32[]{:S(2)}) copy-start(bf16[512,2048]{1,0:T(8,128)(2,1)} %grad_hbm.1) | copy-start | bytes 6291460
  7.3 8.1 %copy-start.16 = (bf16[512,256]{1,0:T(8,128)(2,1)S(1)}, bf16[512,256]{1,0:T(8,128)(2,1)}, u32[]{:S(2)}) copy-start(bf16[512,256]{1,0:T(8,128)(2,1)} %acts_hbm.1) | copy-start | bytes 786436
  8.5 33.5 %copy-start = (bf16[8192,128]{1,0:T(8,128)(2,1)}, bf16[8192,128]{1,0:T(8,128)(2,1)S(1)}, u32[]{:S(2)}) copy-start(bf16[8192,128]{1,0:T(8,128)(2,1)S(1)} %turn_input.1.xt_ref) | copy-start | bytes 6291460
  8.5 33.5 %collective-permute-start = (bf16[8192,128]{1,0:T(8,128)(2,1)S(1)}, bf16[8192,128]{1,0:T(8,128)(2,1)}, u32[]{:S(2)}, u32[]{:S(2)}) collective-permute-start(bf16[8192,128]{1,0:T(8,128)(2,1)S(1)} %turn_input.1.xt_ref), channel_id=1, source_target_pairs={{0,4},{4,0},{1,5},{5,1},{2,6},{6,2},{3,7},{7,3},{8,12},{12,8},{9,1... | collective-permute-start | bytes 6291464 | tf_op jit(solution)/shard_map/ppermute | solution.py:340
  11.8 13.4 %collective-permute-start.1 = (bf16[144,256]{1,0:T(8,128)(2,1)}, bf16[144,256]{1,0:T(8,128)(2,1)S(1)}, u32[]{:S(2)}, u32[]{:S(2)}) collective-permute-start(bf16[144,256]{1,0:T(8,128)(2,1)} %get-tuple-element.24), channel_id=1, source_target_pairs={{0,1},{1,0},{2,3},{3,2},{4,5},{5,4},{6,7},{7,6},{8,9},{9,8},{10,11... | collective-permute-start | bytes 221192 | tf_op jit(solution)/shard_map/ppermute | solution.py:344
  11.8 16.9 %collective-permute-start.2 = (bf16[144,256]{1,0:T(8,128)(2,1)}, bf16[144,256]{1,0:T(8,128)(2,1)S(1)}, u32[]{:S(2)}, u32[]{:S(2)}) collective-permute-start(bf16[144,256]{1,0:T(8,128)(2,1)} %get-tuple-element.25), channel_id=1, source_target_pairs={{0,2},{1,3},{2,0},{3,1},{4,6},{5,7},{6,4},{7,5},{8,10},{9,11},{10,... | collective-permute-start | bytes 221192 | tf_op jit(solution)/shard_map/ppermute | solution.py:344
  14.8 14.6 %copy-start.19 = (bf16[144,256]{1,0:T(8,128)(2,1)S(1)}, bf16[144,256]{1,0:T(8,128)(2,1)}, u32[]{:S(2)}) copy-start(bf16[144,256]{1,0:T(8,128)(2,1)} %get-tuple-element.23.after_ref.refs_0_) | copy-start | bytes 221188
  14.8 14.0 %collective-permute-start.3 = (bf16[144,256]{1,0:T(8,128)(2,1)S(1)}, bf16[144,256]{1,0:T(8,128)(2,1)S(1)}, u32[]{:S(2)}, u32[]{:S(2)}) collective-permute-start(bf16[144,256]{1,0:T(8,128)(2,1)S(1)} %copy-done.23), channel_id=1, source_target_pairs={{0,3},{1,2},{2,1},{3,0},{4,7},{5,6},{6,5},{7,4},{8,11},{9,10},{10,... | collective-permute-start | bytes 221192 | tf_op jit(solution)/shard_map/ppermute | solution.py:344
  17.7 24.3 %all-to-all-start = ((bf16[32,8,2048]{2,1,0:T(8,128)(2,1)}), bf16[32,8,2048]{2,1,0:T(8,128)(2,1)S(1)}, u32[]{:S(2)}, u32[]{:S(2)}) async-start(bf16[32,8,2048]{2,1,0:T(8,128)(2,1)} %bitcast.12), calls=%async_computation | async-start | bytes 2097152 | tf_op jit(solution)/shard_map/all_to_all | solution.py:412
  24.8 26.0 %collective-permute-start.11 = (bf16[128,2048]{1,0:T(8,128)(2,1)}, bf16[128,2048]{1,0:T(8,128)(2,1)}, u32[]{:S(2)}, u32[]{:S(2)}) collective-permute-start(bf16[128,2048]{1,0:T(8,128)(2,1)} %get-tuple-element.33), channel_id=1, source_target_pairs={{0,1},{1,0},{2,3},{3,2},{4,5},{5,4},{6,7},{7,6},{8,9},{9,8},{10,11... | collective-permute-start | bytes 1572872 | tf_op jit(solution)/shard_map/ppermute | solution.py:344
  25.3 16.7 %copy-start.20 = (s32[6]{0:T(128)S(1)}, s32[6]{0:T(128)}, u32[]{:S(2)}) copy-start(s32[6]{0:T(128)} %stack.23.place) | copy-start | bytes 76
  25.3 25.7 %collective-permute-start.12 = (bf16[128,2048]{1,0:T(8,128)(2,1)}, bf16[128,2048]{1,0:T(8,128)(2,1)}, u32[]{:S(2)}, u32[]{:S(2)}) collective-permute-start(bf16[128,2048]{1,0:T(8,128)(2,1)} %get-tuple-element.34), channel_id=1, source_target_pairs={{0,2},{1,3},{2,0},{3,1},{4,6},{5,7},{6,4},{7,5},{8,10},{9,11},{10,... | collective-permute-start | bytes 1572872 | tf_op jit(solution)/shard_map/ppermute | solution.py:344
  31.5 13.8 %copy-start.15 = (bf16[128,256]{1,0:T(8,128)(2,1)}, bf16[128,256]{1,0:T(8,128)(2,1)S(1)}, u32[]{:S(2)}) copy-start(bf16[128,256]{1,0:T(8,128)(2,1)S(1)} %get-tuple-element.27.low_ref) | copy-start | bytes 196612
  31.6 39.7 %copy-start.17 = (s32[32,256]{1,0:T(8,128)}, s32[32,256]{1,0:T(8,128)S(1)}, u32[]{:S(2)}) copy-start(s32[32,256]{1,0:T(8,128)S(1)} %get-tuple-element.30.table) | copy-start | bytes 98308
  31.6 1.8 %collective-permute-start.4 = (bf16[128,256]{1,0:T(8,128)(2,1)S(1)}, bf16[128,256]{1,0:T(8,128)(2,1)S(1)}, u32[]{:S(2)}, u32[]{:S(2)}) collective-permute-start(bf16[128,256]{1,0:T(8,128)(2,1)S(1)} %get-tuple-element.27.low_ref), channel_id=1, source_target_pairs={{0,4},{4,0},{1,5},{5,1},{2,6},{6,2},{3,7},{7,3},{8,12},{12,8},{9,1... | collective-permute-start | bytes 196616 | tf_op jit(solution)/shard_map/ppermute | solution.py:340
  46.7 36.7 %all-to-all-start.1 = ((bf16[16,256,256]{2,1,0:T(8,128)(2,1)}), bf16[16,256,256]{2,1,0:T(8,128)(2,1)S(1)}, u32[]{:S(2)}, u32[]{:S(2)}) async-start(bf16[16,256,256]{2,1,0:T(8,128)(2,1)} %copy-done.5), calls=%async_computation.1 | async-start | bytes 4194304 | tf_op jit(solution)/shard_map/all_to_all | solution.py:424
  50.4 5.0 %collective-permute-start.13 = (bf16[128,2048]{1,0:T(8,128)(2,1)}, bf16[128,2048]{1,0:T(8,128)(2,1)S(1)}, u32[]{:S(2)}, u32[]{:S(2)}) collective-permute-start(bf16[128,2048]{1,0:T(8,128)(2,1)} %get-tuple-element.32.refs_0_), channel_id=1, source_target_pairs={{0,4},{4,0},{1,5},{5,1},{2,6},{6,2},{3,7},{7,3},{8,12},{12,8},{9,1... | collective-permute-start | bytes 1572872 | tf_op jit(solution)/shard_map/ppermute | solution.py:340
  50.9 4.6 %collective-permute-start.14 = (bf16[128,2048]{1,0:T(8,128)(2,1)}, bf16[128,2048]{1,0:T(8,128)(2,1)S(1)}, u32[]{:S(2)}, u32[]{:S(2)}) collective-permute-start(bf16[128,2048]{1,0:T(8,128)(2,1)} %collective-permute-done.11.refs_1_), channel_id=1, source_target_pairs={{0,4},{4,0},{1,5},{5,1},{2,6},{6,2},{3,7},{7,3},{8,12},{12,8},{9,1... | collective-permute-start | bytes 1572872 | tf_op jit(solution)/shard_map/ppermute | solution.py:340
  51.0 4.4 %collective-permute-start.15 = (bf16[128,2048]{1,0:T(8,128)(2,1)}, bf16[128,2048]{1,0:T(8,128)(2,1)S(1)}, u32[]{:S(2)}, u32[]{:S(2)}) collective-permute-start(bf16[128,2048]{1,0:T(8,128)(2,1)} %collective-permute-done.12.refs_2_), channel_id=1, source_target_pairs={{0,4},{4,0},{1,5},{5,1},{2,6},{6,2},{3,7},{7,3},{8,12},{12,8},{9,1... | collective-permute-start | bytes 1572872 | tf_op jit(solution)/shard_map/ppermute | solution.py:340
  53.2 15.6 %collective-permute-start.10 = (bf16[128,2048]{1,0:T(8,128)(2,1)}, bf16[128,2048]{1,0:T(8,128)(2,1)S(1)}, u32[]{:S(2)}, u32[]{:S(2)}) collective-permute-start(bf16[128,2048]{1,0:T(8,128)(2,1)} %get-tuple-element.31), channel_id=1, source_target_pairs={{0,3},{1,2},{2,1},{3,0},{4,7},{5,6},{6,5},{7,4},{8,11},{9,10},{10,... | collective-permute-start | bytes 1572872 | tf_op jit(solution)/shard_map/ppermute | solution.py:344
  68.8 2.4 %collective-permute-start.16 = (bf16[128,2048]{1,0:T(8,128)(2,1)S(1)}, bf16[128,2048]{1,0:T(8,128)(2,1)S(1)}, u32[]{:S(2)}, u32[]{:S(2)}) collective-permute-start(bf16[128,2048]{1,0:T(8,128)(2,1)S(1)} %gate.1.refs_0_.after_ref), channel_id=1, source_target_pairs={{0,4},{4,0},{1,5},{5,1},{2,6},{6,2},{3,7},{7,3},{8,12},{12,8},{9,1... | collective-permute-start | bytes 1572872 | tf_op jit(solution)/shard_map/ppermute | solution.py:340
  83.4 20.1 %all-to-all-start.2 = ((bf16[16,4,64,128]{3,2,1,0:T(8,128)(2,1)}), bf16[16,4,64,128]{3,2,1,0:T(8,128)(2,1)}, u32[]{:S(2)}, u32[]{:S(2)}) async-start(bf16[16,4,64,128]{3,2,1,0:T(8,128)(2,1)} %join.1), calls=%async_computation.2 | async-start | bytes 2097152 | tf_op jit(solution)/shard_map/all_to_all | solution.py:469
  91.5 29.6 %collective-permute-start.17 = (bf16[32,64,128]{2,1,0:T(8,128)(2,1)}, bf16[32,64,128]{2,1,0:T(8,128)(2,1)}, u32[]{:S(2)}, u32[]{:S(2)}) collective-permute-start(bf16[32,64,128]{2,1,0:T(8,128)(2,1)} %pack.1.refs_3_), channel_id=1, source_target_pairs={{0,1},{1,2},{2,3},{3,128},{128,129},{129,130},{130,131},{131,0},{4... | collective-permute-start | bytes 1572872 | tf_op jit(solution)/shard_map/ppermute | solution.py:477
  96.6 24.5 %collective-permute-start.18 = (bf16[32,64,128]{2,1,0:T(8,128)(2,1)}, bf16[32,64,128]{2,1,0:T(8,128)(2,1)}, u32[]{:S(2)}, u32[]{:S(2)}) collective-permute-start(bf16[32,64,128]{2,1,0:T(8,128)(2,1)} %pack.1.refs_3_), channel_id=1, source_target_pairs={{0,131},{1,0},{2,1},{3,2},{128,3},{129,128},{130,129},{131,130},{4... | collective-permute-start | bytes 1572872 | tf_op jit(solution)/shard_map/ppermute | solution.py:478
  96.6 25.7 %collective-permute-start.19 = (bf16[32,64,128]{2,1,0:T(8,128)(2,1)}, bf16[32,64,128]{2,1,0:T(8,128)(2,1)}, u32[]{:S(2)}, u32[]{:S(2)}) collective-permute-start(bf16[32,64,128]{2,1,0:T(8,128)(2,1)} %pack.1.refs_3_), channel_id=1, source_target_pairs={{0,2},{4,134},{1,3},{5,135},{2,128},{6,4},{3,129},{7,5},{128,130},... | collective-permute-start | bytes 1572872 | tf_op jit(solution)/shard_map/ppermute | solution.py:479
  105.5 29.9 %all-to-all-start.3 = ((bf16[8,64,128]{2,1,0:T(8,128)(2,1)}), bf16[8,64,128]{2,1,0:T(8,128)(2,1)S(1)}, u32[]{:S(2)}, u32[]{:S(2)}) async-start(bf16[8,64,128]{2,1,0:T(8,128)(2,1)} %stage.1), calls=%async_computation.3 | async-start | bytes 262144 | tf_op jit(solution)/shard_map/all_to_all | solution.py:503
  115.5 19.8 %collective-permute-start.5 = (bf16[128,256]{1,0:T(8,128)(2,1)S(1)}, bf16[128,256]{1,0:T(8,128)(2,1)S(1)}, u32[]{:S(2)}, u32[]{:S(2)}) collective-permute-start(bf16[128,256]{1,0:T(8,128)(2,1)S(1)} %get-tuple-element.29.after_ref), channel_id=1, source_target_pairs={{0,128},{128,0},{1,129},{129,1},{2,130},{130,2},{3,131},{131,3},{4... | collective-permute-start | bytes 196616 | tf_op jit(solution)/shard_map/ppermute | solution.py:340
  137.8 23.1 %all-to-all-start.4 = ((bf16[32,64,128]{2,1,0:T(8,128)(2,1)}), bf16[32,64,128]{2,1,0:T(8,128)(2,1)S(1)}, u32[]{:S(2)}, u32[]{:S(2)}) async-start(bf16[32,64,128]{2,1,0:T(8,128)(2,1)} %last.1), calls=%async_computation.4 | async-start | bytes 1048576 | tf_op jit(solution)/shard_map/all_to_all | solution.py:508
  149.1 6.8 %collective-permute-start.9 = (f32[4,2048]{1,0:T(4,128)S(1)}, f32[4,2048]{1,0:T(4,128)S(1)}, u32[]{:S(2)}, u32[]{:S(2)}) collective-permute-start(f32[4,2048]{1,0:T(4,128)S(1)} %dynamic-slice_bitcast_fusion), channel_id=1, source_target_pairs={{0,128},{128,0},{1,129},{129,1},{2,130},{130,2},{3,131},{131,3},{4... | collective-permute-start | bytes 98312 | tf_op jit(solution)/shard_map/ppermute | solution.py:340
  151.6 4.9 %collective-permute-start.6 = (bf16[128,256]{1,0:T(8,128)(2,1)S(1)}, bf16[128,256]{1,0:T(8,128)(2,1)S(1)}, u32[]{:S(2)}, u32[]{:S(2)}) collective-permute-start(bf16[128,256]{1,0:T(8,128)(2,1)S(1)} %down_half.1.refs_0_.after_too_ref), channel_id=1, source_target_pairs={{0,1},{1,0},{2,3},{3,2},{4,5},{5,4},{6,7},{7,6},{8,9},{9,8},{10,11... | collective-permute-start | bytes 196616 | tf_op jit(solution)/shard_map/ppermute | solution.py:344
  152.6 4.3 %collective-permute-start.7 = (bf16[128,256]{1,0:T(8,128)(2,1)S(1)}, bf16[128,256]{1,0:T(8,128)(2,1)S(1)}, u32[]{:S(2)}, u32[]{:S(2)}) collective-permute-start(bf16[128,256]{1,0:T(8,128)(2,1)S(1)} %down_half.1.refs_0_.after_too_ref), channel_id=1, source_target_pairs={{0,2},{1,3},{2,0},{3,1},{4,6},{5,7},{6,4},{7,5},{8,10},{9,11},{10,... | collective-permute-start | bytes 196616 | tf_op jit(solution)/shard_map/ppermute | solution.py:344
  154.3 5.9 %collective-permute-start.8 = (bf16[128,256]{1,0:T(8,128)(2,1)S(1)}, bf16[128,256]{1,0:T(8,128)(2,1)S(1)}, u32[]{:S(2)}, u32[]{:S(2)}) collective-permute-start(bf16[128,256]{1,0:T(8,128)(2,1)S(1)} %down_half.1.refs_0_.after_too_ref), channel_id=1, source_target_pairs={{0,3},{1,2},{2,1},{3,0},{4,7},{5,6},{6,5},{7,4},{8,11},{9,10},{10,... | collective-permute-start | bytes 196616 | tf_op jit(solution)/shard_map/ppermute | solution.py:344
  (17 other events, 38.0 us)

commit v3 on v2

--- a/solution.py
+++ b/solution.py
@@ -21,7 +21,7 @@
 MIB = 1024 * 1024
 
 
-GUESS = {"delta_last": 8.0, "delta_most": 0.0, "low": 10.0, "grad_input": 0.0, "stage": 0.0, "pack": 0.0, "values": 0.0}
+GUESS = {"delta_last": 0.0, "delta_most": 0.0, "low": 10.0, "grad_input": 0.0, "stage": 0.0, "pack": 0.0, "values": 20.0, "gate": 12.0}
 
 
 def whole():
@@ -86,7 +86,7 @@
         give.wait()
 
 
-def up_kernel(grad_hbm, acts_hbm, out_ref, grad_ref, acts_ref, sems):
+def up_kernel(place, grad_hbm, acts_hbm, keep_ref, give_ref, grad_ref, acts_ref, sems):
     copies = [
         pltpu.make_async_copy(acts_hbm, acts_ref, sems.at[0]),
         pltpu.make_async_copy(grad_hbm, grad_ref, sems.at[1]),
@@ -95,10 +95,11 @@
         copy.start()
     copies[0].wait()
     rank = acts_ref.shape[1]
+    half = rank // C
     here = lax.broadcasted_iota(jnp.int32, (rank, rank), 1)
-    chunk, zh = here >> 3, (here >> 2) & 1
+    core, yx, zh = (here >> 7) ^ place[0], (here >> 3) & (XY - 1), (here >> 2) & 1
     order = lax.broadcasted_iota(jnp.int32, (rank, rank), 0) == (
-        ((zh * (XY * C) + chunk) << 2) + (here & 3)
+        (((zh * XY + yx) * C + core) << 2) + (here & 3)
     )
     order = jnp.where(order, 1.0, 0.0).astype(BF16)
     acts = jnp.dot(acts_ref[...], order, preferred_element_type=F32).astype(BF16)
@@ -106,10 +107,12 @@
     step = 512
 
     def columns(i, carry):
-        out_ref[:, aligned(i, step)] = lax.dot_general(
+        part = lax.dot_general(
             acts, grad_ref[:, aligned(i, step)], (((0,), (0,)), ((), ())),
             preferred_element_type=F32,
-        ).astype(BF16)
+        )
+        keep_ref[:, aligned(i, step)] = part[:half]
+        give_ref[:, aligned(i, step)] = part[half:].astype(BF16)
         return carry
 
     lax.fori_loop(0, grad_ref.shape[1] // step, columns, 0, unroll=2)
@@ -129,7 +132,7 @@
     pass
 
 
-def pack_kernel(values_ref, after_ref, out_ref):
+def pack_kernel(values_ref, out_ref):
     def one(p, carry):
         out_ref[p] = jnp.concatenate([values_ref[p], values_ref[p + PAIRS]], axis=1)
         return carry
@@ -137,18 +140,23 @@
     lax.fori_loop(0, PAIRS, one, 0, unroll=4)
 
 
-def down_sum_kernel(place, down_ref, keep_ref, give_ref):
-    rows = down_ref.shape[1] // ZH
-    for mine in range(2):
-        zh = place[5] ^ (1 - mine)
-        at = aligned(zh, rows)
-        total = down_ref[0, at, :].astype(F32)
+def down_sum_kernel(place, down_ref, keep_ref, give_ref, up_keep_ref, up_give_ref):
+    def total(at):
+        part = down_ref[0, at, :].astype(F32)
         for i in range(1, XY):
-            total += down_ref[i, at, :].astype(F32)
-        if mine:
-            keep_ref[...] = total
-        else:
-            give_ref[...] = total.astype(BF16)
+            part += down_ref[i, at, :].astype(F32)
+        return part
+
+    zh = place[5]
+    keep_ref[...] = total(aligned(zh, 128))
+    give_ref[...] = total(aligned(1 - zh, 128)).astype(BF16)
+    up = total(slice(256, None))
+    rank = up.shape[1]
+    for j in range(up.shape[0] // 8):
+        low, high = up[j * 8 : j * 8 + 4], up[j * 8 + 4 : j * 8 + 8]
+        at = slice(j * rank, (j + 1) * rank)
+        up_keep_ref[:, at] = jnp.where(zh == 0, low, high)
+        up_give_ref[:, at] = jnp.where(zh == 0, high, low)
 
 
 def down_half_kernel(keep_ref, far_ref, out_ref):
@@ -162,7 +170,8 @@
     refs[-1][...] = total
 
 
-def stage_kernel(place, delta_ref, after_ref, out_ref, sum_ref):
+def stage_kernel(place, delta_ref, *refs):
+    out_ref, sum_ref = refs[-2:]
     for k in range(T):
         total = delta_ref[0, k].astype(F32)
         for i in range(1, XY):
@@ -193,20 +202,30 @@
     lax.fori_loop(0, PAIRS, one, 0, unroll=4)
 
 
-def down_kernel(place, xt_ref, xt_far_ref, low_ref, low_far_ref, *refs):
-    out_ref = refs[-1]
+def down_kernel(
+    place, xt_ref, xt_far_ref, low_ref, low_far_ref, up_ref, up_far_ref, out_hbm, out_ref, sems
+):
     low, low_far = low_ref[...], low_far_ref[...]
     core = place[0]
-
-    def block(i, carry):
+    rank = low.shape[1]
+    copies = []
+    for i in range(XY):
         for zh in range(ZH):
             at = aligned((zh * XY + i) * C + core, 128)
             total = jnp.dot(xt_ref[at, :], low, preferred_element_type=F32)
             total += jnp.dot(xt_far_ref[at, :], low_far, preferred_element_type=F32)
             out_ref[i, zh * 128 : (zh + 1) * 128] = total.astype(BF16)
-        return carry
-
-    lax.fori_loop(0, XY, block, 0, unroll=4)
+        if i % 2 == 0:
+            at = slice(i * 8, i * 8 + 16)
+            up = up_ref[at, :] + up_far_ref[at, :].astype(F32)
+        mine = up[i % 2 * 8 : i % 2 * 8 + 8]
+        for j in range(0, mine.shape[1] // rank, 2):
+            two = [mine[:, (j + n) * rank : (j + n + 1) * rank] for n in range(2)]
+            out_ref[i, 256 + j * 8 : 256 + j * 8 + 16] = jnp.concatenate(two, axis=0).astype(BF16)
+        copies.append(pltpu.make_async_copy(out_ref.at[i], out_hbm.at[i], sems.at[i]))
+        copies[-1].start()
+    for copy in copies:
+        copy.wait()
 
 
 def delta_kernel(pieces, place, table, xt_ref, xt_far_ref, *refs):
@@ -263,7 +282,7 @@
 
 def input_kernel(place, table, low_ref, *refs):
     from_hbm = refs[:7]
-    out_ref, acc_ref, down_ref, gt_ref, values, sems = refs[7:]
+    out_hbm, acc_ref, down_ref, gt_ref, values, out_ref, sems = refs[7:]
     most = from_hbm[1].shape[0]
     to_vmem = (
         down_ref, gt_ref.at[:most], gt_ref.at[most:], values.at[0], values.at[1], values.at[2], values.at[3],
@@ -319,11 +338,18 @@
 
     lax.fori_loop(0, PAIRS // 2, pair, 0)
 
-    def turn(i, carry):
-        out_ref[:, aligned(i, 128)] = acc_ref[aligned(i, 128), :].T.astype(BF16)
-        return carry
-
-    lax.fori_loop(0, acc_ref.shape[0] // 128, turn, 0, unroll=4)
+    gives = []
+    step = 1024
+    for j in range(0, out_ref.shape[1], step):
+        for i in range(j, j + step, 128):
+            out_ref[:, i : i + 128] = acc_ref[i : i + 128, :].T.astype(BF16)
+        at = pl.ds(j, step)
+        gives.append(
+            pltpu.make_async_copy(out_ref.at[:, at], out_hbm.at[:, at], sems.at[7 + j // step])
+        )
+        gives[-1].start()
+    for give in gives:
+        give.wait()
 
 
 def ring(shift_of_core):
@@ -394,38 +420,38 @@
     )
     xt_far = swap(xt)
 
-    up_part = call(
-        up_kernel, "up_part", shape((rank, width), BF16), [anywhere()] * 2, grad, acts,
+    half = shape((rank // C, width), BF16)
+    up_keep, up_give = call(
+        up_kernel, "up_part", (shape(half.shape, F32), half), [scalars()] + [anywhere()] * 2,
+        place, grad, acts,
         scratch=[
             pltpu.VMEM(grad.shape, BF16),
             pltpu.VMEM(acts.shape, BF16),
             pltpu.SemaphoreType.DMA((2,)),
         ],
     )
+    up_got = swap(up_give)
 
     low, table = call(
         low_kernel, "low", (shape((TOK, rank), BF16), shape((8 * T, rank), jnp.int32)),
-        [whole()] * T + [anywhere()], *parts, up_part,
+        [whole()] * T + [anywhere()], *parts, up_give,
     )
     low_far = swap(low)
 
-    up_all = lax.all_to_all(
-        up_part.reshape(XY * C, ZH * 4, width), ("y", "x", "c"), 0, 0, tiled=True
-    )
-    up_sum = jnp.sum(up_all.astype(F32), axis=0).reshape(ZH, 4, width)
-    up_far = swap(lax.dynamic_index_in_dim(up_sum, 1 - zh, 0, keepdims=False), "zh")
-    up_grad = lax.dynamic_index_in_dim(up_sum, zh, 0, keepdims=False) + up_far
-
+    size = XY, ZH * 128 + ZH * 4 * width // rank, rank
     down_part = call(
-        down_kernel, "down_part", shape((XY, ZH * 128, rank), BF16),
-        [scalars()] + [whole()] * 4 + [anywhere()], place, xt, xt_far, low, low_far,
-        up_all,
+        down_kernel, "down_part", shape(size, BF16), [scalars()] + [whole()] * 6,
+        place, xt, xt_far, low, low_far, up_keep, up_got,
+        out_specs=anywhere(),
+        scratch=[pltpu.VMEM(size, BF16), pltpu.SemaphoreType.DMA((XY,))],
     )
     down_all = lax.all_to_all(down_part, ("y", "x"), 0, 0, tiled=True)
-    down_keep, down_give = call(
-        down_sum_kernel, "down_sum", (shape((128, rank), F32), shape((128, rank), BF16)),
+    down_keep, down_give, up_sum, up_give = call(
+        down_sum_kernel, "down_sum",
+        (shape((128, rank), F32), shape((128, rank), BF16)) + (shape((4, width), F32),) * 2,
         [scalars(), whole()], place, down_all,
     )
+    up_grad = up_sum + swap(up_give, "zh")
     down_half = call(
         down_half_kernel, "down_half", shape((128, rank), BF16), [whole()] * 2,
         down_keep, swap(down_give, "zh"),
@@ -469,8 +495,7 @@
     delta_all = lax.all_to_all(delta_part, ("y", "x"), 0, 0, tiled=True)
 
     packed = call(
-        pack_kernel, "pack", shape((PAIRS, BLK, 2 * BLK), BF16), [whole(), anywhere()],
-        values[0], near[3],
+        pack_kernel, "pack", shape((PAIRS, BLK, 2 * BLK), BF16), [whole()], values[0],
     )
     axes = ("zh", "t")
     got = [
@@ -486,24 +511,26 @@
         input_kernel, "grad_input", shape((TOK, feat), BF16),
         [scalars()] * 2 + [whole()] + [anywhere()] * 7,
         place, table, low, down, grad_most, grad_last, packed, *got, room=56,
+        out_specs=anywhere(),
         scratch=[
             pltpu.VMEM((feat, TOK), F32),
             pltpu.VMEM(down.shape, BF16),
             pltpu.VMEM((T * width, TOK), BF16),
             pltpu.VMEM((T, PAIRS, BLK, 2 * BLK), BF16),
-            pltpu.SemaphoreType.DMA((7,)),
+            pltpu.VMEM((TOK, feat), BF16),
+            pltpu.SemaphoreType.DMA((7 + feat // 1024,)),
         ],
     )
 
     stage = call(
         stage_kernel, "stage", shape((ZH * T, BLK, 128), BF16),
-        [scalars(), whole(), anywhere()], place, delta_all, down_give,
+        [scalars(), whole()] + [anywhere()] * 2, place, delta_all, down_half, got[0],
         scratch=[pltpu.VMEM((T, BLK, 2 * BLK), F32)],
     )
     stage_all = lax.all_to_all(stage, ("zh", "t"), 0, 0, tiled=True)
     delta_one = call(
         last_kernel, "last", shape((PAIRS, BLK, 2 * BLK), BF16), [whole()] + [anywhere()] * 2,
-        stage_all, grad_input, down_half,
+        stage_all, down_grad, up_grad,
     )
     delta_full = lax.all_to_all(delta_one, ("y", "x", "c"), 0, 0, tiled=True)
     grad_delta = call(

time: 164 us -> 147 us (0.90)
  starting transfers between devices: 74.9 us -> 66.3 us
  local copies, waits for them, and re-layouts: 14.6 us -> 8.06 us
  waiting for transfers between devices: 30 us -> 27.8 us
    all_to_all x1 -> x0, waiting for transfers between devices: 8.67 us -> none  [per_device(): lax.all_to_all(up_part.reshape(XY * C, ZH * 4, width), ('y', 'x', 'c'), 0...]
    all_to_all x1 -> x0, starting transfers between devices: 7.09 us -> none  [per_device(): lax.all_to_all(up_part.reshape(XY * C, ZH * 4, width), ('y', 'x', 'c'), 0...]
    all_to_all x1, waiting for transfers between devices: 6.7 us -> 0.01 us  [per_device(): down_all = lax.all_to_all(down_part, ('y', 'x'), 0, 0, tiled=True)]
    unnamed x48 -> x44, local copies, waits for them, and re-layouts: 14 us -> 7.41 us
    ppermute x1, waiting for transfers between devices: 1.2 us -> 7 us  [per_device(): lax.ppermute(packed, ('zh', 'c', 't'), ring((2, -2)))]
    all_to_all x1, starting transfers between devices: 10.1 us -> 4.37 us  [per_device(): stage_all = lax.all_to_all(stage, ('zh', 't'), 0, 0, tiled=True)]
    all_to_all x1, starting transfers between devices: 11.2 us -> 6.15 us  [per_device(): delta_full = lax.all_to_all(delta_one, ('y', 'x', 'c'), 0, 0, tiled=True)]
    ppermute x1, starting transfers between devices: 5.08 us -> 9.05 us  [per_device(): lax.ppermute(packed, axes, [(i, (i + 1) % (ZH * T)) for i in range(ZH * T)])]
  transfers between devices with their start and end apart: 25 -> 25, of which waited for: 10 -> 7; matrix products, arithmetic and copies ran while one was open for 0% -> 0% of each run, Pallas kernels for 20% -> 22%
where the time goes in v3:
time: 147 us; the launch traced here: 146 us
  starting transfers between devices  66.3 us (45%)
  Pallas kernels  42.5 us (29%)
  waiting for transfers between devices  27.8 us (19%)
  local copies, waits for them, and re-layouts  8.06 us (5%)
  between operations  1.63 us (1%)
    pallas_call x18, Pallas kernels, call(): pl.pallas_call(kernel, out_shape=outs, in_specs=in_specs, out_specs=out_s...  42.5 us
    ppermute x9, starting transfers between devices, swap(): return lax.ppermute(array, axis, [(0, 1), (1, 0)])  15.4 us
    ppermute x9, starting transfers between devices, cross(): return lax.ppermute(array, 't', [(i, i ^ k) for i in range(T)])  13.1 us
    ppermute x1, starting transfers between devices, per_device(): lax.ppermute(packed, axes, [(i, (i + 1) % (ZH * T)) for i in range(ZH * T)])  9.05 us
    ppermute x9, waiting for transfers between devices, cross(): return lax.ppermute(array, 't', [(i, i ^ k) for i in range(T)])  8.94 us
    unnamed x44, local copies, waits for them, and re-layouts  7.41 us
    ppermute x1, waiting for transfers between devices, per_device(): lax.ppermute(packed, ('zh', 'c', 't'), ring((2, -2)))  7 us
    all_to_all x1, starting transfers between devices, per_device(): down_all = lax.all_to_all(down_part, ('y', 'x'), 0, 0, tiled=True)  6.94 us
  transfers between devices with their start and end apart: 25, of which 7 were waited for; matrix products, arithmetic and copies ran while one was open for 0% of the time, Pallas kernels for 22%

profile of v3, /device:TPU:1, one launch (start us, length us, event | category | flops | bytes accessed | tf_op | source)
XLA Modules:
  0.0 146.3 jit_solution(15723149797850589768)
XLA Ops:
  2.0 4.5 %front.1 = (bf16[144,256]{1,0:T(8,128)(2,1)}, bf16[144,256]{1,0:T(8,128)(2,1)}, bf16[144,256]{1,0:T(8,128)(2,1)}, bf16[144,256]{1,0:T(8,128)(2,1)}, bf16[128,204...) custom-call(s32[6]{0:T(128)} %stack.23.place, ...), custom_call_target="tpu_custom_call" | custom-call | flops 1024 | bytes 1024 | tf_op jit(solution)/shard_map/front/pallas_call | solution.py:374
  8.6 3.3 %collective-permute-start = (bf16[8192,128]{1,0:T(8,128)(2,1)S(1)}, bf16[8192,128]{1,0:T(8,128)(2,1)S(1)}, u32[]{:S(2)}, u32[]{:S(2)}) collective-permute-start(bf16[8192,128]{1,0:T(8,128)(2,1)S(1)} %turn_input.1.xt_ref), channel_id=1, source_target_pairs={{0,4},{4,0},{1,5},{5,1},{2,6},{6,2},{3,7},{7,3},{8,12},{12,8},{9,1... | collective-permute-start | bytes 6291464 | tf_op jit(solution)/shard_map/ppermute | solution.py:366
  11.9 2.9 %collective-permute-start.2 = (bf16[144,256]{1,0:T(8,128)(2,1)S(1)}, bf16[144,256]{1,0:T(8,128)(2,1)S(1)}, u32[]{:S(2)}, u32[]{:S(2)}) collective-permute-start(bf16[144,256]{1,0:T(8,128)(2,1)S(1)} %copy-done.20), channel_id=1, source_target_pairs={{0,2},{1,3},{2,0},{3,1},{4,6},{5,7},{6,4},{7,5},{8,10},{9,11},{10,... | collective-permute-start | bytes 221192 | tf_op jit(solution)/shard_map/ppermute | solution.py:370
  15.5 1.9 %up_part.1 = (f32[128,2048]{1,0:T(8,128)S(1)}, bf16[128,2048]{1,0:T(8,128)(2,1)S(1)}) custom-call(s32[6]{0:T(128)S(1)} %copy-done.18, bf16[512,2048]{1,0:T(8,128)(2,1)S(1)} %copy-done.4, bf16[512,256]{1,0:T(8,128)(2,1)S(1)} %copy-done.15), custom_call_target="tpu_custom_call" | custom-call | flops 1024 | bytes 1024 | tf_op jit(solution)/shard_map/up_part/pallas_call | solution.py:374
  17.4 3.0 %collective-permute-start.13 = (bf16[128,2048]{1,0:T(8,128)(2,1)}, bf16[128,2048]{1,0:T(8,128)(2,1)}, u32[]{:S(2)}, u32[]{:S(2)}) collective-permute-start(bf16[128,2048]{1,0:T(8,128)(2,1)} %get-tuple-element.42), channel_id=1, source_target_pairs={{0,2},{1,3},{2,0},{3,1},{4,6},{5,7},{6,4},{7,5},{8,10},{9,11},{10,... | collective-permute-start | bytes 1572872 | tf_op jit(solution)/shard_map/ppermute | solution.py:370
  20.4 1.5 collective-permute-start.5
  23.5 7.3 %down_part.1 = bf16[16,320,256]{2,1,0:T(8,128)(2,1)S(1)} custom-call(s32[6]{0:T(128)S(1)} %copy-done.18, bf16[8192,128]{1,0:T(8,128)(2,1)S(1)} %turn_input.1.xt_ref, bf16[8192,128]{1,0:T(8,128)(2,1)S(1)} %collective-permute-done.xt_far_ref, bf16[128,256]{1,0:T(8,128)(2,1)S(1)} %get-tuple-element.32.low_ref, ...), custom_call_target="tpu_custom_call" | custom-call | flops 1024 | bytes 1024 | tf_op jit(solution)/shard_map/down_part/pallas_call | solution.py:374
  30.9 1.3 copy-done
  32.2 1.5 %copy-done.3 = bf16[16,320,256]{2,1,0:T(8,128)(2,1)} copy-done((bf16[16,320,256]{2,1,0:T(8,128)(2,1)}, bf16[16,320,256]{2,1,0:T(8,128)(2,1)S(1)}, u32[]{:S(2)}) %copy-start.3) | copy-done | bytes 2621464
  33.7 6.9 %all-to-all-start = ((bf16[16,320,256]{2,1,0:T(8,128)(2,1)}), bf16[16,320,256]{2,1,0:T(8,128)(2,1)}, u32[]{:S(2)}, u32[]{:S(2)}) async-start(bf16[16,320,256]{2,1,0:T(8,128)(2,1)} %copy-done.3), calls=%async_computation | async-start | bytes 5242880 | tf_op jit(solution)/shard_map/all_to_all | solution.py:448
  41.9 2.3 %collective-permute-done.13.refs_2_ = bf16[128,2048]{1,0:T(8,128)(2,1)} collective-permute-done((bf16[128,2048]{1,0:T(8,128)(2,1)}, bf16[128,2048]{1,0:T(8,128)(2,1)}, u32[]{:S(2)}, u32[]{:S(2)}) %collective-permute-start.13) | collective-permute-done | bytes 524320 | tf_op jit(solution)/shard_map/ppermute | solution.py:370
  45.4 2.2 %collective-permute-start.11 = (bf16[128,2048]{1,0:T(8,128)(2,1)}, bf16[128,2048]{1,0:T(8,128)(2,1)S(1)}, u32[]{:S(2)}, u32[]{:S(2)}) collective-permute-start(bf16[128,2048]{1,0:T(8,128)(2,1)} %get-tuple-element.39), channel_id=1, source_target_pairs={{0,3},{1,2},{2,1},{3,0},{4,7},{5,6},{6,5},{7,4},{8,11},{9,10},{10,... | collective-permute-start | bytes 1572872 | tf_op jit(solution)/shard_map/ppermute | solution.py:370
  47.6 1.6 %copy-done.1 = bf16[8192,128]{1,0:T(8,128)(2,1)S(1)} copy-done((bf16[8192,128]{1,0:T(8,128)(2,1)S(1)}, bf16[8192,128]{1,0:T(8,128)(2,1)}, u32[]{:S(2)}) %copy-start.1) | copy-done | bytes 2097176
  49.2 5.2 %delta_most.1 = (bf16[16,4,64,128]{3,2,1,0:T(8,128)(2,1)}, bf16[6144,128]{1,0:T(8,128)(2,1)S(1)}) custom-call(s32[6]{0:T(128)S(1)} %copy-done.18, s32[32,256]{1,0:T(8,128)S(1)} %get-tuple-element.38.table, bf16[8192,128]{1,0:T(8,128)(2,1)S(1)} %turn_input.1.xt_ref, bf16[8192,128]{1,0:T(8,128)(2,1)S(1)} %copy-done.1, bf16[128,2048]{1,0:T(8,128)(2,1)S(1)} %copy-done.11, ...), custom_call_target="tpu_custom_call" | custom-call | flops 1024 | bytes 1024 | tf_op jit(solution)/shard_map/delta_most/pallas_call | solution.py:374
  54.5 6.6 %collective-permute-done.11.refs_0_ = bf16[128,2048]{1,0:T(8,128)(2,1)S(1)} collective-permute-done((bf16[128,2048]{1,0:T(8,128)(2,1)}, bf16[128,2048]{1,0:T(8,128)(2,1)S(1)}, u32[]{:S(2)}, u32[]{:S(2)}) %collective-permute-start.11) | collective-permute-done | bytes 524320 | tf_op jit(solution)/shard_map/ppermute | solution.py:370
  63.0 9.0 %collective-permute-start.18 = (bf16[32,64,128]{2,1,0:T(8,128)(2,1)S(1)}, bf16[32,64,128]{2,1,0:T(8,128)(2,1)S(1)}, u32[]{:S(2)}, u32[]{:S(2)}) collective-permute-start(bf16[32,64,128]{2,1,0:T(8,128)(2,1)S(1)} %pack.1.refs_3_), channel_id=1, source_target_pairs={{0,1},{1,2},{2,3},{3,128},{128,129},{129,130},{130,131},{131,0},{4... | collective-permute-start | bytes 1572872 | tf_op jit(solution)/shard_map/ppermute | solution.py:502
  72.1 4.6 %collective-permute-start.20 = (bf16[32,64,128]{2,1,0:T(8,128)(2,1)S(1)}, bf16[32,64,128]{2,1,0:T(8,128)(2,1)}, u32[]{:S(2)}, u32[]{:S(2)}) collective-permute-start(bf16[32,64,128]{2,1,0:T(8,128)(2,1)S(1)} %pack.1.refs_3_), channel_id=1, source_target_pairs={{0,2},{4,134},{1,3},{5,135},{2,128},{6,4},{3,129},{7,5},{128,130},... | collective-permute-start | bytes 1572872 | tf_op jit(solution)/shard_map/ppermute | solution.py:504
  76.7 3.3 %delta_last.1 = (bf16[16,4,64,128]{3,2,1,0:T(8,128)(2,1)}, bf16[2048,128]{1,0:T(8,128)(2,1)S(1)}) custom-call(s32[6]{0:T(128)S(1)} %copy-done.18, s32[32,256]{1,0:T(8,128)S(1)} %get-tuple-element.38.table, bf16[8192,128]{1,0:T(8,128)(2,1)S(1)} %turn_input.1.xt_ref, bf16[8192,128]{1,0:T(8,128)(2,1)S(1)} %copy-done.2, ...), custom_call_target="tpu_custom_call", output_to_operand_aliasing={{0}: (6, {})} | custom-call | flops 1024 | bytes 1024 | tf_op jit(solution)/shard_map/delta_last/pallas_call | solution.py:374
  80.8 6.8 %all-to-all-start.1 = ((bf16[16,4,64,128]{3,2,1,0:T(8,128)(2,1)}), bf16[16,4,64,128]{3,2,1,0:T(8,128)(2,1)S(1)}, u32[]{:S(2)}, u32[]{:S(2)}) async-start(bf16[16,4,64,128]{3,2,1,0:T(8,128)(2,1)} %join.1), calls=%async_computation.1 | async-start | bytes 2097152 | tf_op jit(solution)/shard_map/all_to_all | solution.py:495
  87.6 2.1 %down_sum.1 = (f32[128,256]{1,0:T(8,128)S(1)}, bf16[128,256]{1,0:T(8,128)(2,1)S(1)}, f32[4,2048]{1,0:T(4,128)S(1)}, f32[4,2048]{1,0:T(4,128)S(1)}) custom-call(s32[6]{0:T(128)S(1)} %copy-done.18, bf16[16,320,256]{2,1,0:T(8,128)(2,1)} %all-to-all-done.down_ref.refs_1_), custom_call_target="tpu_custom_call" | custom-call | flops 1024 | bytes 1024 | tf_op jit(solution)/shard_map/down_sum/pallas_call | solution.py:374
  89.7 2.1 %collective-permute-start.6 = (bf16[128,256]{1,0:T(8,128)(2,1)S(1)}, bf16[128,256]{1,0:T(8,128)(2,1)S(1)}, u32[]{:S(2)}, u32[]{:S(2)}) collective-permute-start(bf16[128,256]{1,0:T(8,128)(2,1)S(1)} %get-tuple-element.35), channel_id=1, source_target_pairs={{0,128},{128,0},{1,129},{129,1},{2,130},{130,2},{3,131},{131,3},{4... | collective-permute-start | bytes 196616 | tf_op jit(solution)/shard_map/ppermute | solution.py:366
  91.8 7.0 %collective-permute-done.20.refs_2_ = bf16[32,64,128]{2,1,0:T(8,128)(2,1)} collective-permute-done((bf16[32,64,128]{2,1,0:T(8,128)(2,1)S(1)}, bf16[32,64,128]{2,1,0:T(8,128)(2,1)}, u32[]{:S(2)}, u32[]{:S(2)}) %collective-permute-start.20) | collective-permute-done | bytes 524320 | tf_op jit(solution)/shard_map/ppermute | solution.py:504
  98.8 5.6 %all-to-all-done.1.delta_ref = bf16[16,4,64,128]{3,2,1,0:T(8,128)(2,1)S(1)} async-done(((bf16[16,4,64,128]{3,2,1,0:T(8,128)(2,1)}), bf16[16,4,64,128]{3,2,1,0:T(8,128)(2,1)S(1)}, u32[]{:S(2)}, u32[]{:S(2)}) %all-to-all-start.1) | async-done | bytes 1048608 | tf_op jit(solution)/shard_map/all_to_all | solution.py:495
  104.4 1.3 stage.1
  105.8 4.4 %all-to-all-start.2 = ((bf16[8,64,128]{2,1,0:T(8,128)(2,1)}), bf16[8,64,128]{2,1,0:T(8,128)(2,1)S(1)}, u32[]{:S(2)}, u32[]{:S(2)}) async-start(bf16[8,64,128]{2,1,0:T(8,128)(2,1)} %stage.1), calls=%async_computation.2 | async-start | bytes 262144 | tf_op jit(solution)/shard_map/all_to_all | solution.py:530
  110.2 2.1 %collective-permute-start.7 = (bf16[128,256]{1,0:T(8,128)(2,1)S(1)}, bf16[128,256]{1,0:T(8,128)(2,1)S(1)}, u32[]{:S(2)}, u32[]{:S(2)}) collective-permute-start(bf16[128,256]{1,0:T(8,128)(2,1)S(1)} %down_half.1.refs_0_), channel_id=1, source_target_pairs={{0,1},{1,0},{2,3},{3,2},{4,5},{5,4},{6,7},{7,6},{8,9},{9,8},{10,11... | collective-permute-start | bytes 196616 | tf_op jit(solution)/shard_map/ppermute | solution.py:370
  112.3 1.4 collective-permute-start.8
  114.5 4.6 %collective-permute-start.10 = (f32[4,2048]{1,0:T(4,128)S(1)}, f32[4,2048]{1,0:T(4,128)S(1)}, u32[]{:S(2)}, u32[]{:S(2)}) collective-permute-start(f32[4,2048]{1,0:T(4,128)S(1)} %get-tuple-element.37), channel_id=1, source_target_pairs={{0,128},{128,0},{1,129},{129,1},{2,130},{130,2},{3,131},{131,3},{4... | collective-permute-start | bytes 98312 | tf_op jit(solution)/shard_map/ppermute | solution.py:366
  119.1 4.9 %collective-permute-done.10 = f32[4,2048]{1,0:T(4,128)S(1)} collective-permute-done((f32[4,2048]{1,0:T(4,128)S(1)}, f32[4,2048]{1,0:T(4,128)S(1)}, u32[]{:S(2)}, u32[]{:S(2)}) %collective-permute-start.10) | collective-permute-done | bytes 32800 | tf_op jit(solution)/shard_map/ppermute | solution.py:366
  126.5 6.1 %all-to-all-start.3 = ((bf16[32,64,128]{2,1,0:T(8,128)(2,1)}), bf16[32,64,128]{2,1,0:T(8,128)(2,1)S(1)}, u32[]{:S(2)}, u32[]{:S(2)}) async-start(bf16[32,64,128]{2,1,0:T(8,128)(2,1)} %last.1), calls=%async_computation.3 | async-start | bytes 1048576 | tf_op jit(solution)/shard_map/all_to_all | solution.py:535
  132.7 11.3 %grad_input.1 = bf16[128,8192]{1,0:T(8,128)(2,1)} custom-call(s32[6]{0:T(128)} %stack.23.place, s32[32,256]{1,0:T(8,128)} %copy-done.13, bf16[128,256]{1,0:T(8,128)(2,1)} %copy-done.14, bf16[8192,256]{1,0:T(8,128)(2,1)} %refs_0_.3, bf16[6144,128]{1,0:T(8,128)(2,1)} %copy-done.8, bf16[2048,128]{1,0:T(8,128)(2,1)} %copy-done.12, ...), custom_call_target="tpu_custom_call" | custom-call | flops 1024 | bytes 1024 | tf_op jit(solution)/shard_map/grad_input/pallas_call | solution.py:374
  144.2 2.0 %unpack.1 = f32[64,64,64]{2,1,0:T(8,128)} custom-call(bf16[32,64,128]{2,1,0:T(8,128)(2,1)S(1)} %all-to-all-done.3.pairs_ref), custom_call_target="tpu_custom_call" | custom-call | flops 1024 | bytes 1024 | tf_op jit(solution)/shard_map/unpack/pallas_call | solution.py:374
  (82 shorter events, 13.8 us)
Async XLA Ops:
  7.3 8.2 %copy-start.4 = (bf16[512,2048]{1,0:T(8,128)(2,1)S(1)}, bf16[512,2048]{1,0:T(8,128)(2,1)}, u32[]{:S(2)}) copy-start(bf16[512,2048]{1,0:T(8,128)(2,1)} %grad_hbm.1) | copy-start | bytes 6291460
  8.6 14.9 %collective-permute-start = (bf16[8192,128]{1,0:T(8,128)(2,1)S(1)}, bf16[8192,128]{1,0:T(8,128)(2,1)S(1)}, u32[]{:S(2)}, u32[]{:S(2)}) collective-permute-start(bf16[8192,128]{1,0:T(8,128)(2,1)S(1)} %turn_input.1.xt_ref), channel_id=1, source_target_pairs={{0,4},{4,0},{1,5},{5,1},{2,6},{6,2},{3,7},{7,3},{8,12},{12,8},{9,1... | collective-permute-start | bytes 6291464 | tf_op jit(solution)/shard_map/ppermute | solution.py:366
  11.9 5.5 %collective-permute-start.1 = (bf16[144,256]{1,0:T(8,128)(2,1)S(1)}, bf16[144,256]{1,0:T(8,128)(2,1)S(1)}, u32[]{:S(2)}, u32[]{:S(2)}) collective-permute-start(bf16[144,256]{1,0:T(8,128)(2,1)S(1)} %copy-done.21), channel_id=1, source_target_pairs={{0,1},{1,0},{2,3},{3,2},{4,5},{5,4},{6,7},{7,6},{8,9},{9,8},{10,11... | collective-permute-start | bytes 221192 | tf_op jit(solution)/shard_map/ppermute | solution.py:370
  11.9 8.5 %collective-permute-start.2 = (bf16[144,256]{1,0:T(8,128)(2,1)S(1)}, bf16[144,256]{1,0:T(8,128)(2,1)S(1)}, u32[]{:S(2)}, u32[]{:S(2)}) collective-permute-start(bf16[144,256]{1,0:T(8,128)(2,1)S(1)} %copy-done.20), channel_id=1, source_target_pairs={{0,2},{1,3},{2,0},{3,1},{4,6},{5,7},{6,4},{7,5},{8,10},{9,11},{10,... | collective-permute-start | bytes 221192 | tf_op jit(solution)/shard_map/ppermute | solution.py:370
  14.8 7.0 %collective-permute-start.3 = (bf16[144,256]{1,0:T(8,128)(2,1)S(1)}, bf16[144,256]{1,0:T(8,128)(2,1)S(1)}, u32[]{:S(2)}, u32[]{:S(2)}) collective-permute-start(bf16[144,256]{1,0:T(8,128)(2,1)S(1)} %copy-done.19), channel_id=1, source_target_pairs={{0,3},{1,2},{2,1},{3,0},{4,7},{5,6},{6,5},{7,4},{8,11},{9,10},{10,... | collective-permute-start | bytes 221192 | tf_op jit(solution)/shard_map/ppermute | solution.py:370
  15.5 25.9 %collective-permute-start.12 = (bf16[128,2048]{1,0:T(8,128)(2,1)}, bf16[128,2048]{1,0:T(8,128)(2,1)S(1)}, u32[]{:S(2)}, u32[]{:S(2)}) collective-permute-start(bf16[128,2048]{1,0:T(8,128)(2,1)} %get-tuple-element.41), channel_id=1, source_target_pairs={{0,1},{1,0},{2,3},{3,2},{4,5},{5,4},{6,7},{7,6},{8,9},{9,8},{10,11... | collective-permute-start | bytes 1572872 | tf_op jit(solution)/shard_map/ppermute | solution.py:370
  17.4 26.7 %collective-permute-start.13 = (bf16[128,2048]{1,0:T(8,128)(2,1)}, bf16[128,2048]{1,0:T(8,128)(2,1)}, u32[]{:S(2)}, u32[]{:S(2)}) collective-permute-start(bf16[128,2048]{1,0:T(8,128)(2,1)} %get-tuple-element.42), channel_id=1, source_target_pairs={{0,2},{1,3},{2,0},{3,1},{4,6},{5,7},{6,4},{7,5},{8,10},{9,11},{10,... | collective-permute-start | bytes 1572872 | tf_op jit(solution)/shard_map/ppermute | solution.py:370
  20.4 3.1 %collective-permute-start.5 = (bf16[128,2048]{1,0:T(8,128)(2,1)S(1)}, bf16[128,2048]{1,0:T(8,128)(2,1)S(1)}, u32[]{:S(2)}, u32[]{:S(2)}) collective-permute-start(bf16[128,2048]{1,0:T(8,128)(2,1)S(1)} %get-tuple-element.31.refs_4_), channel_id=1, source_target_pairs={{0,4},{4,0},{1,5},{5,1},{2,6},{6,2},{3,7},{7,3},{8,12},{12,8},{9,1... | collective-permute-start | bytes 1572872 | tf_op jit(solution)/shard_map/ppermute | solution.py:366
  21.9 8.9 %copy-start.14 = (bf16[128,256]{1,0:T(8,128)(2,1)}, bf16[128,256]{1,0:T(8,128)(2,1)S(1)}, u32[]{:S(2)}) copy-start(bf16[128,256]{1,0:T(8,128)(2,1)S(1)} %get-tuple-element.32.low_ref) | copy-start | bytes 196612
  21.9 54.8 %copy-start.13 = (s32[32,256]{1,0:T(8,128)}, s32[32,256]{1,0:T(8,128)S(1)}, u32[]{:S(2)}) copy-start(s32[32,256]{1,0:T(8,128)S(1)} %get-tuple-element.38.table) | copy-start | bytes 98308
  21.9 1.6 %collective-permute-start.4 = (bf16[128,256]{1,0:T(8,128)(2,1)S(1)}, bf16[128,256]{1,0:T(8,128)(2,1)S(1)}, u32[]{:S(2)}, u32[]{:S(2)}) collective-permute-start(bf16[128,256]{1,0:T(8,128)(2,1)S(1)} %get-tuple-element.32.low_ref), channel_id=1, source_target_pairs={{0,4},{4,0},{1,5},{5,1},{2,6},{6,2},{3,7},{7,3},{8,12},{12,8},{9,1... | collective-permute-start | bytes 196616 | tf_op jit(solution)/shard_map/ppermute | solution.py:366
  33.7 47.2 %all-to-all-start = ((bf16[16,320,256]{2,1,0:T(8,128)(2,1)}), bf16[16,320,256]{2,1,0:T(8,128)(2,1)}, u32[]{:S(2)}, u32[]{:S(2)}) async-start(bf16[16,320,256]{2,1,0:T(8,128)(2,1)} %copy-done.3), calls=%async_computation | async-start | bytes 5242880 | tf_op jit(solution)/shard_map/all_to_all | solution.py:448
  40.6 7.0 %collective-permute-start.14 = (bf16[128,2048]{1,0:T(8,128)(2,1)S(1)}, bf16[128,2048]{1,0:T(8,128)(2,1)S(1)}, u32[]{:S(2)}, u32[]{:S(2)}) collective-permute-start(bf16[128,2048]{1,0:T(8,128)(2,1)S(1)} %copy-done.11), channel_id=1, source_target_pairs={{0,4},{4,0},{1,5},{5,1},{2,6},{6,2},{3,7},{7,3},{8,12},{12,8},{9,1... | collective-permute-start | bytes 1572872 | tf_op jit(solution)/shard_map/ppermute | solution.py:366
  41.4 6.2 %collective-permute-start.15 = (bf16[128,2048]{1,0:T(8,128)(2,1)S(1)}, bf16[128,2048]{1,0:T(8,128)(2,1)S(1)}, u32[]{:S(2)}, u32[]{:S(2)}) collective-permute-start(bf16[128,2048]{1,0:T(8,128)(2,1)S(1)} %collective-permute-done.12.refs_1_), channel_id=1, source_target_pairs={{0,4},{4,0},{1,5},{5,1},{2,6},{6,2},{3,7},{7,3},{8,12},{12,8},{9,1... | collective-permute-start | bytes 1572872 | tf_op jit(solution)/shard_map/ppermute | solution.py:366
  44.2 3.5 %collective-permute-start.16 = (bf16[128,2048]{1,0:T(8,128)(2,1)}, bf16[128,2048]{1,0:T(8,128)(2,1)S(1)}, u32[]{:S(2)}, u32[]{:S(2)}) collective-permute-start(bf16[128,2048]{1,0:T(8,128)(2,1)} %collective-permute-done.13.refs_2_), channel_id=1, source_target_pairs={{0,4},{4,0},{1,5},{5,1},{2,6},{6,2},{3,7},{7,3},{8,12},{12,8},{9,1... | collective-permute-start | bytes 1572872 | tf_op jit(solution)/shard_map/ppermute | solution.py:366
  45.4 15.7 %collective-permute-start.11 = (bf16[128,2048]{1,0:T(8,128)(2,1)}, bf16[128,2048]{1,0:T(8,128)(2,1)S(1)}, u32[]{:S(2)}, u32[]{:S(2)}) collective-permute-start(bf16[128,2048]{1,0:T(8,128)(2,1)} %get-tuple-element.39), channel_id=1, source_target_pairs={{0,3},{1,2},{2,1},{3,0},{4,7},{5,6},{6,5},{7,4},{8,11},{9,10},{10,... | collective-permute-start | bytes 1572872 | tf_op jit(solution)/shard_map/ppermute | solution.py:370
  61.1 15.6 %copy-start.2 = (bf16[8192,128]{1,0:T(8,128)(2,1)S(1)}, bf16[8192,128]{1,0:T(8,128)(2,1)}, u32[]{:S(2)}) copy-start(bf16[8192,128]{1,0:T(8,128)(2,1)} %copy-done) | copy-start | bytes 6291460
  61.1 15.6 %collective-permute-start.17 = (bf16[128,2048]{1,0:T(8,128)(2,1)S(1)}, bf16[128,2048]{1,0:T(8,128)(2,1)S(1)}, u32[]{:S(2)}, u32[]{:S(2)}) collective-permute-start(bf16[128,2048]{1,0:T(8,128)(2,1)S(1)} %gate.1.refs_0_), channel_id=1, source_target_pairs={{0,4},{4,0},{1,5},{5,1},{2,6},{6,2},{3,7},{7,3},{8,12},{12,8},{9,1... | collective-permute-start | bytes 1572872 | tf_op jit(solution)/shard_map/ppermute | solution.py:366
  63.0 17.0 %copy-start.6 = (bf16[32,64,128]{2,1,0:T(8,128)(2,1)}, bf16[32,64,128]{2,1,0:T(8,128)(2,1)S(1)}, u32[]{:S(2)}) copy-start(bf16[32,64,128]{2,1,0:T(8,128)(2,1)S(1)} %pack.1.refs_3_) | copy-start | bytes 1572868
  63.0 28.7 %collective-permute-start.18 = (bf16[32,64,128]{2,1,0:T(8,128)(2,1)S(1)}, bf16[32,64,128]{2,1,0:T(8,128)(2,1)S(1)}, u32[]{:S(2)}, u32[]{:S(2)}) collective-permute-start(bf16[32,64,128]{2,1,0:T(8,128)(2,1)S(1)} %pack.1.refs_3_), channel_id=1, source_target_pairs={{0,1},{1,2},{2,3},{3,128},{128,129},{129,130},{130,131},{131,0},{4... | collective-permute-start | bytes 1572872 | tf_op jit(solution)/shard_map/ppermute | solution.py:502
  72.1 19.7 %collective-permute-start.19 = (bf16[32,64,128]{2,1,0:T(8,128)(2,1)S(1)}, bf16[32,64,128]{2,1,0:T(8,128)(2,1)}, u32[]{:S(2)}, u32[]{:S(2)}) collective-permute-start(bf16[32,64,128]{2,1,0:T(8,128)(2,1)S(1)} %pack.1.refs_3_), channel_id=1, source_target_pairs={{0,131},{1,0},{2,1},{3,2},{128,3},{129,128},{130,129},{131,130},{4... | collective-permute-start | bytes 1572872 | tf_op jit(solution)/shard_map/ppermute | solution.py:503
  72.1 26.7 %collective-permute-start.20 = (bf16[32,64,128]{2,1,0:T(8,128)(2,1)S(1)}, bf16[32,64,128]{2,1,0:T(8,128)(2,1)}, u32[]{:S(2)}, u32[]{:S(2)}) collective-permute-start(bf16[32,64,128]{2,1,0:T(8,128)(2,1)S(1)} %pack.1.refs_3_), channel_id=1, source_target_pairs={{0,2},{4,134},{1,3},{5,135},{2,128},{6,4},{3,129},{7,5},{128,130},... | collective-permute-start | bytes 1572872 | tf_op jit(solution)/shard_map/ppermute | solution.py:504
  80.8 23.6 %all-to-all-start.1 = ((bf16[16,4,64,128]{3,2,1,0:T(8,128)(2,1)}), bf16[16,4,64,128]{3,2,1,0:T(8,128)(2,1)S(1)}, u32[]{:S(2)}, u32[]{:S(2)}) async-start(bf16[16,4,64,128]{3,2,1,0:T(8,128)(2,1)} %join.1), calls=%async_computation.1 | async-start | bytes 2097152 | tf_op jit(solution)/shard_map/all_to_all | solution.py:495
  89.7 9.1 %collective-permute-start.6 = (bf16[128,256]{1,0:T(8,128)(2,1)S(1)}, bf16[128,256]{1,0:T(8,128)(2,1)S(1)}, u32[]{:S(2)}, u32[]{:S(2)}) collective-permute-start(bf16[128,256]{1,0:T(8,128)(2,1)S(1)} %get-tuple-element.35), channel_id=1, source_target_pairs={{0,128},{128,0},{1,129},{129,1},{2,130},{130,2},{3,131},{131,3},{4... | collective-permute-start | bytes 196616 | tf_op jit(solution)/shard_map/ppermute | solution.py:366
  98.8 27.8 %copy-start.7 = (bf16[32,64,128]{2,1,0:T(8,128)(2,1)}, bf16[32,64,128]{2,1,0:T(8,128)(2,1)S(1)}, u32[]{:S(2)}) copy-start(bf16[32,64,128]{2,1,0:T(8,128)(2,1)S(1)} %get-tuple-element.45.refs_1_.refs_4_) | copy-start | bytes 1572868
  105.8 19.0 %all-to-all-start.2 = ((bf16[8,64,128]{2,1,0:T(8,128)(2,1)}), bf16[8,64,128]{2,1,0:T(8,128)(2,1)S(1)}, u32[]{:S(2)}, u32[]{:S(2)}) async-start(bf16[8,64,128]{2,1,0:T(8,128)(2,1)} %stage.1), calls=%async_computation.2 | async-start | bytes 262144 | tf_op jit(solution)/shard_map/all_to_all | solution.py:530
  110.2 13.9 %collective-permute-start.7 = (bf16[128,256]{1,0:T(8,128)(2,1)S(1)}, bf16[128,256]{1,0:T(8,128)(2,1)S(1)}, u32[]{:S(2)}, u32[]{:S(2)}) collective-permute-start(bf16[128,256]{1,0:T(8,128)(2,1)S(1)} %down_half.1.refs_0_), channel_id=1, source_target_pairs={{0,1},{1,0},{2,3},{3,2},{4,5},{5,4},{6,7},{7,6},{8,9},{9,8},{10,11... | collective-permute-start | bytes 196616 | tf_op jit(solution)/shard_map/ppermute | solution.py:370
  112.3 11.7 %collective-permute-start.8 = (bf16[128,256]{1,0:T(8,128)(2,1)S(1)}, bf16[128,256]{1,0:T(8,128)(2,1)S(1)}, u32[]{:S(2)}, u32[]{:S(2)}) collective-permute-start(bf16[128,256]{1,0:T(8,128)(2,1)S(1)} %down_half.1.refs_0_), channel_id=1, source_target_pairs={{0,2},{1,3},{2,0},{3,1},{4,6},{5,7},{6,4},{7,5},{8,10},{9,11},{10,... | collective-permute-start | bytes 196616 | tf_op jit(solution)/shard_map/ppermute | solution.py:370
  113.7 10.4 %collective-permute-start.9 = (bf16[128,256]{1,0:T(8,128)(2,1)S(1)}, bf16[128,256]{1,0:T(8,128)(2,1)S(1)}, u32[]{:S(2)}, u32[]{:S(2)}) collective-permute-start(bf16[128,256]{1,0:T(8,128)(2,1)S(1)} %down_half.1.refs_0_), channel_id=1, source_target_pairs={{0,3},{1,2},{2,1},{3,0},{4,7},{5,6},{6,5},{7,4},{8,11},{9,10},{10,... | collective-permute-start | bytes 196616 | tf_op jit(solution)/shard_map/ppermute | solution.py:370
  114.5 9.5 %collective-permute-start.10 = (f32[4,2048]{1,0:T(4,128)S(1)}, f32[4,2048]{1,0:T(4,128)S(1)}, u32[]{:S(2)}, u32[]{:S(2)}) collective-permute-start(f32[4,2048]{1,0:T(4,128)S(1)} %get-tuple-element.37), channel_id=1, source_target_pairs={{0,128},{128,0},{1,129},{129,1},{2,130},{130,2},{3,131},{131,3},{4... | collective-permute-start | bytes 98312 | tf_op jit(solution)/shard_map/ppermute | solution.py:366
  124.0 19.9 %copy-start.16 = (f32[4,2048]{1,0:T(4,128)}, f32[4,2048]{1,0:T(4,128)S(1)}, u32[]{:S(2)}) copy-start(f32[4,2048]{1,0:T(4,128)S(1)} %add.17.after_too_ref) | copy-start | bytes 98308
  126.5 17.7 %all-to-all-start.3 = ((bf16[32,64,128]{2,1,0:T(8,128)(2,1)}), bf16[32,64,128]{2,1,0:T(8,128)(2,1)S(1)}, u32[]{:S(2)}, u32[]{:S(2)}) async-start(bf16[32,64,128]{2,1,0:T(8,128)(2,1)} %last.1), calls=%async_computation.3 | async-start | bytes 1048576 | tf_op jit(solution)/shard_map/all_to_all | solution.py:535
  (15 other events, 59.3 us)

commit v4 on v3

--- a/solution.py
+++ b/solution.py
@@ -140,7 +140,7 @@
     lax.fori_loop(0, PAIRS, one, 0, unroll=4)
 
 
-def down_sum_kernel(place, down_ref, keep_ref, give_ref, up_keep_ref, up_give_ref):
+def down_sum_kernel(place, down_ref, keep_ref, give_ref, up_ref):
     def total(at):
         part = down_ref[0, at, :].astype(F32)
         for i in range(1, XY):
@@ -149,18 +149,24 @@
 
     zh = place[5]
     keep_ref[...] = total(aligned(zh, 128))
-    give_ref[...] = total(aligned(1 - zh, 128)).astype(BF16)
+    give_ref[:128] = total(aligned(1 - zh, 128)).astype(BF16)
     up = total(slice(256, None))
     rank = up.shape[1]
+    give = []
     for j in range(up.shape[0] // 8):
         low, high = up[j * 8 : j * 8 + 4], up[j * 8 + 4 : j * 8 + 8]
+        up_ref[:, j * rank : (j + 1) * rank] = jnp.where(zh == 0, low, high)
+        give.append(jnp.where(zh == 0, high, low))
+    give_ref[128:] = jnp.concatenate(give, axis=0).astype(BF16)
+
+
+def down_half_kernel(keep_ref, far_ref, up_ref, out_ref, up_out_ref):
+    out_ref[...] = (keep_ref[...] + far_ref[:128].astype(F32)).astype(BF16)
+    up = far_ref[128:].astype(F32)
+    rank = up.shape[1]
+    for j in range(up.shape[0] // 4):
         at = slice(j * rank, (j + 1) * rank)
-        up_keep_ref[:, at] = jnp.where(zh == 0, low, high)
-        up_give_ref[:, at] = jnp.where(zh == 0, high, low)
-
-
-def down_half_kernel(keep_ref, far_ref, out_ref):
-    out_ref[...] = (keep_ref[...] + far_ref[...].astype(F32)).astype(BF16)
+        up_out_ref[:, at] = up_ref[:, at] + up[j * 4 : j * 4 + 4]
 
 
 def down_last_kernel(*refs):
@@ -183,7 +189,7 @@
             out_ref[zh * T + t] = part
 
 
-def last_kernel(parts_ref, after_ref, after_too_ref, delta_ref):
+def last_kernel(parts_ref, after_ref, delta_ref):
     total = parts_ref[0].astype(F32)
     for i in range(1, ZH * T):
         total += parts_ref[i].astype(F32)
@@ -202,30 +208,30 @@
     lax.fori_loop(0, PAIRS, one, 0, unroll=4)
 
 
-def down_kernel(
-    place, xt_ref, xt_far_ref, low_ref, low_far_ref, up_ref, up_far_ref, out_hbm, out_ref, sems
-):
+def down_kernel(place, xt_ref, xt_far_ref, low_ref, low_far_ref, up_ref, up_far_ref, out_ref):
     low, low_far = low_ref[...], low_far_ref[...]
     core = place[0]
     rank = low.shape[1]
-    copies = []
-    for i in range(XY):
+
+    def block(i, carry):
         for zh in range(ZH):
             at = aligned((zh * XY + i) * C + core, 128)
             total = jnp.dot(xt_ref[at, :], low, preferred_element_type=F32)
             total += jnp.dot(xt_far_ref[at, :], low_far, preferred_element_type=F32)
             out_ref[i, zh * 128 : (zh + 1) * 128] = total.astype(BF16)
-        if i % 2 == 0:
-            at = slice(i * 8, i * 8 + 16)
-            up = up_ref[at, :] + up_far_ref[at, :].astype(F32)
-        mine = up[i % 2 * 8 : i % 2 * 8 + 8]
-        for j in range(0, mine.shape[1] // rank, 2):
-            two = [mine[:, (j + n) * rank : (j + n + 1) * rank] for n in range(2)]
-            out_ref[i, 256 + j * 8 : 256 + j * 8 + 16] = jnp.concatenate(two, axis=0).astype(BF16)
-        copies.append(pltpu.make_async_copy(out_ref.at[i], out_hbm.at[i], sems.at[i]))
-        copies[-1].start()
-    for copy in copies:
-        copy.wait()
+        return carry
+
+    lax.fori_loop(0, XY, block, 0, unroll=4)
+    for i in range(0, XY, 2):
+        at = slice(i * 8, i * 8 + 16)
+        for j in range(0, up_ref.shape[1] // rank, 2):
+            two = []
+            for n in (j, j + 1):
+                lanes = slice(n * rank, (n + 1) * rank)
+                two.append(up_ref[at, lanes] + up_far_ref[at, lanes].astype(F32))
+            for n in range(2):
+                both = [part[n * 8 : n * 8 + 8] for part in two]
+                out_ref[i + n, 256 + j * 8 : 256 + j * 8 + 16] = jnp.concatenate(both, 0).astype(BF16)
 
 
 def delta_kernel(pieces, place, table, xt_ref, xt_far_ref, *refs):
@@ -415,7 +421,7 @@
 
     xt = call(
         turn_kernel, "turn_input", shape((feat, TOK), BF16),
-        [anywhere()] * 2, x_own, given[0],
+        [anywhere()] * 2, x_own, given[T],
         scratch=[pltpu.VMEM(x_own.shape, BF16), pltpu.SemaphoreType.DMA((8,))],
     )
     xt_far = swap(xt)
@@ -442,19 +448,20 @@
     down_part = call(
         down_kernel, "down_part", shape(size, BF16), [scalars()] + [whole()] * 6,
         place, xt, xt_far, low, low_far, up_keep, up_got,
-        out_specs=anywhere(),
-        scratch=[pltpu.VMEM(size, BF16), pltpu.SemaphoreType.DMA((XY,))],
     )
     down_all = lax.all_to_all(down_part, ("y", "x"), 0, 0, tiled=True)
-    down_keep, down_give, up_sum, up_give = call(
+    down_keep, down_give, up_sum = call(
         down_sum_kernel, "down_sum",
-        (shape((128, rank), F32), shape((128, rank), BF16)) + (shape((4, width), F32),) * 2,
+        (
+            shape((128, rank), F32),
+            shape((128 + 4 * width // rank, rank), BF16),
+            shape((4, width), F32),
+        ),
         [scalars(), whole()], place, down_all,
     )
-    up_grad = up_sum + swap(up_give, "zh")
-    down_half = call(
-        down_half_kernel, "down_half", shape((128, rank), BF16), [whole()] * 2,
-        down_keep, swap(down_give, "zh"),
+    down_half, up_grad = call(
+        down_half_kernel, "down_half", (shape((128, rank), BF16), shape((4, width), F32)),
+        [whole()] * 3, down_keep, swap(down_give, "zh"), up_sum,
     )
     down_grad = call(
         down_last_kernel, "down_last", shape((128, rank), F32), [whole()] * T,
@@ -524,13 +531,13 @@
 
     stage = call(
         stage_kernel, "stage", shape((ZH * T, BLK, 128), BF16),
-        [scalars(), whole()] + [anywhere()] * 2, place, delta_all, down_half, got[0],
+        [scalars()] + [whole()] * 2 + [anywhere()], place, delta_all, down_half, got[0],
         scratch=[pltpu.VMEM((T, BLK, 2 * BLK), F32)],
     )
+
     stage_all = lax.all_to_all(stage, ("zh", "t"), 0, 0, tiled=True)
     delta_one = call(
-        last_kernel, "last", shape((PAIRS, BLK, 2 * BLK), BF16), [whole()] + [anywhere()] * 2,
-        stage_all, down_grad, up_grad,
+        last_kernel, "last", shape((PAIRS, BLK, 2 * BLK), BF16), [whole()] * 2, stage_all, down_grad,
     )
     delta_full = lax.all_to_all(delta_one, ("y", "x", "c"), 0, 0, tiled=True)
     grad_delta = call(

time: 147 us -> 145 us (0.986)
  waiting for transfers between devices: 27.8 us -> 34.7 us
  Pallas kernels: 42.5 us -> 38.1 us
  starting transfers between devices: 66.3 us -> 61.9 us
    ppermute x9, waiting for transfers between devices: 8.94 us -> 19.7 us  [cross(): return lax.ppermute(array, 't', [(i, i ^ k) for i in range(T)])]
    ppermute x9 -> x8, starting transfers between devices: 15.4 us -> 9.72 us  [swap(): return lax.ppermute(array, axis, [(0, 1), (1, 0)])]
    ppermute x9 -> x8, waiting for transfers between devices: 5.87 us -> 0.95 us  [swap(): return lax.ppermute(array, axis, [(0, 1), (1, 0)])]
    pallas_call x18, Pallas kernels: 42.5 us -> 38.1 us  [call(): pl.pallas_call(kernel, out_shape=outs, in_specs=in_specs, out_specs=out_s...]
    all_to_all x1, starting transfers between devices: 6.15 us -> 9.22 us  [per_device(): delta_full = lax.all_to_all(delta_one, ('y', 'x', 'c'), 0, 0, tiled=True)]
    ppermute x1, waiting for transfers between devices: 7 us -> 9.99 us  [per_device(): lax.ppermute(packed, ('zh', 'c', 't'), ring((2, -2)))]
    all_to_all x1, waiting for transfers between devices: 5.65 us -> 3.75 us  [per_device(): delta_all = lax.all_to_all(delta_part, ('y', 'x'), 0, 0, tiled=True)]
  transfers between devices with their start and end apart: 25 -> 24, of which waited for: 7 -> 10; matrix products, arithmetic and copies ran while one was open for 0% -> 0% of each run, Pallas kernels for 22% -> 20%
where the time goes in v4:
time: 145 us
  starting transfers between devices  61.9 us (43%)
  Pallas kernels  38.1 us (26%)
  waiting for transfers between devices  34.7 us (24%)
  local copies, waits for them, and re-layouts  8.22 us (6%)
  between operations  1.6 us (1%)
    pallas_call x18, Pallas kernels, call(): pl.pallas_call(kernel, out_shape=outs, in_specs=in_specs, out_specs=out_s...  38.1 us
    ppermute x9, waiting for transfers between devices, cross(): return lax.ppermute(array, 't', [(i, i ^ k) for i in range(T)])  19.7 us
    ppermute x9, starting transfers between devices, cross(): return lax.ppermute(array, 't', [(i, i ^ k) for i in range(T)])  12.3 us
    ppermute x1, waiting for transfers between devices, per_device(): lax.ppermute(packed, ('zh', 'c', 't'), ring((2, -2)))  9.99 us
    ppermute x8, starting transfers between devices, swap(): return lax.ppermute(array, axis, [(0, 1), (1, 0)])  9.72 us
    all_to_all x1, starting transfers between devices, per_device(): delta_full = lax.all_to_all(delta_one, ('y', 'x', 'c'), 0, 0, tiled=True)  9.22 us
    ppermute x1, starting transfers between devices, per_device(): lax.ppermute(packed, axes, [(i, (i + 1) % (ZH * T)) for i in range(ZH * T)])  8.86 us
    unnamed x44, local copies, waits for them, and re-layouts  7.56 us
  transfers between devices with their start and end apart: 24, of which 10 were waited for; matrix products, arithmetic and copies ran while one was open for 0% of the time, Pallas kernels for 20%

profile of v4, /device:TPU:1, one launch (start us, length us, event | category | flops | bytes accessed | tf_op | source)
XLA Modules:
  0.0 144.5 jit_solution(1223044799039949893)
XLA Ops:
  2.0 4.5 %front.1 = (bf16[144,256]{1,0:T(8,128)(2,1)}, bf16[144,256]{1,0:T(8,128)(2,1)}, bf16[144,256]{1,0:T(8,128)(2,1)}, bf16[144,256]{1,0:T(8,128)(2,1)}, bf16[128,204...) custom-call(s32[6]{0:T(128)} %stack.23.place, ...), custom_call_target="tpu_custom_call" | custom-call | flops 1024 | bytes 1024 | tf_op jit(solution)/shard_map/front/pallas_call | solution.py:380
  8.8 3.3 %collective-permute-start = (bf16[8192,128]{1,0:T(8,128)(2,1)S(1)}, bf16[8192,128]{1,0:T(8,128)(2,1)S(1)}, u32[]{:S(2)}, u32[]{:S(2)}) collective-permute-start(bf16[8192,128]{1,0:T(8,128)(2,1)S(1)} %turn_input.1.xt_ref), channel_id=1, source_target_pairs={{0,4},{4,0},{1,5},{5,1},{2,6},{6,2},{3,7},{7,3},{8,12},{12,8},{9,1... | collective-permute-start | bytes 6291464 | tf_op jit(solution)/shard_map/ppermute | solution.py:372
  12.1 2.9 %collective-permute-start.2 = (bf16[144,256]{1,0:T(8,128)(2,1)S(1)}, bf16[144,256]{1,0:T(8,128)(2,1)S(1)}, u32[]{:S(2)}, u32[]{:S(2)}) collective-permute-start(bf16[144,256]{1,0:T(8,128)(2,1)S(1)} %copy-done.20), channel_id=1, source_target_pairs={{0,2},{1,3},{2,0},{3,1},{4,6},{5,7},{6,4},{7,5},{8,10},{9,11},{10,... | collective-permute-start | bytes 221192 | tf_op jit(solution)/shard_map/ppermute | solution.py:376
  15.7 1.9 %up_part.1 = (f32[128,2048]{1,0:T(8,128)S(1)}, bf16[128,2048]{1,0:T(8,128)(2,1)S(1)}) custom-call(s32[6]{0:T(128)S(1)} %copy-done.17, bf16[512,2048]{1,0:T(8,128)(2,1)S(1)} %copy-done.4, bf16[512,256]{1,0:T(8,128)(2,1)S(1)} %copy-done.16), custom_call_target="tpu_custom_call" | custom-call | flops 1024 | bytes 1024 | tf_op jit(solution)/shard_map/up_part/pallas_call | solution.py:380
  17.6 3.0 %collective-permute-start.12 = (bf16[128,2048]{1,0:T(8,128)(2,1)}, bf16[128,2048]{1,0:T(8,128)(2,1)}, u32[]{:S(2)}, u32[]{:S(2)}) collective-permute-start(bf16[128,2048]{1,0:T(8,128)(2,1)} %get-tuple-element.44), channel_id=1, source_target_pairs={{0,2},{1,3},{2,0},{3,1},{4,6},{5,7},{6,4},{7,5},{8,10},{9,11},{10,... | collective-permute-start | bytes 1572872 | tf_op jit(solution)/shard_map/ppermute | solution.py:376
  20.6 1.5 %collective-permute-start.5 = (bf16[128,2048]{1,0:T(8,128)(2,1)S(1)}, bf16[128,2048]{1,0:T(8,128)(2,1)S(1)}, u32[]{:S(2)}, u32[]{:S(2)}) collective-permute-start(bf16[128,2048]{1,0:T(8,128)(2,1)S(1)} %get-tuple-element.33.refs_4_), channel_id=1, source_target_pairs={{0,4},{4,0},{1,5},{5,1},{2,6},{6,2},{3,7},{7,3},{8,12},{12,8},{9,1... | collective-permute-start | bytes 1572872 | tf_op jit(solution)/shard_map/ppermute | solution.py:372
  23.7 2.3 %down_part.1 = bf16[16,320,256]{2,1,0:T(8,128)(2,1)S(1)} custom-call(s32[6]{0:T(128)S(1)} %copy-done.17, bf16[8192,128]{1,0:T(8,128)(2,1)S(1)} %turn_input.1.xt_ref, bf16[8192,128]{1,0:T(8,128)(2,1)S(1)} %collective-permute-done.xt_far_ref, bf16[128,256]{1,0:T(8,128)(2,1)S(1)} %get-tuple-element.34.low_ref, ...), custom_call_target="tpu_custom_call" | custom-call | flops 1024 | bytes 1024 | tf_op jit(solution)/shard_map/down_part/pallas_call | solution.py:380
  26.1 1.3 copy-done
  27.4 1.5 %copy-done.3 = bf16[16,320,256]{2,1,0:T(8,128)(2,1)} copy-done((bf16[16,320,256]{2,1,0:T(8,128)(2,1)}, bf16[16,320,256]{2,1,0:T(8,128)(2,1)S(1)}, u32[]{:S(2)}) %copy-start.3) | copy-done | bytes 2621464
  28.9 6.9 %all-to-all-start = ((bf16[16,320,256]{2,1,0:T(8,128)(2,1)}), bf16[16,320,256]{2,1,0:T(8,128)(2,1)}, u32[]{:S(2)}, u32[]{:S(2)}) async-start(bf16[16,320,256]{2,1,0:T(8,128)(2,1)} %copy-done.3), calls=%async_computation | async-start | bytes 5242880 | tf_op jit(solution)/shard_map/all_to_all | solution.py:452
  36.6 4.3 %collective-permute-done.11.refs_1_ = bf16[128,2048]{1,0:T(8,128)(2,1)S(1)} collective-permute-done((bf16[128,2048]{1,0:T(8,128)(2,1)}, bf16[128,2048]{1,0:T(8,128)(2,1)S(1)}, u32[]{:S(2)}, u32[]{:S(2)}) %collective-permute-start.11) | collective-permute-done | bytes 524320 | tf_op jit(solution)/shard_map/ppermute | solution.py:376
  42.0 2.3 %collective-permute-done.12.refs_2_ = bf16[128,2048]{1,0:T(8,128)(2,1)} collective-permute-done((bf16[128,2048]{1,0:T(8,128)(2,1)}, bf16[128,2048]{1,0:T(8,128)(2,1)}, u32[]{:S(2)}, u32[]{:S(2)}) %collective-permute-start.12) | collective-permute-done | bytes 524320 | tf_op jit(solution)/shard_map/ppermute | solution.py:376
  45.6 2.2 %collective-permute-start.10 = (bf16[128,2048]{1,0:T(8,128)(2,1)}, bf16[128,2048]{1,0:T(8,128)(2,1)S(1)}, u32[]{:S(2)}, u32[]{:S(2)}) collective-permute-start(bf16[128,2048]{1,0:T(8,128)(2,1)} %get-tuple-element.42), channel_id=1, source_target_pairs={{0,3},{1,2},{2,1},{3,0},{4,7},{5,6},{6,5},{7,4},{8,11},{9,10},{10,... | collective-permute-start | bytes 1572872 | tf_op jit(solution)/shard_map/ppermute | solution.py:376
  47.8 1.6 %copy-done.1 = bf16[8192,128]{1,0:T(8,128)(2,1)S(1)} copy-done((bf16[8192,128]{1,0:T(8,128)(2,1)S(1)}, bf16[8192,128]{1,0:T(8,128)(2,1)}, u32[]{:S(2)}) %copy-start.1) | copy-done | bytes 2097176
  49.4 5.2 %delta_most.1 = (bf16[16,4,64,128]{3,2,1,0:T(8,128)(2,1)}, bf16[6144,128]{1,0:T(8,128)(2,1)S(1)}) custom-call(s32[6]{0:T(128)S(1)} %copy-done.17, s32[32,256]{1,0:T(8,128)S(1)} %get-tuple-element.41.table, bf16[8192,128]{1,0:T(8,128)(2,1)S(1)} %turn_input.1.xt_ref, bf16[8192,128]{1,0:T(8,128)(2,1)S(1)} %copy-done.1, bf16[128,2048]{1,0:T(8,128)(2,1)S(1)} %copy-done.7, ...), custom_call_target="tpu_custom_call" | custom-call | flops 1024 | bytes 1024 | tf_op jit(solution)/shard_map/delta_most/pallas_call | solution.py:380
  54.6 6.6 %collective-permute-done.10.refs_0_ = bf16[128,2048]{1,0:T(8,128)(2,1)S(1)} collective-permute-done((bf16[128,2048]{1,0:T(8,128)(2,1)}, bf16[128,2048]{1,0:T(8,128)(2,1)S(1)}, u32[]{:S(2)}, u32[]{:S(2)}) %collective-permute-start.10) | collective-permute-done | bytes 524320 | tf_op jit(solution)/shard_map/ppermute | solution.py:376
  63.2 8.9 %collective-permute-start.17 = (bf16[32,64,128]{2,1,0:T(8,128)(2,1)S(1)}, bf16[32,64,128]{2,1,0:T(8,128)(2,1)S(1)}, u32[]{:S(2)}, u32[]{:S(2)}) collective-permute-start(bf16[32,64,128]{2,1,0:T(8,128)(2,1)S(1)} %pack.1.refs_3_), channel_id=1, source_target_pairs={{0,1},{1,2},{2,3},{3,128},{128,129},{129,130},{130,131},{131,0},{4... | collective-permute-start | bytes 1572872 | tf_op jit(solution)/shard_map/ppermute | solution.py:509
  72.1 4.5 %collective-permute-start.19 = (bf16[32,64,128]{2,1,0:T(8,128)(2,1)S(1)}, bf16[32,64,128]{2,1,0:T(8,128)(2,1)}, u32[]{:S(2)}, u32[]{:S(2)}) collective-permute-start(bf16[32,64,128]{2,1,0:T(8,128)(2,1)S(1)} %pack.1.refs_3_), channel_id=1, source_target_pairs={{0,2},{4,134},{1,3},{5,135},{2,128},{6,4},{3,129},{7,5},{128,130},... | collective-permute-start | bytes 1572872 | tf_op jit(solution)/shard_map/ppermute | solution.py:511
  76.6 3.3 %delta_last.1 = (bf16[16,4,64,128]{3,2,1,0:T(8,128)(2,1)}, bf16[2048,128]{1,0:T(8,128)(2,1)S(1)}) custom-call(s32[6]{0:T(128)S(1)} %copy-done.17, s32[32,256]{1,0:T(8,128)S(1)} %get-tuple-element.41.table, bf16[8192,128]{1,0:T(8,128)(2,1)S(1)} %turn_input.1.xt_ref, bf16[8192,128]{1,0:T(8,128)(2,1)S(1)} %copy-done.2, ...), custom_call_target="tpu_custom_call", output_to_operand_aliasing={{0}: (6, {})} | custom-call | flops 1024 | bytes 1024 | tf_op jit(solution)/shard_map/delta_last/pallas_call | solution.py:380
  80.8 6.8 %all-to-all-start.1 = ((bf16[16,4,64,128]{3,2,1,0:T(8,128)(2,1)}), bf16[16,4,64,128]{3,2,1,0:T(8,128)(2,1)S(1)}, u32[]{:S(2)}, u32[]{:S(2)}) async-start(bf16[16,4,64,128]{3,2,1,0:T(8,128)(2,1)} %join.1), calls=%async_computation.1 | async-start | bytes 2097152 | tf_op jit(solution)/shard_map/all_to_all | solution.py:502
  87.6 2.1 %down_sum.1 = (f32[128,256]{1,0:T(8,128)S(1)}, bf16[160,256]{1,0:T(8,128)(2,1)S(1)}, f32[4,2048]{1,0:T(4,128)S(1)}) custom-call(s32[6]{0:T(128)S(1)} %copy-done.17, bf16[16,320,256]{2,1,0:T(8,128)(2,1)} %all-to-all-done.down_ref.refs_1_), custom_call_target="tpu_custom_call" | custom-call | flops 1024 | bytes 1024 | tf_op jit(solution)/shard_map/down_sum/pallas_call | solution.py:380
  90.0 10.0 %collective-permute-done.19.refs_2_ = bf16[32,64,128]{2,1,0:T(8,128)(2,1)} collective-permute-done((bf16[32,64,128]{2,1,0:T(8,128)(2,1)S(1)}, bf16[32,64,128]{2,1,0:T(8,128)(2,1)}, u32[]{:S(2)}, u32[]{:S(2)}) %collective-permute-start.19) | collective-permute-done | bytes 524320 | tf_op jit(solution)/shard_map/ppermute | solution.py:511
  100.7 3.7 %all-to-all-done.1.delta_ref = bf16[16,4,64,128]{3,2,1,0:T(8,128)(2,1)S(1)} async-done(((bf16[16,4,64,128]{3,2,1,0:T(8,128)(2,1)}), bf16[16,4,64,128]{3,2,1,0:T(8,128)(2,1)S(1)}, u32[]{:S(2)}, u32[]{:S(2)}) %all-to-all-start.1) | async-done | bytes 1048608 | tf_op jit(solution)/shard_map/all_to_all | solution.py:502
  104.4 1.3 stage.1
  105.8 3.5 %all-to-all-start.2 = ((bf16[8,64,128]{2,1,0:T(8,128)(2,1)}), bf16[8,64,128]{2,1,0:T(8,128)(2,1)S(1)}, u32[]{:S(2)}, u32[]{:S(2)}) async-start(bf16[8,64,128]{2,1,0:T(8,128)(2,1)} %stage.1), calls=%async_computation.2 | async-start | bytes 262144 | tf_op jit(solution)/shard_map/all_to_all | solution.py:538
  109.2 1.5 %collective-permute-start.7 = (bf16[128,256]{1,0:T(8,128)(2,1)S(1)}, bf16[128,256]{1,0:T(8,128)(2,1)S(1)}, u32[]{:S(2)}, u32[]{:S(2)}) collective-permute-start(bf16[128,256]{1,0:T(8,128)(2,1)S(1)} %get-tuple-element.39.refs_0_), channel_id=1, source_target_pairs={{0,1},{1,0},{2,3},{3,2},{4,5},{5,4},{6,7},{7,6},{8,9},{9,8},{10,11... | collective-permute-start | bytes 196616 | tf_op jit(solution)/shard_map/ppermute | solution.py:376
  110.7 2.1 %collective-permute-start.8 = (bf16[128,256]{1,0:T(8,128)(2,1)S(1)}, bf16[128,256]{1,0:T(8,128)(2,1)S(1)}, u32[]{:S(2)}, u32[]{:S(2)}) collective-permute-start(bf16[128,256]{1,0:T(8,128)(2,1)S(1)} %get-tuple-element.39.refs_0_), channel_id=1, source_target_pairs={{0,2},{1,3},{2,0},{3,1},{4,6},{5,7},{6,4},{7,5},{8,10},{9,11},{10,... | collective-permute-start | bytes 196616 | tf_op jit(solution)/shard_map/ppermute | solution.py:376
  114.1 3.6 %collective-permute-done.8.refs_2_ = bf16[128,256]{1,0:T(8,128)(2,1)S(1)} collective-permute-done((bf16[128,256]{1,0:T(8,128)(2,1)S(1)}, bf16[128,256]{1,0:T(8,128)(2,1)S(1)}, u32[]{:S(2)}, u32[]{:S(2)}) %collective-permute-start.8) | collective-permute-done | bytes 65568 | tf_op jit(solution)/shard_map/ppermute | solution.py:376
  117.7 1.6 %collective-permute-done.9.refs_3_ = bf16[128,256]{1,0:T(8,128)(2,1)S(1)} collective-permute-done((bf16[128,256]{1,0:T(8,128)(2,1)S(1)}, bf16[128,256]{1,0:T(8,128)(2,1)S(1)}, u32[]{:S(2)}, u32[]{:S(2)}) %collective-permute-start.9) | collective-permute-done | bytes 65568 | tf_op jit(solution)/shard_map/ppermute | solution.py:376
  121.7 9.2 %all-to-all-start.3 = ((bf16[32,64,128]{2,1,0:T(8,128)(2,1)}), bf16[32,64,128]{2,1,0:T(8,128)(2,1)S(1)}, u32[]{:S(2)}, u32[]{:S(2)}) async-start(bf16[32,64,128]{2,1,0:T(8,128)(2,1)} %last.1), calls=%async_computation.3 | async-start | bytes 1048576 | tf_op jit(solution)/shard_map/all_to_all | solution.py:542
  131.0 11.2 %grad_input.1 = bf16[128,8192]{1,0:T(8,128)(2,1)} custom-call(s32[6]{0:T(128)} %stack.23.place, s32[32,256]{1,0:T(8,128)} %copy-done.14, bf16[128,256]{1,0:T(8,128)(2,1)} %copy-done.15, bf16[8192,256]{1,0:T(8,128)(2,1)} %refs_0_.3, bf16[6144,128]{1,0:T(8,128)(2,1)} %copy-done.10, bf16[2048,128]{1,0:T(8,128)(2,1)} %copy-done.13, ...), custom_call_target="tpu_custom_call" | custom-call | flops 1024 | bytes 1024 | tf_op jit(solution)/shard_map/grad_input/pallas_call | solution.py:380
  142.5 2.0 %unpack.1 = f32[64,64,64]{2,1,0:T(8,128)} custom-call(bf16[32,64,128]{2,1,0:T(8,128)(2,1)S(1)} %all-to-all-done.3.pairs_ref), custom_call_target="tpu_custom_call" | custom-call | flops 1024 | bytes 1024 | tf_op jit(solution)/shard_map/unpack/pallas_call | solution.py:380
  (79 shorter events, 16.1 us)
Async XLA Ops:
  7.5 8.2 %copy-start.4 = (bf16[512,2048]{1,0:T(8,128)(2,1)S(1)}, bf16[512,2048]{1,0:T(8,128)(2,1)}, u32[]{:S(2)}) copy-start(bf16[512,2048]{1,0:T(8,128)(2,1)} %grad_hbm.1) | copy-start | bytes 6291460
  7.5 8.2 %copy-start.16 = (bf16[512,256]{1,0:T(8,128)(2,1)S(1)}, bf16[512,256]{1,0:T(8,128)(2,1)}, u32[]{:S(2)}) copy-start(bf16[512,256]{1,0:T(8,128)(2,1)} %acts_hbm.1) | copy-start | bytes 786436
  7.5 8.2 %copy-start.17 = (s32[6]{0:T(128)S(1)}, s32[6]{0:T(128)}, u32[]{:S(2)}) copy-start(s32[6]{0:T(128)} %stack.23.place) | copy-start | bytes 76
  8.8 13.3 %copy-start.18 = (bf16[144,256]{1,0:T(8,128)(2,1)S(1)}, bf16[144,256]{1,0:T(8,128)(2,1)}, u32[]{:S(2)}) copy-start(bf16[144,256]{1,0:T(8,128)(2,1)} %get-tuple-element.29.refs_0_) | copy-start | bytes 221188
  8.8 14.9 %collective-permute-start = (bf16[8192,128]{1,0:T(8,128)(2,1)S(1)}, bf16[8192,128]{1,0:T(8,128)(2,1)S(1)}, u32[]{:S(2)}, u32[]{:S(2)}) collective-permute-start(bf16[8192,128]{1,0:T(8,128)(2,1)S(1)} %turn_input.1.xt_ref), channel_id=1, source_target_pairs={{0,4},{4,0},{1,5},{5,1},{2,6},{6,2},{3,7},{7,3},{8,12},{12,8},{9,1... | collective-permute-start | bytes 6291464 | tf_op jit(solution)/shard_map/ppermute | solution.py:372
  12.1 5.5 %collective-permute-start.1 = (bf16[144,256]{1,0:T(8,128)(2,1)S(1)}, bf16[144,256]{1,0:T(8,128)(2,1)S(1)}, u32[]{:S(2)}, u32[]{:S(2)}) collective-permute-start(bf16[144,256]{1,0:T(8,128)(2,1)S(1)} %copy-done.21), channel_id=1, source_target_pairs={{0,1},{1,0},{2,3},{3,2},{4,5},{5,4},{6,7},{7,6},{8,9},{9,8},{10,11... | collective-permute-start | bytes 221192 | tf_op jit(solution)/shard_map/ppermute | solution.py:376
  12.1 8.5 %collective-permute-start.2 = (bf16[144,256]{1,0:T(8,128)(2,1)S(1)}, bf16[144,256]{1,0:T(8,128)(2,1)S(1)}, u32[]{:S(2)}, u32[]{:S(2)}) collective-permute-start(bf16[144,256]{1,0:T(8,128)(2,1)S(1)} %copy-done.20), channel_id=1, source_target_pairs={{0,2},{1,3},{2,0},{3,1},{4,6},{5,7},{6,4},{7,5},{8,10},{9,11},{10,... | collective-permute-start | bytes 221192 | tf_op jit(solution)/shard_map/ppermute | solution.py:376
  15.0 7.1 %collective-permute-start.3 = (bf16[144,256]{1,0:T(8,128)(2,1)S(1)}, bf16[144,256]{1,0:T(8,128)(2,1)S(1)}, u32[]{:S(2)}, u32[]{:S(2)}) collective-permute-start(bf16[144,256]{1,0:T(8,128)(2,1)S(1)} %copy-done.19), channel_id=1, source_target_pairs={{0,3},{1,2},{2,1},{3,0},{4,7},{5,6},{6,5},{7,4},{8,11},{9,10},{10,... | collective-permute-start | bytes 221192 | tf_op jit(solution)/shard_map/ppermute | solution.py:376
  15.7 25.2 %collective-permute-start.11 = (bf16[128,2048]{1,0:T(8,128)(2,1)}, bf16[128,2048]{1,0:T(8,128)(2,1)S(1)}, u32[]{:S(2)}, u32[]{:S(2)}) collective-permute-start(bf16[128,2048]{1,0:T(8,128)(2,1)} %get-tuple-element.43), channel_id=1, source_target_pairs={{0,1},{1,0},{2,3},{3,2},{4,5},{5,4},{6,7},{7,6},{8,9},{9,8},{10,11... | collective-permute-start | bytes 1572872 | tf_op jit(solution)/shard_map/ppermute | solution.py:376
  17.6 26.7 %collective-permute-start.12 = (bf16[128,2048]{1,0:T(8,128)(2,1)}, bf16[128,2048]{1,0:T(8,128)(2,1)}, u32[]{:S(2)}, u32[]{:S(2)}) collective-permute-start(bf16[128,2048]{1,0:T(8,128)(2,1)} %get-tuple-element.44), channel_id=1, source_target_pairs={{0,2},{1,3},{2,0},{3,1},{4,6},{5,7},{6,4},{7,5},{8,10},{9,11},{10,... | collective-permute-start | bytes 1572872 | tf_op jit(solution)/shard_map/ppermute | solution.py:376
  20.6 3.1 %collective-permute-start.5 = (bf16[128,2048]{1,0:T(8,128)(2,1)S(1)}, bf16[128,2048]{1,0:T(8,128)(2,1)S(1)}, u32[]{:S(2)}, u32[]{:S(2)}) collective-permute-start(bf16[128,2048]{1,0:T(8,128)(2,1)S(1)} %get-tuple-element.33.refs_4_), channel_id=1, source_target_pairs={{0,4},{4,0},{1,5},{5,1},{2,6},{6,2},{3,7},{7,3},{8,12},{12,8},{9,1... | collective-permute-start | bytes 1572872 | tf_op jit(solution)/shard_map/ppermute | solution.py:372
  22.1 54.5 %copy-start.14 = (s32[32,256]{1,0:T(8,128)}, s32[32,256]{1,0:T(8,128)S(1)}, u32[]{:S(2)}) copy-start(s32[32,256]{1,0:T(8,128)S(1)} %get-tuple-element.41.table) | copy-start | bytes 98308
  22.1 1.6 %collective-permute-start.4 = (bf16[128,256]{1,0:T(8,128)(2,1)S(1)}, bf16[128,256]{1,0:T(8,128)(2,1)S(1)}, u32[]{:S(2)}, u32[]{:S(2)}) collective-permute-start(bf16[128,256]{1,0:T(8,128)(2,1)S(1)} %get-tuple-element.34.low_ref), channel_id=1, source_target_pairs={{0,4},{4,0},{1,5},{5,1},{2,6},{6,2},{3,7},{7,3},{8,12},{12,8},{9,1... | collective-permute-start | bytes 196616 | tf_op jit(solution)/shard_map/ppermute | solution.py:372
  28.9 51.9 %all-to-all-start = ((bf16[16,320,256]{2,1,0:T(8,128)(2,1)}), bf16[16,320,256]{2,1,0:T(8,128)(2,1)}, u32[]{:S(2)}, u32[]{:S(2)}) async-start(bf16[16,320,256]{2,1,0:T(8,128)(2,1)} %copy-done.3), calls=%async_computation | async-start | bytes 5242880 | tf_op jit(solution)/shard_map/all_to_all | solution.py:452
  35.8 11.9 %collective-permute-start.13 = (bf16[128,2048]{1,0:T(8,128)(2,1)S(1)}, bf16[128,2048]{1,0:T(8,128)(2,1)S(1)}, u32[]{:S(2)}, u32[]{:S(2)}) collective-permute-start(bf16[128,2048]{1,0:T(8,128)(2,1)S(1)} %copy-done.7), channel_id=1, source_target_pairs={{0,4},{4,0},{1,5},{5,1},{2,6},{6,2},{3,7},{7,3},{8,12},{12,8},{9,1... | collective-permute-start | bytes 1572872 | tf_op jit(solution)/shard_map/ppermute | solution.py:372
  40.9 6.9 %collective-permute-start.14 = (bf16[128,2048]{1,0:T(8,128)(2,1)S(1)}, bf16[128,2048]{1,0:T(8,128)(2,1)S(1)}, u32[]{:S(2)}, u32[]{:S(2)}) collective-permute-start(bf16[128,2048]{1,0:T(8,128)(2,1)S(1)} %collective-permute-done.11.refs_1_), channel_id=1, source_target_pairs={{0,4},{4,0},{1,5},{5,1},{2,6},{6,2},{3,7},{7,3},{8,12},{12,8},{9,1... | collective-permute-start | bytes 1572872 | tf_op jit(solution)/shard_map/ppermute | solution.py:372
  44.3 3.5 %collective-permute-start.15 = (bf16[128,2048]{1,0:T(8,128)(2,1)}, bf16[128,2048]{1,0:T(8,128)(2,1)S(1)}, u32[]{:S(2)}, u32[]{:S(2)}) collective-permute-start(bf16[128,2048]{1,0:T(8,128)(2,1)} %collective-permute-done.12.refs_2_), channel_id=1, source_target_pairs={{0,4},{4,0},{1,5},{5,1},{2,6},{6,2},{3,7},{7,3},{8,12},{12,8},{9,1... | collective-permute-start | bytes 1572872 | tf_op jit(solution)/shard_map/ppermute | solution.py:372
  45.6 15.7 %collective-permute-start.10 = (bf16[128,2048]{1,0:T(8,128)(2,1)}, bf16[128,2048]{1,0:T(8,128)(2,1)S(1)}, u32[]{:S(2)}, u32[]{:S(2)}) collective-permute-start(bf16[128,2048]{1,0:T(8,128)(2,1)} %get-tuple-element.42), channel_id=1, source_target_pairs={{0,3},{1,2},{2,1},{3,0},{4,7},{5,6},{6,5},{7,4},{8,11},{9,10},{10,... | collective-permute-start | bytes 1572872 | tf_op jit(solution)/shard_map/ppermute | solution.py:376
  61.3 15.3 %copy-start.2 = (bf16[8192,128]{1,0:T(8,128)(2,1)S(1)}, bf16[8192,128]{1,0:T(8,128)(2,1)}, u32[]{:S(2)}) copy-start(bf16[8192,128]{1,0:T(8,128)(2,1)} %copy-done) | copy-start | bytes 6291460
  61.3 15.3 %collective-permute-start.16 = (bf16[128,2048]{1,0:T(8,128)(2,1)S(1)}, bf16[128,2048]{1,0:T(8,128)(2,1)S(1)}, u32[]{:S(2)}, u32[]{:S(2)}) collective-permute-start(bf16[128,2048]{1,0:T(8,128)(2,1)S(1)} %gate.1.refs_0_), channel_id=1, source_target_pairs={{0,4},{4,0},{1,5},{5,1},{2,6},{6,2},{3,7},{7,3},{8,12},{12,8},{9,1... | collective-permute-start | bytes 1572872 | tf_op jit(solution)/shard_map/ppermute | solution.py:372
  63.2 16.8 %copy-start.8 = (bf16[32,64,128]{2,1,0:T(8,128)(2,1)}, bf16[32,64,128]{2,1,0:T(8,128)(2,1)S(1)}, u32[]{:S(2)}) copy-start(bf16[32,64,128]{2,1,0:T(8,128)(2,1)S(1)} %pack.1.refs_3_) | copy-start | bytes 1572868
  63.2 26.8 %collective-permute-start.17 = (bf16[32,64,128]{2,1,0:T(8,128)(2,1)S(1)}, bf16[32,64,128]{2,1,0:T(8,128)(2,1)S(1)}, u32[]{:S(2)}, u32[]{:S(2)}) collective-permute-start(bf16[32,64,128]{2,1,0:T(8,128)(2,1)S(1)} %pack.1.refs_3_), channel_id=1, source_target_pairs={{0,1},{1,2},{2,3},{3,128},{128,129},{129,130},{130,131},{131,0},{4... | collective-permute-start | bytes 1572872 | tf_op jit(solution)/shard_map/ppermute | solution.py:509
  72.1 17.9 %collective-permute-start.18 = (bf16[32,64,128]{2,1,0:T(8,128)(2,1)S(1)}, bf16[32,64,128]{2,1,0:T(8,128)(2,1)}, u32[]{:S(2)}, u32[]{:S(2)}) collective-permute-start(bf16[32,64,128]{2,1,0:T(8,128)(2,1)S(1)} %pack.1.refs_3_), channel_id=1, source_target_pairs={{0,131},{1,0},{2,1},{3,2},{128,3},{129,128},{130,129},{131,130},{4... | collective-permute-start | bytes 1572872 | tf_op jit(solution)/shard_map/ppermute | solution.py:510
  72.1 27.9 %collective-permute-start.19 = (bf16[32,64,128]{2,1,0:T(8,128)(2,1)S(1)}, bf16[32,64,128]{2,1,0:T(8,128)(2,1)}, u32[]{:S(2)}, u32[]{:S(2)}) collective-permute-start(bf16[32,64,128]{2,1,0:T(8,128)(2,1)S(1)} %pack.1.refs_3_), channel_id=1, source_target_pairs={{0,2},{4,134},{1,3},{5,135},{2,128},{6,4},{3,129},{7,5},{128,130},... | collective-permute-start | bytes 1572872 | tf_op jit(solution)/shard_map/ppermute | solution.py:511
  80.8 23.7 %all-to-all-start.1 = ((bf16[16,4,64,128]{3,2,1,0:T(8,128)(2,1)}), bf16[16,4,64,128]{3,2,1,0:T(8,128)(2,1)S(1)}, u32[]{:S(2)}, u32[]{:S(2)}) async-start(bf16[16,4,64,128]{3,2,1,0:T(8,128)(2,1)} %join.1), calls=%async_computation.1 | async-start | bytes 2097152 | tf_op jit(solution)/shard_map/all_to_all | solution.py:502
  89.7 10.3 %collective-permute-start.6 = (bf16[160,256]{1,0:T(8,128)(2,1)S(1)}, bf16[160,256]{1,0:T(8,128)(2,1)S(1)}, u32[]{:S(2)}, u32[]{:S(2)}) collective-permute-start(bf16[160,256]{1,0:T(8,128)(2,1)S(1)} %get-tuple-element.37), channel_id=1, source_target_pairs={{0,128},{128,0},{1,129},{129,1},{2,130},{130,2},{3,131},{131,3},{4... | collective-permute-start | bytes 245768 | tf_op jit(solution)/shard_map/ppermute | solution.py:372
  100.0 21.8 %copy-start.9 = (bf16[32,64,128]{2,1,0:T(8,128)(2,1)}, bf16[32,64,128]{2,1,0:T(8,128)(2,1)S(1)}, u32[]{:S(2)}) copy-start(bf16[32,64,128]{2,1,0:T(8,128)(2,1)S(1)} %get-tuple-element.47.refs_1_.refs_4_) | copy-start | bytes 1572868
  105.8 14.2 %all-to-all-start.2 = ((bf16[8,64,128]{2,1,0:T(8,128)(2,1)}), bf16[8,64,128]{2,1,0:T(8,128)(2,1)S(1)}, u32[]{:S(2)}, u32[]{:S(2)}) async-start(bf16[8,64,128]{2,1,0:T(8,128)(2,1)} %stage.1), calls=%async_computation.2 | async-start | bytes 262144 | tf_op jit(solution)/shard_map/all_to_all | solution.py:538
  109.2 4.8 %collective-permute-start.7 = (bf16[128,256]{1,0:T(8,128)(2,1)S(1)}, bf16[128,256]{1,0:T(8,128)(2,1)S(1)}, u32[]{:S(2)}, u32[]{:S(2)}) collective-permute-start(bf16[128,256]{1,0:T(8,128)(2,1)S(1)} %get-tuple-element.39.refs_0_), channel_id=1, source_target_pairs={{0,1},{1,0},{2,3},{3,2},{4,5},{5,4},{6,7},{7,6},{8,9},{9,8},{10,11... | collective-permute-start | bytes 196616 | tf_op jit(solution)/shard_map/ppermute | solution.py:376
  110.7 7.0 %collective-permute-start.8 = (bf16[128,256]{1,0:T(8,128)(2,1)S(1)}, bf16[128,256]{1,0:T(8,128)(2,1)S(1)}, u32[]{:S(2)}, u32[]{:S(2)}) collective-permute-start(bf16[128,256]{1,0:T(8,128)(2,1)S(1)} %get-tuple-element.39.refs_0_), channel_id=1, source_target_pairs={{0,2},{1,3},{2,0},{3,1},{4,6},{5,7},{6,4},{7,5},{8,10},{9,11},{10,... | collective-permute-start | bytes 196616 | tf_op jit(solution)/shard_map/ppermute | solution.py:376
  112.8 6.5 %collective-permute-start.9 = (bf16[128,256]{1,0:T(8,128)(2,1)S(1)}, bf16[128,256]{1,0:T(8,128)(2,1)S(1)}, u32[]{:S(2)}, u32[]{:S(2)}) collective-permute-start(bf16[128,256]{1,0:T(8,128)(2,1)S(1)} %get-tuple-element.39.refs_0_), channel_id=1, source_target_pairs={{0,3},{1,2},{2,1},{3,0},{4,7},{5,6},{6,5},{7,4},{8,11},{9,10},{10,... | collective-permute-start | bytes 196616 | tf_op jit(solution)/shard_map/ppermute | solution.py:376
  121.7 20.8 %all-to-all-start.3 = ((bf16[32,64,128]{2,1,0:T(8,128)(2,1)}), bf16[32,64,128]{2,1,0:T(8,128)(2,1)S(1)}, u32[]{:S(2)}, u32[]{:S(2)}) async-start(bf16[32,64,128]{2,1,0:T(8,128)(2,1)} %last.1), calls=%async_computation.3 | async-start | bytes 1048576 | tf_op jit(solution)/shard_map/all_to_all | solution.py:542
  (14 other events, 47.1 us)

commit v5 on v4

--- a/solution.py
+++ b/solution.py
@@ -21,7 +21,7 @@
 MIB = 1024 * 1024
 
 
-GUESS = {"delta_last": 0.0, "delta_most": 0.0, "low": 10.0, "grad_input": 0.0, "stage": 0.0, "pack": 0.0, "values": 20.0, "gate": 12.0}
+GUESS = {"delta_last": 0.0, "delta_most": 0.0, "low": 10.0, "grad_input": 0.0, "stage": 0.0, "pack": 0.0, "values": 10.0, "gate": 12.0}
 
 
 def whole():
@@ -56,7 +56,7 @@
 
 def front_kernel(place, count, *refs):
     from_hbm, lows, pieces = refs[:4], refs[4 : 4 + T], refs[4 + T : 4 + 2 * T]
-    grad_ref, up_ref, rows_ref, cols_ref, low_ref, sems = refs[4 + 2 * T :]
+    grad_ref, up_ref, rows_ref, cols_ref, low_ref, ext_ref, sems = refs[4 + 2 * T :]
     copies = [
         pltpu.make_async_copy(there, here, sems.at[i])
         for i, (there, here) in enumerate(zip(from_hbm, (grad_ref, up_ref, rows_ref, cols_ref)))
@@ -80,8 +80,10 @@
     ).astype(F32)
     line = jnp.broadcast_to(line, (16, line.shape[1])).astype(BF16)
     for k in range(T):
-        lows[k][:TOK] = low_ref[aligned(place[4] ^ k, TOK), :]
-        lows[k][TOK:] = line
+        ext_ref[k, :TOK] = low_ref[aligned(place[4] ^ k, TOK), :]
+        ext_ref[k, TOK:] = line
+        gives.append(pltpu.make_async_copy(ext_ref.at[k], lows[k], sems.at[4 + T + k]))
+        gives[-1].start()
     for give in gives:
         give.wait()
 
@@ -286,64 +288,82 @@
     give.wait()
 
 
-def input_kernel(place, table, low_ref, *refs):
-    from_hbm = refs[:7]
-    out_hbm, acc_ref, down_ref, gt_ref, values, out_ref, sems = refs[7:]
-    most = from_hbm[1].shape[0]
-    to_vmem = (
-        down_ref, gt_ref.at[:most], gt_ref.at[most:], values.at[0], values.at[1], values.at[2], values.at[3],
-    )
-    copies = [
-        pltpu.make_async_copy(there, here, sems.at[n])
-        for n, (there, here) in enumerate(zip(from_hbm, to_vmem))
-    ]
-    for copy in copies:
-        copy.start()
-    low = low_ref[...]
-    step = 512
-    width = gt_ref.shape[0] // T
-
-    def dense(i, carry):
-        acc_ref[aligned(i, step), :] = lax.dot_general(
-            down_ref[aligned(i, step), :], low, LANES_OVER, preferred_element_type=F32
-        )
-        return carry
-
-    copies[0].wait()
-    lax.fori_loop(0, acc_ref.shape[0] // step, dense, 0, unroll=2)
-    for copy in copies[1:]:
-        copy.wait()
+def spread(table, gt_ref, acc_ref, parts):
     lane = lax.broadcasted_iota(jnp.int32, (BLK, 2 * BLK), 1)
-
-    def product(v, k, s0, s1):
+    done = []
+    for v, k, base, s0, s1 in parts:
         zero = jnp.zeros_like(v)
         live = table[8 * k, 2 * SLOTS]
         top = jnp.where((lane < BLK) & (s0 < live), v, zero)
         bottom = jnp.where((lane >= BLK) & (s1 < live), v, zero)
         gt = jnp.concatenate(
-            [
-                gt_ref[aligned(table[8 * k, SLOTS + s] + k * (width // BLK), BLK), :]
-                for s in (s0, s1)
-            ],
-            axis=0,
+            [gt_ref[aligned(table[8 * k, SLOTS + s] + base, BLK), :] for s in (s0, s1)], axis=0
         )
-        return jnp.dot(jnp.concatenate([top, bottom], axis=0), gt, preferred_element_type=F32)
+        both = jnp.concatenate([top, bottom], axis=0)
+        done.append(jnp.dot(both, gt, preferred_element_type=F32))
+    for (_, k, _, s0, s1), part in zip(parts, done):
+        for s, add in ((s0, part[:BLK]), (s1, part[BLK:])):
+            at = aligned(table[8 * k, s], BLK)
+            acc_ref[at, :] = acc_ref[at, :] + add
+
+
+def dense_kernel(table, low_ref, down_hbm, gt_hbm, own_hbm, acc_ref, token_ref, *refs):
+    down_ref, gt_ref, own_ref, sems = refs
+    step = 1024
+    chunks = down_ref.shape[0] // step
+    copies = []
+    for i in range(chunks):
+        at = pl.ds(i * step, step)
+        copies.append(pltpu.make_async_copy(down_hbm.at[at], down_ref.at[at], sems.at[i]))
+    copies.append(pltpu.make_async_copy(gt_hbm.at[: gt_ref.shape[0]], gt_ref, sems.at[chunks]))
+    copies.append(pltpu.make_async_copy(own_hbm, own_ref, sems.at[chunks + 1]))
+    for copy in copies:
+        copy.start()
+    low = low_ref[...]
+    for i in range(chunks):
+        copies[i].wait()
+        at = slice(i * step, (i + 1) * step)
+        acc_ref[at, :] = lax.dot_general(
+            down_ref[at, :], low, LANES_OVER, preferred_element_type=F32
+        )
+    copies[chunks].wait()
+    copies[chunks + 1].wait()
 
     def pair(i, carry):
-        done = []
+        slots = [4 * i + n for n in range(4)]
+        spread(table, gt_ref, acc_ref, [(own_ref[s], 0, 0, s, s + PAIRS) for s in slots])
+        return carry
+
+    lax.fori_loop(0, PAIRS // 4, pair, 0)
+    token_ref[...] = jnp.zeros_like(token_ref)
+
+
+def input_kernel(place, table, acc_in, *refs):
+    from_hbm = refs[:5]
+    out_hbm, acc_ref, token_ref, gt_ref, values, out_ref, sems = refs[5:]
+    most = from_hbm[0].shape[0]
+    width = from_hbm[1].shape[0]
+    to_vmem = [gt_ref.at[width:most], gt_ref.at[most:]] + [values.at[n] for n in range(T - 1)]
+    here = [from_hbm[0].at[width:], *from_hbm[1:]]
+    copies = [
+        pltpu.make_async_copy(there, at, sems.at[n])
+        for n, (there, at) in enumerate(zip(here, to_vmem))
+    ]
+    for copy in copies:
+        copy.start()
+    for copy in copies:
+        copy.wait()
+
+    def pair(i, carry):
+        parts = []
         for s0 in (2 * i, 2 * i + 1):
-            s1 = s0 + PAIRS
-            for m in range(T):
-                k = 0 if m == 0 else place[m]
-                done.append((k, s0, s1, product(values[m, s0], k, s0, s1)))
-        for k, s0, s1, part in done:
-            for s, add in ((s0, part[:BLK]), (s1, part[BLK:])):
-                at = aligned(table[8 * k, s], BLK)
-                acc_ref[at, :] = acc_ref[at, :] + add
+            for m in range(1, T):
+                k = place[m]
+                parts.append((values[m - 1, s0], k, k * (width // BLK), s0, s0 + PAIRS))
+        spread(table, gt_ref, acc_ref, parts)
         return carry
 
     lax.fori_loop(0, PAIRS // 2, pair, 0)
-
     gives = []
     step = 1024
     for j in range(0, out_ref.shape[1], step):
@@ -351,11 +371,12 @@
             out_ref[:, i : i + 128] = acc_ref[i : i + 128, :].T.astype(BF16)
         at = pl.ds(j, step)
         gives.append(
-            pltpu.make_async_copy(out_ref.at[:, at], out_hbm.at[:, at], sems.at[7 + j // step])
+            pltpu.make_async_copy(out_ref.at[:, at], out_hbm.at[:, at], sems.at[5 + j // step])
         )
         gives[-1].start()
     for give in gives:
         give.wait()
+    token_ref[...] = jnp.zeros_like(token_ref)
 
 
 def ring(shift_of_core):
@@ -405,14 +426,15 @@
         front_kernel, "front",
         (shape((rows, rank), BF16),) * T + (shape((TOK, width), BF16),) * T,
         [scalars()] * 2 + [anywhere()] * 4, place, count, grad, up, slot_rows, slot_cols,
-        out_specs=(whole(),) * T + (anywhere(),) * T, room=56,
+        out_specs=(anywhere(),) * (2 * T), room=56,
         scratch=[
             pltpu.VMEM(grad.shape, BF16),
             pltpu.VMEM(up.shape, BF16),
             pltpu.VMEM((1, SLOTS), jnp.int32),
             pltpu.VMEM((1, SLOTS), jnp.int32),
             pltpu.VMEM((T * TOK, rank), BF16),
-            pltpu.SemaphoreType.DMA((4 + T,)),
+            pltpu.VMEM((T, rows, rank), BF16),
+            pltpu.SemaphoreType.DMA((4 + 2 * T,)),
         ],
     )
     parts, near = given[:T], given[T:]
@@ -450,24 +472,6 @@
         place, xt, xt_far, low, low_far, up_keep, up_got,
     )
     down_all = lax.all_to_all(down_part, ("y", "x"), 0, 0, tiled=True)
-    down_keep, down_give, up_sum = call(
-        down_sum_kernel, "down_sum",
-        (
-            shape((128, rank), F32),
-            shape((128 + 4 * width // rank, rank), BF16),
-            shape((4, width), F32),
-        ),
-        [scalars(), whole()], place, down_all,
-    )
-    down_half, up_grad = call(
-        down_half_kernel, "down_half", (shape((128, rank), BF16), shape((4, width), F32)),
-        [whole()] * 3, down_keep, swap(down_give, "zh"), up_sum,
-    )
-    down_grad = call(
-        down_last_kernel, "down_last", shape((128, rank), F32), [whole()] * T,
-        down_half, *[cross(down_half, k) for k in (1, 2, 3)],
-    )
-
     def delta_call(pieces, *before):
         n = len(pieces)
         return call(
@@ -488,8 +492,23 @@
 
     far = [swap(near[k]) for k in (0, 1, 2)]
     delta_most, grad_most = delta_call((0, 1, 2))
+    token = shape((8, 128), F32)
+    packed = call(
+        pack_kernel, "pack", shape((PAIRS, BLK, 2 * BLK), BF16), [whole()], values[0],
+    )
+    acc, token = call(
+        dense_kernel, "dense", (shape((feat, TOK), F32), token),
+        [scalars(), whole()] + [anywhere()] * 3, table, low, down, grad_most, packed, room=24,
+        scratch=[
+            pltpu.VMEM(down.shape, BF16),
+            pltpu.VMEM((width, TOK), BF16),
+            pltpu.VMEM((PAIRS, BLK, 2 * BLK), BF16),
+            pltpu.SemaphoreType.DMA((10,)),
+        ],
+    )
+
     near[3] = call(
-        pass_kernel, "gate", shape((TOK, width), BF16), [anywhere()] * 2, near[3], delta_most,
+        pass_kernel, "gate", shape((TOK, width), BF16), [anywhere(), whole()], near[3], token,
         out_specs=anywhere(), input_output_aliases={0: 0},
     )
     far.append(swap(near[3]))
@@ -501,9 +520,25 @@
     )
     delta_all = lax.all_to_all(delta_part, ("y", "x"), 0, 0, tiled=True)
 
-    packed = call(
-        pack_kernel, "pack", shape((PAIRS, BLK, 2 * BLK), BF16), [whole()], values[0],
-    )
+    down_keep, down_give, up_sum = call(
+        down_sum_kernel, "down_sum",
+        (
+            shape((128, rank), F32),
+            shape((128 + 4 * width // rank, rank), BF16),
+            shape((4, width), F32),
+        ),
+        [scalars(), whole()], place, down_all,
+    )
+    down_half, up_grad = call(
+        down_half_kernel, "down_half", (shape((128, rank), BF16), shape((4, width), F32)),
+        [whole()] * 3, down_keep, swap(down_give, "zh"), up_sum,
+    )
+    down_grad = call(
+        down_last_kernel, "down_last", shape((128, rank), F32), [whole()] * T,
+        down_half, *[cross(down_half, k) for k in (1, 2, 3)],
+    )
+
+
     axes = ("zh", "t")
     got = [
         lax.ppermute(packed, axes, [(i, (i + 1) % (ZH * T)) for i in range(ZH * T)]),
@@ -514,19 +549,19 @@
         pass_kernel, "values", (shape(packed.shape, BF16),) * 3, [anywhere()] * 3, *got,
         out_specs=(anywhere(),) * 3, input_output_aliases={0: 0, 1: 1, 2: 2},
     )
-    grad_input = call(
-        input_kernel, "grad_input", shape((TOK, feat), BF16),
-        [scalars()] * 2 + [whole()] + [anywhere()] * 7,
-        place, table, low, down, grad_most, grad_last, packed, *got, room=56,
-        out_specs=anywhere(),
+    grad_input, _, token = call(
+        input_kernel, "grad_input",
+        (shape((TOK, feat), BF16), shape((feat, TOK), F32), shape((8, 128), F32)),
+        [scalars()] * 2 + [whole()] + [anywhere()] * 5,
+        place, table, acc, grad_most, grad_last, *got, room=24,
+        out_specs=(anywhere(), whole(), whole()),
         scratch=[
-            pltpu.VMEM((feat, TOK), F32),
-            pltpu.VMEM(down.shape, BF16),
             pltpu.VMEM((T * width, TOK), BF16),
-            pltpu.VMEM((T, PAIRS, BLK, 2 * BLK), BF16),
+            pltpu.VMEM((T - 1, PAIRS, BLK, 2 * BLK), BF16),
             pltpu.VMEM((TOK, feat), BF16),
-            pltpu.SemaphoreType.DMA((7 + feat // 1024,)),
+            pltpu.SemaphoreType.DMA((5 + feat // 1024,)),
         ],
+        input_output_aliases={2: 1},
     )
 
     stage = call(
@@ -537,7 +572,7 @@
 
     stage_all = lax.all_to_all(stage, ("zh", "t"), 0, 0, tiled=True)
     delta_one = call(
-        last_kernel, "last", shape((PAIRS, BLK, 2 * BLK), BF16), [whole()] * 2, stage_all, down_grad,
+        last_kernel, "last", shape((PAIRS, BLK, 2 * BLK), BF16), [whole()] * 2, stage_all, token,
     )
     delta_full = lax.all_to_all(delta_one, ("y", "x", "c"), 0, 0, tiled=True)
     grad_delta = call(

time: 145 us -> 142 us (0.979)
  waiting for transfers between devices: 34.7 us -> 28 us
  local copies, waits for them, and re-layouts: 8.22 us -> 12.3 us
  starting transfers between devices: 61.9 us -> 58.1 us
  Pallas kernels: 38.1 us -> 41 us
    ppermute x9, waiting for transfers between devices: 19.7 us -> 12.6 us  [cross(): return lax.ppermute(array, 't', [(i, i ^ k) for i in range(T)])]
    unnamed x44 -> x46, local copies, waits for them, and re-layouts: 7.56 us -> 11.7 us
    all_to_all x1, starting transfers between devices: 9.22 us -> 6.31 us  [per_device(): delta_full = lax.all_to_all(delta_one, ('y', 'x', 'c'), 0, 0, tiled=True)]
    pallas_call x18 -> x19, Pallas kernels: 38.1 us -> 41 us  [call(): pl.pallas_call(kernel, out_shape=outs, in_specs=in_specs, out_specs=out_s...]
    ppermute x1, starting transfers between devices: 8.86 us -> 6.1 us  [per_device(): lax.ppermute(packed, axes, [(i, (i + 1) % (ZH * T)) for i in range(ZH * T)])]
    all_to_all x1, starting transfers between devices: 3.47 us -> 6.03 us  [per_device(): stage_all = lax.all_to_all(stage, ('zh', 't'), 0, 0, tiled=True)]
    all_to_all x1, waiting for transfers between devices: 0.29 us -> 1.84 us  [per_device(): delta_full = lax.all_to_all(delta_one, ('y', 'x', 'c'), 0, 0, tiled=True)]
  transfers between devices with their start and end apart: 24 -> 24, of which waited for: 10 -> 7; matrix products, arithmetic and copies ran while one was open for 0% -> 0% of each run, Pallas kernels for 20% -> 22%
where the time goes in v5:
time: 142 us; the launch traced here: 141 us
  starting transfers between devices  58.1 us (41%)
  Pallas kernels  41 us (29%)
  waiting for transfers between devices  28 us (20%)
  local copies, waits for them, and re-layouts  12.3 us (9%)
  between operations  1.65 us (1%)
    pallas_call x19, Pallas kernels, call(): pl.pallas_call(kernel, out_shape=outs, in_specs=in_specs, out_specs=out_s...  41 us
    ppermute x9, waiting for transfers between devices, cross(): return lax.ppermute(array, 't', [(i, i ^ k) for i in range(T)])  12.6 us
    ppermute x9, starting transfers between devices, cross(): return lax.ppermute(array, 't', [(i, i ^ k) for i in range(T)])  12.5 us
    unnamed x46, local copies, waits for them, and re-layouts  11.7 us
    ppermute x1, waiting for transfers between devices, per_device(): lax.ppermute(packed, ('zh', 'c', 't'), ring((2, -2)))  8.83 us
    ppermute x8, starting transfers between devices, swap(): return lax.ppermute(array, axis, [(0, 1), (1, 0)])  8.5 us
    all_to_all x1, starting transfers between devices, per_device(): down_all = lax.all_to_all(down_part, ('y', 'x'), 0, 0, tiled=True)  6.94 us
    all_to_all x1, starting transfers between devices, per_device(): delta_all = lax.all_to_all(delta_part, ('y', 'x'), 0, 0, tiled=True)  6.77 us
  transfers between devices with their start and end apart: 24, of which 7 were waited for; matrix products, arithmetic and copies ran while one was open for 0% of the time, Pallas kernels for 22%

profile of v5, /device:TPU:1, one launch (start us, length us, event | category | flops | bytes accessed | tf_op | source)
XLA Modules:
  0.0 141.1 jit_solution(18119216257948486853)
XLA Ops:
  1.9 4.2 %front.1 = (bf16[144,256]{1,0:T(8,128)(2,1)}, bf16[144,256]{1,0:T(8,128)(2,1)}, bf16[144,256]{1,0:T(8,128)(2,1)}, bf16[144,256]{1,0:T(8,128)(2,1)}, bf16[128,204...) custom-call(s32[6]{0:T(128)} %stack.23.place, ...), custom_call_target="tpu_custom_call" | custom-call | flops 1024 | bytes 1024 | tf_op jit(solution)/shard_map/front/pallas_call | solution.py:401
  8.5 3.3 %collective-permute-start = (bf16[8192,128]{1,0:T(8,128)(2,1)S(1)}, bf16[8192,128]{1,0:T(8,128)(2,1)S(1)}, u32[]{:S(2)}, u32[]{:S(2)}) collective-permute-start(bf16[8192,128]{1,0:T(8,128)(2,1)S(1)} %turn_input.1.xt_ref), channel_id=1, source_target_pairs={{0,4},{4,0},{1,5},{5,1},{2,6},{6,2},{3,7},{7,3},{8,12},{12,8},{9,1... | collective-permute-start | bytes 6291464 | tf_op jit(solution)/shard_map/ppermute | solution.py:393
  11.8 2.9 %collective-permute-start.2 = (bf16[144,256]{1,0:T(8,128)(2,1)S(1)}, bf16[144,256]{1,0:T(8,128)(2,1)S(1)}, u32[]{:S(2)}, u32[]{:S(2)}) collective-permute-start(bf16[144,256]{1,0:T(8,128)(2,1)S(1)} %copy-done.21), channel_id=1, source_target_pairs={{0,2},{1,3},{2,0},{3,1},{4,6},{5,7},{6,4},{7,5},{8,10},{9,11},{10,... | collective-permute-start | bytes 221192 | tf_op jit(solution)/shard_map/ppermute | solution.py:397
  15.4 1.9 %up_part.1 = (f32[128,2048]{1,0:T(8,128)S(1)}, bf16[128,2048]{1,0:T(8,128)(2,1)S(1)}) custom-call(s32[6]{0:T(128)S(1)} %copy-done.17, bf16[512,2048]{1,0:T(8,128)(2,1)S(1)} %copy-done.4, bf16[512,256]{1,0:T(8,128)(2,1)S(1)} %copy-done.16), custom_call_target="tpu_custom_call" | custom-call | flops 1024 | bytes 1024 | tf_op jit(solution)/shard_map/up_part/pallas_call | solution.py:401
  18.3 2.9 %collective-permute-start.12 = (bf16[128,2048]{1,0:T(8,128)(2,1)S(1)}, bf16[128,2048]{1,0:T(8,128)(2,1)}, u32[]{:S(2)}, u32[]{:S(2)}) collective-permute-start(bf16[128,2048]{1,0:T(8,128)(2,1)S(1)} %copy-done.19), channel_id=1, source_target_pairs={{0,2},{1,3},{2,0},{3,1},{4,6},{5,7},{6,4},{7,5},{8,10},{9,11},{10,... | collective-permute-start | bytes 1572872 | tf_op jit(solution)/shard_map/ppermute | solution.py:397
  22.9 2.3 %down_part.1 = bf16[16,320,256]{2,1,0:T(8,128)(2,1)S(1)} custom-call(s32[6]{0:T(128)S(1)} %copy-done.17, bf16[8192,128]{1,0:T(8,128)(2,1)S(1)} %turn_input.1.xt_ref, bf16[8192,128]{1,0:T(8,128)(2,1)S(1)} %collective-permute-done.xt_far_ref, bf16[128,256]{1,0:T(8,128)(2,1)S(1)} %get-tuple-element.38.low_ref, ...), custom_call_target="tpu_custom_call" | custom-call | flops 1024 | bytes 1024 | tf_op jit(solution)/shard_map/down_part/pallas_call | solution.py:401
  26.6 1.6 %copy-done.3 = bf16[16,320,256]{2,1,0:T(8,128)(2,1)} copy-done((bf16[16,320,256]{2,1,0:T(8,128)(2,1)}, bf16[16,320,256]{2,1,0:T(8,128)(2,1)S(1)}, u32[]{:S(2)}) %copy-start.3) | copy-done | bytes 2621464
  28.1 6.9 %all-to-all-start = ((bf16[16,320,256]{2,1,0:T(8,128)(2,1)}), bf16[16,320,256]{2,1,0:T(8,128)(2,1)}, u32[]{:S(2)}, u32[]{:S(2)}) async-start(bf16[16,320,256]{2,1,0:T(8,128)(2,1)} %copy-done.3), calls=%async_computation | async-start | bytes 5242880 | tf_op jit(solution)/shard_map/all_to_all | solution.py:474
  35.8 7.5 %collective-permute-done.11.refs_1_ = bf16[128,2048]{1,0:T(8,128)(2,1)} collective-permute-done((bf16[128,2048]{1,0:T(8,128)(2,1)}, bf16[128,2048]{1,0:T(8,128)(2,1)}, u32[]{:S(2)}, u32[]{:S(2)}) %collective-permute-start.11) | collective-permute-done | bytes 524320 | tf_op jit(solution)/shard_map/ppermute | solution.py:397
  45.5 2.1 %collective-permute-start.10 = (bf16[128,2048]{1,0:T(8,128)(2,1)}, bf16[128,2048]{1,0:T(8,128)(2,1)S(1)}, u32[]{:S(2)}, u32[]{:S(2)}) collective-permute-start(bf16[128,2048]{1,0:T(8,128)(2,1)} %get-tuple-element.46), channel_id=1, source_target_pairs={{0,3},{1,2},{2,1},{3,0},{4,7},{5,6},{6,5},{7,4},{8,11},{9,10},{10,... | collective-permute-start | bytes 1572872 | tf_op jit(solution)/shard_map/ppermute | solution.py:397
  49.6 1.6 %copy-done.1 = bf16[8192,128]{1,0:T(8,128)(2,1)S(1)} copy-done((bf16[8192,128]{1,0:T(8,128)(2,1)S(1)}, bf16[8192,128]{1,0:T(8,128)(2,1)}, u32[]{:S(2)}) %copy-start.1) | copy-done | bytes 2097176
  51.2 5.5 %delta_most.1 = (bf16[16,4,64,128]{3,2,1,0:T(8,128)(2,1)}, bf16[6144,128]{1,0:T(8,128)(2,1)S(1)}) custom-call(s32[6]{0:T(128)S(1)} %copy-done.17, s32[32,256]{1,0:T(8,128)S(1)} %get-tuple-element.45.table, bf16[8192,128]{1,0:T(8,128)(2,1)S(1)} %turn_input.1.xt_ref, bf16[8192,128]{1,0:T(8,128)(2,1)S(1)} %copy-done.1, bf16[128,2048]{1,0:T(8,128)(2,1)S(1)} %copy-done.12, ...), custom_call_target="tpu_custom_call" | custom-call | flops 1024 | bytes 1024 | tf_op jit(solution)/shard_map/delta_most/pallas_call | solution.py:401
  56.7 6.4 %dense.1 = (f32[8192,128]{1,0:T(8,128)S(1)}, f32[8,128]{1,0:T(8,128)S(1)}) custom-call(s32[32,256]{1,0:T(8,128)S(1)} %get-tuple-element.45.table, bf16[128,256]{1,0:T(8,128)(2,1)S(1)} %get-tuple-element.38.low_ref, bf16[8192,256]{1,0:T(8,128)(2,1)S(1)} %copy-done.7, bf16[6144,128]{1,0:T(8,128)(2,1)S(1)} %get-tuple-element.49.gt_hbm.refs_0_, ...), custom_call_target="tpu_custom_call" | custom-call | flops 1024 | bytes 1024 | tf_op jit(solution)/shard_map/dense/pallas_call | solution.py:401
  63.1 2.0 %copy-done.8 = f32[8192,128]{1,0:T(8,128)} copy-done((f32[8192,128]{1,0:T(8,128)}, f32[8192,128]{1,0:T(8,128)S(1)}, u32[]{:S(2)}) %copy-start.8) | copy-done | bytes 4194328
  65.4 6.1 %collective-permute-start.17 = (bf16[32,64,128]{2,1,0:T(8,128)(2,1)S(1)}, bf16[32,64,128]{2,1,0:T(8,128)(2,1)}, u32[]{:S(2)}, u32[]{:S(2)}) collective-permute-start(bf16[32,64,128]{2,1,0:T(8,128)(2,1)S(1)} %pack.1.own_hbm), channel_id=1, source_target_pairs={{0,1},{1,2},{2,3},{3,128},{128,129},{129,130},{130,131},{131,0},{4... | collective-permute-start | bytes 1572872 | tf_op jit(solution)/shard_map/ppermute | solution.py:544
  71.5 5.0 %collective-permute-start.19 = (bf16[32,64,128]{2,1,0:T(8,128)(2,1)S(1)}, bf16[32,64,128]{2,1,0:T(8,128)(2,1)}, u32[]{:S(2)}, u32[]{:S(2)}) collective-permute-start(bf16[32,64,128]{2,1,0:T(8,128)(2,1)S(1)} %pack.1.own_hbm), channel_id=1, source_target_pairs={{0,2},{4,134},{1,3},{5,135},{2,128},{6,4},{3,129},{7,5},{128,130},... | collective-permute-start | bytes 1572872 | tf_op jit(solution)/shard_map/ppermute | solution.py:546
  76.5 3.3 %delta_last.1 = (bf16[16,4,64,128]{3,2,1,0:T(8,128)(2,1)}, bf16[2048,128]{1,0:T(8,128)(2,1)S(1)}) custom-call(s32[6]{0:T(128)S(1)} %copy-done.17, s32[32,256]{1,0:T(8,128)S(1)} %get-tuple-element.45.table, bf16[8192,128]{1,0:T(8,128)(2,1)S(1)} %turn_input.1.xt_ref, bf16[8192,128]{1,0:T(8,128)(2,1)S(1)} %copy-done.2, ...), custom_call_target="tpu_custom_call", output_to_operand_aliasing={{0}: (6, {})} | custom-call | flops 1024 | bytes 1024 | tf_op jit(solution)/shard_map/delta_last/pallas_call | solution.py:401
  80.6 6.8 %all-to-all-start.1 = ((bf16[16,4,64,128]{3,2,1,0:T(8,128)(2,1)}), bf16[16,4,64,128]{3,2,1,0:T(8,128)(2,1)S(1)}, u32[]{:S(2)}, u32[]{:S(2)}) async-start(bf16[16,4,64,128]{3,2,1,0:T(8,128)(2,1)} %join.1), calls=%async_computation.1 | async-start | bytes 2097152 | tf_op jit(solution)/shard_map/all_to_all | solution.py:521
  87.4 2.1 %down_sum.1 = (f32[128,256]{1,0:T(8,128)S(1)}, bf16[160,256]{1,0:T(8,128)(2,1)S(1)}, f32[4,2048]{1,0:T(4,128)S(1)}) custom-call(s32[6]{0:T(128)S(1)} %copy-done.17, bf16[16,320,256]{2,1,0:T(8,128)(2,1)} %all-to-all-done.down_ref.refs_1_), custom_call_target="tpu_custom_call" | custom-call | flops 1024 | bytes 1024 | tf_op jit(solution)/shard_map/down_sum/pallas_call | solution.py:401
  89.8 8.8 %collective-permute-done.19.refs_2_ = bf16[32,64,128]{2,1,0:T(8,128)(2,1)} collective-permute-done((bf16[32,64,128]{2,1,0:T(8,128)(2,1)S(1)}, bf16[32,64,128]{2,1,0:T(8,128)(2,1)}, u32[]{:S(2)}, u32[]{:S(2)}) %collective-permute-start.19) | collective-permute-done | bytes 524320 | tf_op jit(solution)/shard_map/ppermute | solution.py:546
  99.2 3.8 %all-to-all-done.1.delta_ref = bf16[16,4,64,128]{3,2,1,0:T(8,128)(2,1)S(1)} async-done(((bf16[16,4,64,128]{3,2,1,0:T(8,128)(2,1)}), bf16[16,4,64,128]{3,2,1,0:T(8,128)(2,1)S(1)}, u32[]{:S(2)}, u32[]{:S(2)}) %all-to-all-start.1) | async-done | bytes 1048608 | tf_op jit(solution)/shard_map/all_to_all | solution.py:521
  103.0 1.3 stage.1
  104.3 6.0 %all-to-all-start.2 = ((bf16[8,64,128]{2,1,0:T(8,128)(2,1)}), bf16[8,64,128]{2,1,0:T(8,128)(2,1)S(1)}, u32[]{:S(2)}, u32[]{:S(2)}) async-start(bf16[8,64,128]{2,1,0:T(8,128)(2,1)} %stage.1), calls=%async_computation.2 | async-start | bytes 262144 | tf_op jit(solution)/shard_map/all_to_all | solution.py:573
  110.4 2.2 %copy-done.9 = f32[8192,128]{1,0:T(8,128)S(1)} copy-done((f32[8192,128]{1,0:T(8,128)S(1)}, f32[8192,128]{1,0:T(8,128)}, u32[]{:S(2)}) %copy-start.9) | copy-done | bytes 4194328
  112.6 7.8 %grad_input.1 = (bf16[128,8192]{1,0:T(8,128)(2,1)}, f32[8192,128]{1,0:T(8,128)S(1)}, f32[8,128]{1,0:T(8,128)S(1)}) custom-call(s32[6]{0:T(128)S(1)} %copy-done.17, s32[32,256]{1,0:T(8,128)S(1)} %get-tuple-element.45.table, f32[8192,128]{1,0:T(8,128)S(1)} %copy-done.9, bf16[6144,128]{1,0:T(8,128)(2,1)S(1)} %copy-done.6, ...), custom_call_target="tpu_custom_call", output_to_operand_aliasing={{1}: (2, {})} | custom-call | flops 1024 | bytes 1024 | tf_op jit(solution)/shard_map/grad_input/pallas_call | solution.py:401
  121.2 6.3 %all-to-all-start.3 = ((bf16[32,64,128]{2,1,0:T(8,128)(2,1)}), bf16[32,64,128]{2,1,0:T(8,128)(2,1)S(1)}, u32[]{:S(2)}, u32[]{:S(2)}) async-start(bf16[32,64,128]{2,1,0:T(8,128)(2,1)} %last.1), calls=%async_computation.3 | async-start | bytes 1048576 | tf_op jit(solution)/shard_map/all_to_all | solution.py:577
  127.6 1.7 %collective-permute-start.7 = (bf16[128,256]{1,0:T(8,128)(2,1)S(1)}, bf16[128,256]{1,0:T(8,128)(2,1)S(1)}, u32[]{:S(2)}, u32[]{:S(2)}) collective-permute-start(bf16[128,256]{1,0:T(8,128)(2,1)S(1)} %get-tuple-element.43.refs_0_), channel_id=1, source_target_pairs={{0,1},{1,0},{2,3},{3,2},{4,5},{5,4},{6,7},{7,6},{8,9},{9,8},{10,11... | collective-permute-start | bytes 196616 | tf_op jit(solution)/shard_map/ppermute | solution.py:397
  129.3 2.1 %collective-permute-start.8 = (bf16[128,256]{1,0:T(8,128)(2,1)S(1)}, bf16[128,256]{1,0:T(8,128)(2,1)S(1)}, u32[]{:S(2)}, u32[]{:S(2)}) collective-permute-start(bf16[128,256]{1,0:T(8,128)(2,1)S(1)} %get-tuple-element.43.refs_0_), channel_id=1, source_target_pairs={{0,2},{1,3},{2,0},{3,1},{4,6},{5,7},{6,4},{7,5},{8,10},{9,11},{10,... | collective-permute-start | bytes 196616 | tf_op jit(solution)/shard_map/ppermute | solution.py:397
  131.5 2.3 %collective-permute-done.8.refs_2_ = bf16[128,256]{1,0:T(8,128)(2,1)S(1)} collective-permute-done((bf16[128,256]{1,0:T(8,128)(2,1)S(1)}, bf16[128,256]{1,0:T(8,128)(2,1)S(1)}, u32[]{:S(2)}, u32[]{:S(2)}) %collective-permute-start.8) | collective-permute-done | bytes 65568 | tf_op jit(solution)/shard_map/ppermute | solution.py:397
  133.8 2.8 %collective-permute-done.9.refs_3_ = bf16[128,256]{1,0:T(8,128)(2,1)S(1)} collective-permute-done((bf16[128,256]{1,0:T(8,128)(2,1)S(1)}, bf16[128,256]{1,0:T(8,128)(2,1)S(1)}, u32[]{:S(2)}, u32[]{:S(2)}) %collective-permute-start.9) | collective-permute-done | bytes 65568 | tf_op jit(solution)/shard_map/ppermute | solution.py:397
  137.3 1.8 %all-to-all-done.3.pairs_ref = bf16[32,64,128]{2,1,0:T(8,128)(2,1)S(1)} async-done(((bf16[32,64,128]{2,1,0:T(8,128)(2,1)}), bf16[32,64,128]{2,1,0:T(8,128)(2,1)S(1)}, u32[]{:S(2)}, u32[]{:S(2)}) %all-to-all-start.3) | async-done | bytes 524320 | tf_op jit(solution)/shard_map/all_to_all | solution.py:577
  139.1 2.0 %unpack.1 = f32[64,64,64]{2,1,0:T(8,128)} custom-call(bf16[32,64,128]{2,1,0:T(8,128)(2,1)S(1)} %all-to-all-done.3.pairs_ref), custom_call_target="tpu_custom_call" | custom-call | flops 1024 | bytes 1024 | tf_op jit(solution)/shard_map/unpack/pallas_call | solution.py:401
  (82 shorter events, 16.0 us)
Async XLA Ops:
  7.2 8.2 %copy-start.4 = (bf16[512,2048]{1,0:T(8,128)(2,1)S(1)}, bf16[512,2048]{1,0:T(8,128)(2,1)}, u32[]{:S(2)}) copy-start(bf16[512,2048]{1,0:T(8,128)(2,1)} %grad_hbm.1) | copy-start | bytes 6291460
  7.2 8.2 %copy-start.16 = (bf16[512,256]{1,0:T(8,128)(2,1)S(1)}, bf16[512,256]{1,0:T(8,128)(2,1)}, u32[]{:S(2)}) copy-start(bf16[512,256]{1,0:T(8,128)(2,1)} %acts_hbm.1) | copy-start | bytes 786436
  7.2 8.2 %copy-start.17 = (s32[6]{0:T(128)S(1)}, s32[6]{0:T(128)}, u32[]{:S(2)}) copy-start(s32[6]{0:T(128)} %stack.23.place) | copy-start | bytes 76
  8.4 9.9 %copy-start.19 = (bf16[128,2048]{1,0:T(8,128)(2,1)S(1)}, bf16[128,2048]{1,0:T(8,128)(2,1)}, u32[]{:S(2)}) copy-start(bf16[128,2048]{1,0:T(8,128)(2,1)} %get-tuple-element.48) | copy-start | bytes 1572868
  8.5 12.8 %copy-start.18 = (bf16[144,256]{1,0:T(8,128)(2,1)S(1)}, bf16[144,256]{1,0:T(8,128)(2,1)}, u32[]{:S(2)}) copy-start(bf16[144,256]{1,0:T(8,128)(2,1)} %get-tuple-element.33.refs_0_) | copy-start | bytes 221188
  8.5 14.4 %collective-permute-start = (bf16[8192,128]{1,0:T(8,128)(2,1)S(1)}, bf16[8192,128]{1,0:T(8,128)(2,1)S(1)}, u32[]{:S(2)}, u32[]{:S(2)}) collective-permute-start(bf16[8192,128]{1,0:T(8,128)(2,1)S(1)} %turn_input.1.xt_ref), channel_id=1, source_target_pairs={{0,4},{4,0},{1,5},{5,1},{2,6},{6,2},{3,7},{7,3},{8,12},{12,8},{9,1... | collective-permute-start | bytes 6291464 | tf_op jit(solution)/shard_map/ppermute | solution.py:393
  11.8 6.5 %collective-permute-start.1 = (bf16[144,256]{1,0:T(8,128)(2,1)S(1)}, bf16[144,256]{1,0:T(8,128)(2,1)S(1)}, u32[]{:S(2)}, u32[]{:S(2)}) collective-permute-start(bf16[144,256]{1,0:T(8,128)(2,1)S(1)} %copy-done.22), channel_id=1, source_target_pairs={{0,1},{1,0},{2,3},{3,2},{4,5},{5,4},{6,7},{7,6},{8,9},{9,8},{10,11... | collective-permute-start | bytes 221192 | tf_op jit(solution)/shard_map/ppermute | solution.py:397
  11.8 6.5 %collective-permute-start.2 = (bf16[144,256]{1,0:T(8,128)(2,1)S(1)}, bf16[144,256]{1,0:T(8,128)(2,1)S(1)}, u32[]{:S(2)}, u32[]{:S(2)}) collective-permute-start(bf16[144,256]{1,0:T(8,128)(2,1)S(1)} %copy-done.21), channel_id=1, source_target_pairs={{0,2},{1,3},{2,0},{3,1},{4,6},{5,7},{6,4},{7,5},{8,10},{9,11},{10,... | collective-permute-start | bytes 221192 | tf_op jit(solution)/shard_map/ppermute | solution.py:397
  14.7 6.5 %collective-permute-start.3 = (bf16[144,256]{1,0:T(8,128)(2,1)S(1)}, bf16[144,256]{1,0:T(8,128)(2,1)S(1)}, u32[]{:S(2)}, u32[]{:S(2)}) collective-permute-start(bf16[144,256]{1,0:T(8,128)(2,1)S(1)} %copy-done.20), channel_id=1, source_target_pairs={{0,3},{1,2},{2,1},{3,0},{4,7},{5,6},{6,5},{7,4},{8,11},{9,10},{10,... | collective-permute-start | bytes 221192 | tf_op jit(solution)/shard_map/ppermute | solution.py:397
  17.3 5.6 %collective-permute-start.5 = (bf16[128,2048]{1,0:T(8,128)(2,1)S(1)}, bf16[128,2048]{1,0:T(8,128)(2,1)S(1)}, u32[]{:S(2)}, u32[]{:S(2)}) collective-permute-start(bf16[128,2048]{1,0:T(8,128)(2,1)S(1)} %get-tuple-element.37.refs_4_), channel_id=1, source_target_pairs={{0,4},{4,0},{1,5},{5,1},{2,6},{6,2},{3,7},{7,3},{8,12},{12,8},{9,1... | collective-permute-start | bytes 1572872 | tf_op jit(solution)/shard_map/ppermute | solution.py:393
  18.3 25.0 %collective-permute-start.11 = (bf16[128,2048]{1,0:T(8,128)(2,1)}, bf16[128,2048]{1,0:T(8,128)(2,1)}, u32[]{:S(2)}, u32[]{:S(2)}) collective-permute-start(bf16[128,2048]{1,0:T(8,128)(2,1)} %get-tuple-element.47), channel_id=1, source_target_pairs={{0,1},{1,0},{2,3},{3,2},{4,5},{5,4},{6,7},{7,6},{8,9},{9,8},{10,11... | collective-permute-start | bytes 1572872 | tf_op jit(solution)/shard_map/ppermute | solution.py:397
  18.3 25.9 %collective-permute-start.12 = (bf16[128,2048]{1,0:T(8,128)(2,1)S(1)}, bf16[128,2048]{1,0:T(8,128)(2,1)}, u32[]{:S(2)}, u32[]{:S(2)}) collective-permute-start(bf16[128,2048]{1,0:T(8,128)(2,1)S(1)} %copy-done.19), channel_id=1, source_target_pairs={{0,2},{1,3},{2,0},{3,1},{4,6},{5,7},{6,4},{7,5},{8,10},{9,11},{10,... | collective-permute-start | bytes 1572872 | tf_op jit(solution)/shard_map/ppermute | solution.py:397
  21.3 1.6 %collective-permute-start.4 = (bf16[128,256]{1,0:T(8,128)(2,1)S(1)}, bf16[128,256]{1,0:T(8,128)(2,1)S(1)}, u32[]{:S(2)}, u32[]{:S(2)}) collective-permute-start(bf16[128,256]{1,0:T(8,128)(2,1)S(1)} %get-tuple-element.38.low_ref), channel_id=1, source_target_pairs={{0,4},{4,0},{1,5},{5,1},{2,6},{6,2},{3,7},{7,3},{8,12},{12,8},{9,1... | collective-permute-start | bytes 196616 | tf_op jit(solution)/shard_map/ppermute | solution.py:393
  28.1 51.7 %all-to-all-start = ((bf16[16,320,256]{2,1,0:T(8,128)(2,1)}), bf16[16,320,256]{2,1,0:T(8,128)(2,1)}, u32[]{:S(2)}, u32[]{:S(2)}) async-start(bf16[16,320,256]{2,1,0:T(8,128)(2,1)} %copy-done.3), calls=%async_computation | async-start | bytes 5242880 | tf_op jit(solution)/shard_map/all_to_all | solution.py:474
  35.1 14.5 %collective-permute-start.13 = (bf16[128,2048]{1,0:T(8,128)(2,1)S(1)}, bf16[128,2048]{1,0:T(8,128)(2,1)S(1)}, u32[]{:S(2)}, u32[]{:S(2)}) collective-permute-start(bf16[128,2048]{1,0:T(8,128)(2,1)S(1)} %copy-done.12), channel_id=1, source_target_pairs={{0,4},{4,0},{1,5},{5,1},{2,6},{6,2},{3,7},{7,3},{8,12},{12,8},{9,1... | collective-permute-start | bytes 1572872 | tf_op jit(solution)/shard_map/ppermute | solution.py:393
  43.3 6.3 %collective-permute-start.14 = (bf16[128,2048]{1,0:T(8,128)(2,1)}, bf16[128,2048]{1,0:T(8,128)(2,1)S(1)}, u32[]{:S(2)}, u32[]{:S(2)}) collective-permute-start(bf16[128,2048]{1,0:T(8,128)(2,1)} %collective-permute-done.11.refs_1_), channel_id=1, source_target_pairs={{0,4},{4,0},{1,5},{5,1},{2,6},{6,2},{3,7},{7,3},{8,12},{12,8},{9,1... | collective-permute-start | bytes 1572872 | tf_op jit(solution)/shard_map/ppermute | solution.py:393
  44.2 5.4 %collective-permute-start.15 = (bf16[128,2048]{1,0:T(8,128)(2,1)}, bf16[128,2048]{1,0:T(8,128)(2,1)S(1)}, u32[]{:S(2)}, u32[]{:S(2)}) collective-permute-start(bf16[128,2048]{1,0:T(8,128)(2,1)} %collective-permute-done.12.refs_2_), channel_id=1, source_target_pairs={{0,4},{4,0},{1,5},{5,1},{2,6},{6,2},{3,7},{7,3},{8,12},{12,8},{9,1... | collective-permute-start | bytes 1572872 | tf_op jit(solution)/shard_map/ppermute | solution.py:393
  45.5 19.6 %collective-permute-start.10 = (bf16[128,2048]{1,0:T(8,128)(2,1)}, bf16[128,2048]{1,0:T(8,128)(2,1)S(1)}, u32[]{:S(2)}, u32[]{:S(2)}) collective-permute-start(bf16[128,2048]{1,0:T(8,128)(2,1)} %get-tuple-element.46), channel_id=1, source_target_pairs={{0,3},{1,2},{2,1},{3,0},{4,7},{5,6},{6,5},{7,4},{8,11},{9,10},{10,... | collective-permute-start | bytes 1572872 | tf_op jit(solution)/shard_map/ppermute | solution.py:397
  65.1 11.3 %copy-start.2 = (bf16[8192,128]{1,0:T(8,128)(2,1)S(1)}, bf16[8192,128]{1,0:T(8,128)(2,1)}, u32[]{:S(2)}) copy-start(bf16[8192,128]{1,0:T(8,128)(2,1)} %copy-done) | copy-start | bytes 6291460
  65.1 11.3 %collective-permute-start.16 = (bf16[128,2048]{1,0:T(8,128)(2,1)S(1)}, bf16[128,2048]{1,0:T(8,128)(2,1)S(1)}, u32[]{:S(2)}, u32[]{:S(2)}) collective-permute-start(bf16[128,2048]{1,0:T(8,128)(2,1)S(1)} %gate.1.refs_0_), channel_id=1, source_target_pairs={{0,4},{4,0},{1,5},{5,1},{2,6},{6,2},{3,7},{7,3},{8,12},{12,8},{9,1... | collective-permute-start | bytes 1572872 | tf_op jit(solution)/shard_map/ppermute | solution.py:393
  65.4 24.3 %collective-permute-start.17 = (bf16[32,64,128]{2,1,0:T(8,128)(2,1)S(1)}, bf16[32,64,128]{2,1,0:T(8,128)(2,1)}, u32[]{:S(2)}, u32[]{:S(2)}) collective-permute-start(bf16[32,64,128]{2,1,0:T(8,128)(2,1)S(1)} %pack.1.own_hbm), channel_id=1, source_target_pairs={{0,1},{1,2},{2,3},{3,128},{128,129},{129,130},{130,131},{131,0},{4... | collective-permute-start | bytes 1572872 | tf_op jit(solution)/shard_map/ppermute | solution.py:544
  71.5 18.2 %collective-permute-start.18 = (bf16[32,64,128]{2,1,0:T(8,128)(2,1)S(1)}, bf16[32,64,128]{2,1,0:T(8,128)(2,1)}, u32[]{:S(2)}, u32[]{:S(2)}) collective-permute-start(bf16[32,64,128]{2,1,0:T(8,128)(2,1)S(1)} %pack.1.own_hbm), channel_id=1, source_target_pairs={{0,131},{1,0},{2,1},{3,2},{128,3},{129,128},{130,129},{131,130},{4... | collective-permute-start | bytes 1572872 | tf_op jit(solution)/shard_map/ppermute | solution.py:545
  71.5 27.1 %collective-permute-start.19 = (bf16[32,64,128]{2,1,0:T(8,128)(2,1)S(1)}, bf16[32,64,128]{2,1,0:T(8,128)(2,1)}, u32[]{:S(2)}, u32[]{:S(2)}) collective-permute-start(bf16[32,64,128]{2,1,0:T(8,128)(2,1)S(1)} %pack.1.own_hbm), channel_id=1, source_target_pairs={{0,2},{4,134},{1,3},{5,135},{2,128},{6,4},{3,129},{7,5},{128,130},... | collective-permute-start | bytes 1572872 | tf_op jit(solution)/shard_map/ppermute | solution.py:546
  80.6 22.4 %all-to-all-start.1 = ((bf16[16,4,64,128]{3,2,1,0:T(8,128)(2,1)}), bf16[16,4,64,128]{3,2,1,0:T(8,128)(2,1)S(1)}, u32[]{:S(2)}, u32[]{:S(2)}) async-start(bf16[16,4,64,128]{3,2,1,0:T(8,128)(2,1)} %join.1), calls=%async_computation.1 | async-start | bytes 2097152 | tf_op jit(solution)/shard_map/all_to_all | solution.py:521
  89.5 9.1 %collective-permute-start.6 = (bf16[160,256]{1,0:T(8,128)(2,1)S(1)}, bf16[160,256]{1,0:T(8,128)(2,1)S(1)}, u32[]{:S(2)}, u32[]{:S(2)}) collective-permute-start(bf16[160,256]{1,0:T(8,128)(2,1)S(1)} %get-tuple-element.41), channel_id=1, source_target_pairs={{0,128},{128,0},{1,129},{129,1},{2,130},{130,2},{3,131},{131,3},{4... | collective-permute-start | bytes 245768 | tf_op jit(solution)/shard_map/ppermute | solution.py:393
  98.6 11.8 %copy-start.6 = (bf16[6144,128]{1,0:T(8,128)(2,1)S(1)}, bf16[6144,128]{1,0:T(8,128)(2,1)}, u32[]{:S(2)}) copy-start(bf16[6144,128]{1,0:T(8,128)(2,1)} %copy-done.5) | copy-start | bytes 4718596
  98.6 11.8 %copy-start.15 = (bf16[2048,128]{1,0:T(8,128)(2,1)S(1)}, bf16[2048,128]{1,0:T(8,128)(2,1)}, u32[]{:S(2)}) copy-start(bf16[2048,128]{1,0:T(8,128)(2,1)} %copy-done.14) | copy-start | bytes 1572868
  104.3 16.0 %all-to-all-start.2 = ((bf16[8,64,128]{2,1,0:T(8,128)(2,1)}), bf16[8,64,128]{2,1,0:T(8,128)(2,1)S(1)}, u32[]{:S(2)}, u32[]{:S(2)}) async-start(bf16[8,64,128]{2,1,0:T(8,128)(2,1)} %stage.1), calls=%async_computation.2 | async-start | bytes 262144 | tf_op jit(solution)/shard_map/all_to_all | solution.py:573
  121.2 17.9 %all-to-all-start.3 = ((bf16[32,64,128]{2,1,0:T(8,128)(2,1)}), bf16[32,64,128]{2,1,0:T(8,128)(2,1)S(1)}, u32[]{:S(2)}, u32[]{:S(2)}) async-start(bf16[32,64,128]{2,1,0:T(8,128)(2,1)} %last.1), calls=%async_computation.3 | async-start | bytes 1048576 | tf_op jit(solution)/shard_map/all_to_all | solution.py:577
  127.6 3.9 %collective-permute-start.7 = (bf16[128,256]{1,0:T(8,128)(2,1)S(1)}, bf16[128,256]{1,0:T(8,128)(2,1)S(1)}, u32[]{:S(2)}, u32[]{:S(2)}) collective-permute-start(bf16[128,256]{1,0:T(8,128)(2,1)S(1)} %get-tuple-element.43.refs_0_), channel_id=1, source_target_pairs={{0,1},{1,0},{2,3},{3,2},{4,5},{5,4},{6,7},{7,6},{8,9},{9,8},{10,11... | collective-permute-start | bytes 196616 | tf_op jit(solution)/shard_map/ppermute | solution.py:397
  129.3 4.5 %collective-permute-start.8 = (bf16[128,256]{1,0:T(8,128)(2,1)S(1)}, bf16[128,256]{1,0:T(8,128)(2,1)S(1)}, u32[]{:S(2)}, u32[]{:S(2)}) collective-permute-start(bf16[128,256]{1,0:T(8,128)(2,1)S(1)} %get-tuple-element.43.refs_0_), channel_id=1, source_target_pairs={{0,2},{1,3},{2,0},{3,1},{4,6},{5,7},{6,4},{7,5},{8,10},{9,11},{10,... | collective-permute-start | bytes 196616 | tf_op jit(solution)/shard_map/ppermute | solution.py:397
  131.4 5.2 %collective-permute-start.9 = (bf16[128,256]{1,0:T(8,128)(2,1)S(1)}, bf16[128,256]{1,0:T(8,128)(2,1)S(1)}, u32[]{:S(2)}, u32[]{:S(2)}) collective-permute-start(bf16[128,256]{1,0:T(8,128)(2,1)S(1)} %get-tuple-element.43.refs_0_), channel_id=1, source_target_pairs={{0,3},{1,2},{2,1},{3,0},{4,7},{5,6},{6,5},{7,4},{8,11},{9,10},{10,... | collective-permute-start | bytes 196616 | tf_op jit(solution)/shard_map/ppermute | solution.py:397
  (15 other events, 51.6 us)

commit v6 on v5

--- a/solution.py
+++ b/solution.py
@@ -338,13 +338,14 @@
     token_ref[...] = jnp.zeros_like(token_ref)
 
 
-def input_kernel(place, table, acc_in, *refs):
+def input_kernel(place, table, acc_hbm, *refs):
     from_hbm = refs[:5]
-    out_hbm, acc_ref, token_ref, gt_ref, values, out_ref, sems = refs[5:]
+    out_hbm, token_ref, acc_ref, gt_ref, values, out_ref, sems = refs[5:]
     most = from_hbm[0].shape[0]
     width = from_hbm[1].shape[0]
     to_vmem = [gt_ref.at[width:most], gt_ref.at[most:]] + [values.at[n] for n in range(T - 1)]
-    here = [from_hbm[0].at[width:], *from_hbm[1:]]
+    here = [from_hbm[0].at[width:], *from_hbm[1:], acc_hbm]
+    to_vmem.append(acc_ref)
     copies = [
         pltpu.make_async_copy(there, at, sems.at[n])
         for n, (there, at) in enumerate(zip(here, to_vmem))
@@ -371,7 +372,7 @@
             out_ref[:, i : i + 128] = acc_ref[i : i + 128, :].T.astype(BF16)
         at = pl.ds(j, step)
         gives.append(
-            pltpu.make_async_copy(out_ref.at[:, at], out_hbm.at[:, at], sems.at[5 + j // step])
+            pltpu.make_async_copy(out_ref.at[:, at], out_hbm.at[:, at], sems.at[6 + j // step])
         )
         gives[-1].start()
     for give in gives:
@@ -549,19 +550,19 @@
         pass_kernel, "values", (shape(packed.shape, BF16),) * 3, [anywhere()] * 3, *got,
         out_specs=(anywhere(),) * 3, input_output_aliases={0: 0, 1: 1, 2: 2},
     )
-    grad_input, _, token = call(
+    grad_input, token = call(
         input_kernel, "grad_input",
-        (shape((TOK, feat), BF16), shape((feat, TOK), F32), shape((8, 128), F32)),
-        [scalars()] * 2 + [whole()] + [anywhere()] * 5,
+        (shape((TOK, feat), BF16), shape((8, 128), F32)),
+        [scalars()] * 2 + [anywhere()] * 6,
         place, table, acc, grad_most, grad_last, *got, room=24,
-        out_specs=(anywhere(), whole(), whole()),
+        out_specs=(anywhere(), whole()),
         scratch=[
+            pltpu.VMEM((feat, TOK), F32),
             pltpu.VMEM((T * width, TOK), BF16),
             pltpu.VMEM((T - 1, PAIRS, BLK, 2 * BLK), BF16),
             pltpu.VMEM((TOK, feat), BF16),
-            pltpu.SemaphoreType.DMA((5 + feat // 1024,)),
+            pltpu.SemaphoreType.DMA((6 + feat // 1024,)),
         ],
-        input_output_aliases={2: 1},
     )
 
     stage = call(

time: 142 us -> 140 us (0.986)
  starting transfers between devices: 58.1 us -> 56.6 us
  transfers between devices with their start and end apart: 24 -> 24, of which waited for: 7 -> 8; matrix products, arithmetic and copies ran while one was open for 0% -> 0% of each run, Pallas kernels for 22% -> 22%
where the time goes in v6:
time: 140 us
  starting transfers between devices  56.6 us (40%)
  Pallas kernels  41 us (29%)
  waiting for transfers between devices  28 us (20%)
  local copies, waits for them, and re-layouts  12.3 us (9%)
  between operations  1.66 us (1%)
    pallas_call x19, Pallas kernels, call(): pl.pallas_call(kernel, out_shape=outs, in_specs=in_specs, out_specs=out_s...  41 us
    ppermute x9, starting transfers between devices, cross(): return lax.ppermute(array, 't', [(i, i ^ k) for i in range(T)])  12.7 us
    ppermute x9, waiting for transfers between devices, cross(): return lax.ppermute(array, 't', [(i, i ^ k) for i in range(T)])  11.7 us
    unnamed x46, local copies, waits for them, and re-layouts  11.7 us
    ppermute x1, waiting for transfers between devices, per_device(): lax.ppermute(packed, ('zh', 'c', 't'), ring((2, -2)))  9.94 us
    ppermute x8, starting transfers between devices, swap(): return lax.ppermute(array, axis, [(0, 1), (1, 0)])  9.07 us
    all_to_all x1, starting transfers between devices, per_device(): down_all = lax.all_to_all(down_part, ('y', 'x'), 0, 0, tiled=True)  6.92 us
    all_to_all x1, starting transfers between devices, per_device(): delta_all = lax.all_to_all(delta_part, ('y', 'x'), 0, 0, tiled=True)  6.76 us
  transfers between devices with their start and end apart: 24, of which 8 were waited for; matrix products, arithmetic and copies ran while one was open for 0% of the time, Pallas kernels for 22%

profile of v6, /device:TPU:1, one launch (start us, length us, event | category | flops | bytes accessed | tf_op | source)
XLA Modules:
  0.0 139.6 jit_solution(382659615130995373)
XLA Ops:
  1.9 4.2 %front.1 = (bf16[144,256]{1,0:T(8,128)(2,1)}, bf16[144,256]{1,0:T(8,128)(2,1)}, bf16[144,256]{1,0:T(8,128)(2,1)}, bf16[144,256]{1,0:T(8,128)(2,1)}, bf16[128,204...) custom-call(s32[6]{0:T(128)} %stack.23.place, ...), custom_call_target="tpu_custom_call" | custom-call | flops 1024 | bytes 1024 | tf_op jit(solution)/shard_map/front/pallas_call | solution.py:402
  8.5 3.3 %collective-permute-start = (bf16[8192,128]{1,0:T(8,128)(2,1)S(1)}, bf16[8192,128]{1,0:T(8,128)(2,1)S(1)}, u32[]{:S(2)}, u32[]{:S(2)}) collective-permute-start(bf16[8192,128]{1,0:T(8,128)(2,1)S(1)} %turn_input.1.xt_ref), channel_id=1, source_target_pairs={{0,4},{4,0},{1,5},{5,1},{2,6},{6,2},{3,7},{7,3},{8,12},{12,8},{9,1... | collective-permute-start | bytes 6291464 | tf_op jit(solution)/shard_map/ppermute | solution.py:394
  11.8 2.9 %collective-permute-start.2 = (bf16[144,256]{1,0:T(8,128)(2,1)S(1)}, bf16[144,256]{1,0:T(8,128)(2,1)S(1)}, u32[]{:S(2)}, u32[]{:S(2)}) collective-permute-start(bf16[144,256]{1,0:T(8,128)(2,1)S(1)} %copy-done.21), channel_id=1, source_target_pairs={{0,2},{1,3},{2,0},{3,1},{4,6},{5,7},{6,4},{7,5},{8,10},{9,11},{10,... | collective-permute-start | bytes 221192 | tf_op jit(solution)/shard_map/ppermute | solution.py:398
  15.4 1.9 %up_part.1 = (f32[128,2048]{1,0:T(8,128)S(1)}, bf16[128,2048]{1,0:T(8,128)(2,1)S(1)}) custom-call(s32[6]{0:T(128)S(1)} %copy-done.17, bf16[512,2048]{1,0:T(8,128)(2,1)S(1)} %copy-done.4, bf16[512,256]{1,0:T(8,128)(2,1)S(1)} %copy-done.16), custom_call_target="tpu_custom_call" | custom-call | flops 1024 | bytes 1024 | tf_op jit(solution)/shard_map/up_part/pallas_call | solution.py:402
  17.3 3.0 %collective-permute-start.12 = (bf16[128,2048]{1,0:T(8,128)(2,1)S(1)}, bf16[128,2048]{1,0:T(8,128)(2,1)}, u32[]{:S(2)}, u32[]{:S(2)}) collective-permute-start(bf16[128,2048]{1,0:T(8,128)(2,1)S(1)} %copy-done.19), channel_id=1, source_target_pairs={{0,2},{1,3},{2,0},{3,1},{4,6},{5,7},{6,4},{7,5},{8,10},{9,11},{10,... | collective-permute-start | bytes 1572872 | tf_op jit(solution)/shard_map/ppermute | solution.py:398
  23.4 2.3 %down_part.1 = bf16[16,320,256]{2,1,0:T(8,128)(2,1)S(1)} custom-call(s32[6]{0:T(128)S(1)} %copy-done.17, bf16[8192,128]{1,0:T(8,128)(2,1)S(1)} %turn_input.1.xt_ref, bf16[8192,128]{1,0:T(8,128)(2,1)S(1)} %collective-permute-done.xt_far_ref, bf16[128,256]{1,0:T(8,128)(2,1)S(1)} %get-tuple-element.38.low_ref, ...), custom_call_target="tpu_custom_call" | custom-call | flops 1024 | bytes 1024 | tf_op jit(solution)/shard_map/down_part/pallas_call | solution.py:402
  27.1 1.6 %copy-done.3 = bf16[16,320,256]{2,1,0:T(8,128)(2,1)} copy-done((bf16[16,320,256]{2,1,0:T(8,128)(2,1)}, bf16[16,320,256]{2,1,0:T(8,128)(2,1)S(1)}, u32[]{:S(2)}) %copy-start.3) | copy-done | bytes 2621464
  28.6 6.9 %all-to-all-start = ((bf16[16,320,256]{2,1,0:T(8,128)(2,1)}), bf16[16,320,256]{2,1,0:T(8,128)(2,1)}, u32[]{:S(2)}, u32[]{:S(2)}) async-start(bf16[16,320,256]{2,1,0:T(8,128)(2,1)} %copy-done.3), calls=%async_computation | async-start | bytes 5242880 | tf_op jit(solution)/shard_map/all_to_all | solution.py:475
  36.3 4.3 %collective-permute-done.11.refs_1_ = bf16[128,2048]{1,0:T(8,128)(2,1)} collective-permute-done((bf16[128,2048]{1,0:T(8,128)(2,1)}, bf16[128,2048]{1,0:T(8,128)(2,1)}, u32[]{:S(2)}, u32[]{:S(2)}) %collective-permute-start.11) | collective-permute-done | bytes 524320 | tf_op jit(solution)/shard_map/ppermute | solution.py:398
  41.9 2.3 %collective-permute-done.12.refs_2_ = bf16[128,2048]{1,0:T(8,128)(2,1)} collective-permute-done((bf16[128,2048]{1,0:T(8,128)(2,1)S(1)}, bf16[128,2048]{1,0:T(8,128)(2,1)}, u32[]{:S(2)}, u32[]{:S(2)}) %collective-permute-start.12) | collective-permute-done | bytes 524320 | tf_op jit(solution)/shard_map/ppermute | solution.py:398
  45.3 2.2 %collective-permute-start.10 = (bf16[128,2048]{1,0:T(8,128)(2,1)}, bf16[128,2048]{1,0:T(8,128)(2,1)S(1)}, u32[]{:S(2)}, u32[]{:S(2)}) collective-permute-start(bf16[128,2048]{1,0:T(8,128)(2,1)} %get-tuple-element.46), channel_id=1, source_target_pairs={{0,3},{1,2},{2,1},{3,0},{4,7},{5,6},{6,5},{7,4},{8,11},{9,10},{10,... | collective-permute-start | bytes 1572872 | tf_op jit(solution)/shard_map/ppermute | solution.py:398
  49.5 1.6 %copy-done.1 = bf16[8192,128]{1,0:T(8,128)(2,1)S(1)} copy-done((bf16[8192,128]{1,0:T(8,128)(2,1)S(1)}, bf16[8192,128]{1,0:T(8,128)(2,1)}, u32[]{:S(2)}) %copy-start.1) | copy-done | bytes 2097176
  51.0 5.5 %delta_most.1 = (bf16[16,4,64,128]{3,2,1,0:T(8,128)(2,1)}, bf16[6144,128]{1,0:T(8,128)(2,1)S(1)}) custom-call(s32[6]{0:T(128)S(1)} %copy-done.17, s32[32,256]{1,0:T(8,128)S(1)} %get-tuple-element.45.table, bf16[8192,128]{1,0:T(8,128)(2,1)S(1)} %turn_input.1.xt_ref, bf16[8192,128]{1,0:T(8,128)(2,1)S(1)} %copy-done.1, bf16[128,2048]{1,0:T(8,128)(2,1)S(1)} %copy-done.12, ...), custom_call_target="tpu_custom_call" | custom-call | flops 1024 | bytes 1024 | tf_op jit(solution)/shard_map/delta_most/pallas_call | solution.py:402
  56.5 6.4 %dense.1 = (f32[8192,128]{1,0:T(8,128)S(1)}, f32[8,128]{1,0:T(8,128)S(1)}) custom-call(s32[32,256]{1,0:T(8,128)S(1)} %get-tuple-element.45.table, bf16[128,256]{1,0:T(8,128)(2,1)S(1)} %get-tuple-element.38.low_ref, bf16[8192,256]{1,0:T(8,128)(2,1)S(1)} %copy-done.7, bf16[6144,128]{1,0:T(8,128)(2,1)S(1)} %get-tuple-element.49.gt_hbm.refs_0_, ...), custom_call_target="tpu_custom_call" | custom-call | flops 1024 | bytes 1024 | tf_op jit(solution)/shard_map/dense/pallas_call | solution.py:402
  63.0 2.0 %copy-done.8 = f32[8192,128]{1,0:T(8,128)} copy-done((f32[8192,128]{1,0:T(8,128)}, f32[8192,128]{1,0:T(8,128)S(1)}, u32[]{:S(2)}) %copy-start.8) | copy-done | bytes 4194328
  65.3 5.1 %collective-permute-start.17 = (bf16[32,64,128]{2,1,0:T(8,128)(2,1)S(1)}, bf16[32,64,128]{2,1,0:T(8,128)(2,1)}, u32[]{:S(2)}, u32[]{:S(2)}) collective-permute-start(bf16[32,64,128]{2,1,0:T(8,128)(2,1)S(1)} %pack.1.own_hbm), channel_id=1, source_target_pairs={{0,1},{1,2},{2,3},{3,128},{128,129},{129,130},{130,131},{131,0},{4... | collective-permute-start | bytes 1572872 | tf_op jit(solution)/shard_map/ppermute | solution.py:545
  70.4 4.6 %collective-permute-start.19 = (bf16[32,64,128]{2,1,0:T(8,128)(2,1)S(1)}, bf16[32,64,128]{2,1,0:T(8,128)(2,1)}, u32[]{:S(2)}, u32[]{:S(2)}) collective-permute-start(bf16[32,64,128]{2,1,0:T(8,128)(2,1)S(1)} %pack.1.own_hbm), channel_id=1, source_target_pairs={{0,2},{4,134},{1,3},{5,135},{2,128},{6,4},{3,129},{7,5},{128,130},... | collective-permute-start | bytes 1572872 | tf_op jit(solution)/shard_map/ppermute | solution.py:547
  75.0 3.3 %delta_last.1 = (bf16[16,4,64,128]{3,2,1,0:T(8,128)(2,1)}, bf16[2048,128]{1,0:T(8,128)(2,1)S(1)}) custom-call(s32[6]{0:T(128)S(1)} %copy-done.17, s32[32,256]{1,0:T(8,128)S(1)} %get-tuple-element.45.table, bf16[8192,128]{1,0:T(8,128)(2,1)S(1)} %turn_input.1.xt_ref, bf16[8192,128]{1,0:T(8,128)(2,1)S(1)} %copy-done.2, ...), custom_call_target="tpu_custom_call", output_to_operand_aliasing={{0}: (6, {})} | custom-call | flops 1024 | bytes 1024 | tf_op jit(solution)/shard_map/delta_last/pallas_call | solution.py:402
  79.1 6.8 %all-to-all-start.1 = ((bf16[16,4,64,128]{3,2,1,0:T(8,128)(2,1)}), bf16[16,4,64,128]{3,2,1,0:T(8,128)(2,1)S(1)}, u32[]{:S(2)}, u32[]{:S(2)}) async-start(bf16[16,4,64,128]{3,2,1,0:T(8,128)(2,1)} %join.1), calls=%async_computation.1 | async-start | bytes 2097152 | tf_op jit(solution)/shard_map/all_to_all | solution.py:522
  85.9 2.1 %down_sum.1 = (f32[128,256]{1,0:T(8,128)S(1)}, bf16[160,256]{1,0:T(8,128)(2,1)S(1)}, f32[4,2048]{1,0:T(4,128)S(1)}) custom-call(s32[6]{0:T(128)S(1)} %copy-done.17, bf16[16,320,256]{2,1,0:T(8,128)(2,1)} %all-to-all-done.down_ref.refs_1_), custom_call_target="tpu_custom_call" | custom-call | flops 1024 | bytes 1024 | tf_op jit(solution)/shard_map/down_sum/pallas_call | solution.py:402
  88.3 9.9 %collective-permute-done.19.refs_2_ = bf16[32,64,128]{2,1,0:T(8,128)(2,1)} collective-permute-done((bf16[32,64,128]{2,1,0:T(8,128)(2,1)S(1)}, bf16[32,64,128]{2,1,0:T(8,128)(2,1)}, u32[]{:S(2)}, u32[]{:S(2)}) %collective-permute-start.19) | collective-permute-done | bytes 524320 | tf_op jit(solution)/shard_map/ppermute | solution.py:547
  98.9 3.5 %all-to-all-done.1.delta_ref = bf16[16,4,64,128]{3,2,1,0:T(8,128)(2,1)S(1)} async-done(((bf16[16,4,64,128]{3,2,1,0:T(8,128)(2,1)}), bf16[16,4,64,128]{3,2,1,0:T(8,128)(2,1)S(1)}, u32[]{:S(2)}, u32[]{:S(2)}) %all-to-all-start.1) | async-done | bytes 1048608 | tf_op jit(solution)/shard_map/all_to_all | solution.py:522
  103.7 5.6 %all-to-all-start.2 = ((bf16[8,64,128]{2,1,0:T(8,128)(2,1)}), bf16[8,64,128]{2,1,0:T(8,128)(2,1)S(1)}, u32[]{:S(2)}, u32[]{:S(2)}) async-start(bf16[8,64,128]{2,1,0:T(8,128)(2,1)} %stage.1), calls=%async_computation.2 | async-start | bytes 262144 | tf_op jit(solution)/shard_map/all_to_all | solution.py:574
  109.3 2.2 %copy-done.9 = f32[8192,128]{1,0:T(8,128)S(1)} copy-done((f32[8192,128]{1,0:T(8,128)S(1)}, f32[8192,128]{1,0:T(8,128)}, u32[]{:S(2)}) %copy-start.9) | copy-done | bytes 4194328
  111.5 7.8 %grad_input.1 = (bf16[128,8192]{1,0:T(8,128)(2,1)}, f32[8,128]{1,0:T(8,128)S(1)}) custom-call(s32[6]{0:T(128)S(1)} %copy-done.17, s32[32,256]{1,0:T(8,128)S(1)} %get-tuple-element.45.table, f32[8192,128]{1,0:T(8,128)S(1)} %copy-done.9, bf16[6144,128]{1,0:T(8,128)(2,1)S(1)} %copy-done.6, bf16[2048,128]{1,0:T(8,128)(2,1)S(1)} %copy-done.15, ...), custom_call_target="tpu_custom_call" | custom-call | flops 1024 | bytes 1024 | tf_op jit(solution)/shard_map/grad_input/pallas_call | solution.py:402
  120.1 5.9 %all-to-all-start.3 = ((bf16[32,64,128]{2,1,0:T(8,128)(2,1)}), bf16[32,64,128]{2,1,0:T(8,128)(2,1)S(1)}, u32[]{:S(2)}, u32[]{:S(2)}) async-start(bf16[32,64,128]{2,1,0:T(8,128)(2,1)} %last.1), calls=%async_computation.3 | async-start | bytes 1048576 | tf_op jit(solution)/shard_map/all_to_all | solution.py:578
  126.1 1.7 %collective-permute-start.7 = (bf16[128,256]{1,0:T(8,128)(2,1)S(1)}, bf16[128,256]{1,0:T(8,128)(2,1)S(1)}, u32[]{:S(2)}, u32[]{:S(2)}) collective-permute-start(bf16[128,256]{1,0:T(8,128)(2,1)S(1)} %get-tuple-element.43.refs_0_), channel_id=1, source_target_pairs={{0,1},{1,0},{2,3},{3,2},{4,5},{5,4},{6,7},{7,6},{8,9},{9,8},{10,11... | collective-permute-start | bytes 196616 | tf_op jit(solution)/shard_map/ppermute | solution.py:398
  127.8 2.1 %collective-permute-start.8 = (bf16[128,256]{1,0:T(8,128)(2,1)S(1)}, bf16[128,256]{1,0:T(8,128)(2,1)S(1)}, u32[]{:S(2)}, u32[]{:S(2)}) collective-permute-start(bf16[128,256]{1,0:T(8,128)(2,1)S(1)} %get-tuple-element.43.refs_0_), channel_id=1, source_target_pairs={{0,2},{1,3},{2,0},{3,1},{4,6},{5,7},{6,4},{7,5},{8,10},{9,11},{10,... | collective-permute-start | bytes 196616 | tf_op jit(solution)/shard_map/ppermute | solution.py:398
  130.0 2.3 %collective-permute-done.8.refs_2_ = bf16[128,256]{1,0:T(8,128)(2,1)S(1)} collective-permute-done((bf16[128,256]{1,0:T(8,128)(2,1)S(1)}, bf16[128,256]{1,0:T(8,128)(2,1)S(1)}, u32[]{:S(2)}, u32[]{:S(2)}) %collective-permute-start.8) | collective-permute-done | bytes 65568 | tf_op jit(solution)/shard_map/ppermute | solution.py:398
  132.3 2.8 %collective-permute-done.9.refs_3_ = bf16[128,256]{1,0:T(8,128)(2,1)S(1)} collective-permute-done((bf16[128,256]{1,0:T(8,128)(2,1)S(1)}, bf16[128,256]{1,0:T(8,128)(2,1)S(1)}, u32[]{:S(2)}, u32[]{:S(2)}) %collective-permute-start.9) | collective-permute-done | bytes 65568 | tf_op jit(solution)/shard_map/ppermute | solution.py:398
  135.8 1.8 %all-to-all-done.3.pairs_ref = bf16[32,64,128]{2,1,0:T(8,128)(2,1)S(1)} async-done(((bf16[32,64,128]{2,1,0:T(8,128)(2,1)}), bf16[32,64,128]{2,1,0:T(8,128)(2,1)S(1)}, u32[]{:S(2)}, u32[]{:S(2)}) %all-to-all-start.3) | async-done | bytes 524320 | tf_op jit(solution)/shard_map/all_to_all | solution.py:578
  137.6 2.0 %unpack.1 = f32[64,64,64]{2,1,0:T(8,128)} custom-call(bf16[32,64,128]{2,1,0:T(8,128)(2,1)S(1)} %all-to-all-done.3.pairs_ref), custom_call_target="tpu_custom_call" | custom-call | flops 1024 | bytes 1024 | tf_op jit(solution)/shard_map/unpack/pallas_call | solution.py:402
  (82 shorter events, 18.0 us)
Async XLA Ops:
  7.2 8.2 %copy-start.4 = (bf16[512,2048]{1,0:T(8,128)(2,1)S(1)}, bf16[512,2048]{1,0:T(8,128)(2,1)}, u32[]{:S(2)}) copy-start(bf16[512,2048]{1,0:T(8,128)(2,1)} %grad_hbm.1) | copy-start | bytes 6291460
  7.2 8.2 %copy-start.16 = (bf16[512,256]{1,0:T(8,128)(2,1)S(1)}, bf16[512,256]{1,0:T(8,128)(2,1)}, u32[]{:S(2)}) copy-start(bf16[512,256]{1,0:T(8,128)(2,1)} %acts_hbm.1) | copy-start | bytes 786436
  7.2 8.2 %copy-start.17 = (s32[6]{0:T(128)S(1)}, s32[6]{0:T(128)}, u32[]{:S(2)}) copy-start(s32[6]{0:T(128)} %stack.23.place) | copy-start | bytes 76
  8.4 8.9 %copy-start.19 = (bf16[128,2048]{1,0:T(8,128)(2,1)S(1)}, bf16[128,2048]{1,0:T(8,128)(2,1)}, u32[]{:S(2)}) copy-start(bf16[128,2048]{1,0:T(8,128)(2,1)} %get-tuple-element.48) | copy-start | bytes 1572868
  8.5 13.3 %copy-start.18 = (bf16[144,256]{1,0:T(8,128)(2,1)S(1)}, bf16[144,256]{1,0:T(8,128)(2,1)}, u32[]{:S(2)}) copy-start(bf16[144,256]{1,0:T(8,128)(2,1)} %get-tuple-element.33.refs_0_) | copy-start | bytes 221188
  8.5 15.0 %collective-permute-start = (bf16[8192,128]{1,0:T(8,128)(2,1)S(1)}, bf16[8192,128]{1,0:T(8,128)(2,1)S(1)}, u32[]{:S(2)}, u32[]{:S(2)}) collective-permute-start(bf16[8192,128]{1,0:T(8,128)(2,1)S(1)} %turn_input.1.xt_ref), channel_id=1, source_target_pairs={{0,4},{4,0},{1,5},{5,1},{2,6},{6,2},{3,7},{7,3},{8,12},{12,8},{9,1... | collective-permute-start | bytes 6291464 | tf_op jit(solution)/shard_map/ppermute | solution.py:394
  11.8 5.5 %collective-permute-start.1 = (bf16[144,256]{1,0:T(8,128)(2,1)S(1)}, bf16[144,256]{1,0:T(8,128)(2,1)S(1)}, u32[]{:S(2)}, u32[]{:S(2)}) collective-permute-start(bf16[144,256]{1,0:T(8,128)(2,1)S(1)} %copy-done.22), channel_id=1, source_target_pairs={{0,1},{1,0},{2,3},{3,2},{4,5},{5,4},{6,7},{7,6},{8,9},{9,8},{10,11... | collective-permute-start | bytes 221192 | tf_op jit(solution)/shard_map/ppermute | solution.py:398
  11.8 8.5 %collective-permute-start.2 = (bf16[144,256]{1,0:T(8,128)(2,1)S(1)}, bf16[144,256]{1,0:T(8,128)(2,1)S(1)}, u32[]{:S(2)}, u32[]{:S(2)}) collective-permute-start(bf16[144,256]{1,0:T(8,128)(2,1)S(1)} %copy-done.21), channel_id=1, source_target_pairs={{0,2},{1,3},{2,0},{3,1},{4,6},{5,7},{6,4},{7,5},{8,10},{9,11},{10,... | collective-permute-start | bytes 221192 | tf_op jit(solution)/shard_map/ppermute | solution.py:398
  14.7 7.1 %collective-permute-start.3 = (bf16[144,256]{1,0:T(8,128)(2,1)S(1)}, bf16[144,256]{1,0:T(8,128)(2,1)S(1)}, u32[]{:S(2)}, u32[]{:S(2)}) collective-permute-start(bf16[144,256]{1,0:T(8,128)(2,1)S(1)} %copy-done.20), channel_id=1, source_target_pairs={{0,3},{1,2},{2,1},{3,0},{4,7},{5,6},{6,5},{7,4},{8,11},{9,10},{10,... | collective-permute-start | bytes 221192 | tf_op jit(solution)/shard_map/ppermute | solution.py:398
  15.4 25.2 %collective-permute-start.11 = (bf16[128,2048]{1,0:T(8,128)(2,1)}, bf16[128,2048]{1,0:T(8,128)(2,1)}, u32[]{:S(2)}, u32[]{:S(2)}) collective-permute-start(bf16[128,2048]{1,0:T(8,128)(2,1)} %get-tuple-element.47), channel_id=1, source_target_pairs={{0,1},{1,0},{2,3},{3,2},{4,5},{5,4},{6,7},{7,6},{8,9},{9,8},{10,11... | collective-permute-start | bytes 1572872 | tf_op jit(solution)/shard_map/ppermute | solution.py:398
  17.3 26.9 %collective-permute-start.12 = (bf16[128,2048]{1,0:T(8,128)(2,1)S(1)}, bf16[128,2048]{1,0:T(8,128)(2,1)}, u32[]{:S(2)}, u32[]{:S(2)}) collective-permute-start(bf16[128,2048]{1,0:T(8,128)(2,1)S(1)} %copy-done.19), channel_id=1, source_target_pairs={{0,2},{1,3},{2,0},{3,1},{4,6},{5,7},{6,4},{7,5},{8,10},{9,11},{10,... | collective-permute-start | bytes 1572872 | tf_op jit(solution)/shard_map/ppermute | solution.py:398
  20.3 3.1 %collective-permute-start.5 = (bf16[128,2048]{1,0:T(8,128)(2,1)S(1)}, bf16[128,2048]{1,0:T(8,128)(2,1)S(1)}, u32[]{:S(2)}, u32[]{:S(2)}) collective-permute-start(bf16[128,2048]{1,0:T(8,128)(2,1)S(1)} %get-tuple-element.37.refs_4_), channel_id=1, source_target_pairs={{0,4},{4,0},{1,5},{5,1},{2,6},{6,2},{3,7},{7,3},{8,12},{12,8},{9,1... | collective-permute-start | bytes 1572872 | tf_op jit(solution)/shard_map/ppermute | solution.py:394
  21.8 1.6 %collective-permute-start.4 = (bf16[128,256]{1,0:T(8,128)(2,1)S(1)}, bf16[128,256]{1,0:T(8,128)(2,1)S(1)}, u32[]{:S(2)}, u32[]{:S(2)}) collective-permute-start(bf16[128,256]{1,0:T(8,128)(2,1)S(1)} %get-tuple-element.38.low_ref), channel_id=1, source_target_pairs={{0,4},{4,0},{1,5},{5,1},{2,6},{6,2},{3,7},{7,3},{8,12},{12,8},{9,1... | collective-permute-start | bytes 196616 | tf_op jit(solution)/shard_map/ppermute | solution.py:394
  28.6 49.7 %all-to-all-start = ((bf16[16,320,256]{2,1,0:T(8,128)(2,1)}), bf16[16,320,256]{2,1,0:T(8,128)(2,1)}, u32[]{:S(2)}, u32[]{:S(2)}) async-start(bf16[16,320,256]{2,1,0:T(8,128)(2,1)} %copy-done.3), calls=%async_computation | async-start | bytes 5242880 | tf_op jit(solution)/shard_map/all_to_all | solution.py:475
  35.6 13.8 %collective-permute-start.13 = (bf16[128,2048]{1,0:T(8,128)(2,1)S(1)}, bf16[128,2048]{1,0:T(8,128)(2,1)S(1)}, u32[]{:S(2)}, u32[]{:S(2)}) collective-permute-start(bf16[128,2048]{1,0:T(8,128)(2,1)S(1)} %copy-done.12), channel_id=1, source_target_pairs={{0,4},{4,0},{1,5},{5,1},{2,6},{6,2},{3,7},{7,3},{8,12},{12,8},{9,1... | collective-permute-start | bytes 1572872 | tf_op jit(solution)/shard_map/ppermute | solution.py:394
  40.6 8.8 %collective-permute-start.14 = (bf16[128,2048]{1,0:T(8,128)(2,1)}, bf16[128,2048]{1,0:T(8,128)(2,1)S(1)}, u32[]{:S(2)}, u32[]{:S(2)}) collective-permute-start(bf16[128,2048]{1,0:T(8,128)(2,1)} %collective-permute-done.11.refs_1_), channel_id=1, source_target_pairs={{0,4},{4,0},{1,5},{5,1},{2,6},{6,2},{3,7},{7,3},{8,12},{12,8},{9,1... | collective-permute-start | bytes 1572872 | tf_op jit(solution)/shard_map/ppermute | solution.py:394
  44.2 5.2 %collective-permute-start.15 = (bf16[128,2048]{1,0:T(8,128)(2,1)}, bf16[128,2048]{1,0:T(8,128)(2,1)S(1)}, u32[]{:S(2)}, u32[]{:S(2)}) collective-permute-start(bf16[128,2048]{1,0:T(8,128)(2,1)} %collective-permute-done.12.refs_2_), channel_id=1, source_target_pairs={{0,4},{4,0},{1,5},{5,1},{2,6},{6,2},{3,7},{7,3},{8,12},{12,8},{9,1... | collective-permute-start | bytes 1572872 | tf_op jit(solution)/shard_map/ppermute | solution.py:394
  45.3 19.7 %collective-permute-start.10 = (bf16[128,2048]{1,0:T(8,128)(2,1)}, bf16[128,2048]{1,0:T(8,128)(2,1)S(1)}, u32[]{:S(2)}, u32[]{:S(2)}) collective-permute-start(bf16[128,2048]{1,0:T(8,128)(2,1)} %get-tuple-element.46), channel_id=1, source_target_pairs={{0,3},{1,2},{2,1},{3,0},{4,7},{5,6},{6,5},{7,4},{8,11},{9,10},{10,... | collective-permute-start | bytes 1572872 | tf_op jit(solution)/shard_map/ppermute | solution.py:398
  65.0 10.0 %copy-start.2 = (bf16[8192,128]{1,0:T(8,128)(2,1)S(1)}, bf16[8192,128]{1,0:T(8,128)(2,1)}, u32[]{:S(2)}) copy-start(bf16[8192,128]{1,0:T(8,128)(2,1)} %copy-done) | copy-start | bytes 6291460
  65.0 10.0 %collective-permute-start.16 = (bf16[128,2048]{1,0:T(8,128)(2,1)S(1)}, bf16[128,2048]{1,0:T(8,128)(2,1)S(1)}, u32[]{:S(2)}, u32[]{:S(2)}) collective-permute-start(bf16[128,2048]{1,0:T(8,128)(2,1)S(1)} %gate.1.refs_0_), channel_id=1, source_target_pairs={{0,4},{4,0},{1,5},{5,1},{2,6},{6,2},{3,7},{7,3},{8,12},{12,8},{9,1... | collective-permute-start | bytes 1572872 | tf_op jit(solution)/shard_map/ppermute | solution.py:394
  65.3 23.0 %collective-permute-start.17 = (bf16[32,64,128]{2,1,0:T(8,128)(2,1)S(1)}, bf16[32,64,128]{2,1,0:T(8,128)(2,1)}, u32[]{:S(2)}, u32[]{:S(2)}) collective-permute-start(bf16[32,64,128]{2,1,0:T(8,128)(2,1)S(1)} %pack.1.own_hbm), channel_id=1, source_target_pairs={{0,1},{1,2},{2,3},{3,128},{128,129},{129,130},{130,131},{131,0},{4... | collective-permute-start | bytes 1572872 | tf_op jit(solution)/shard_map/ppermute | solution.py:545
  70.4 17.9 %collective-permute-start.18 = (bf16[32,64,128]{2,1,0:T(8,128)(2,1)S(1)}, bf16[32,64,128]{2,1,0:T(8,128)(2,1)}, u32[]{:S(2)}, u32[]{:S(2)}) collective-permute-start(bf16[32,64,128]{2,1,0:T(8,128)(2,1)S(1)} %pack.1.own_hbm), channel_id=1, source_target_pairs={{0,131},{1,0},{2,1},{3,2},{128,3},{129,128},{130,129},{131,130},{4... | collective-permute-start | bytes 1572872 | tf_op jit(solution)/shard_map/ppermute | solution.py:546
  70.4 27.8 %collective-permute-start.19 = (bf16[32,64,128]{2,1,0:T(8,128)(2,1)S(1)}, bf16[32,64,128]{2,1,0:T(8,128)(2,1)}, u32[]{:S(2)}, u32[]{:S(2)}) collective-permute-start(bf16[32,64,128]{2,1,0:T(8,128)(2,1)S(1)} %pack.1.own_hbm), channel_id=1, source_target_pairs={{0,2},{4,134},{1,3},{5,135},{2,128},{6,4},{3,129},{7,5},{128,130},... | collective-permute-start | bytes 1572872 | tf_op jit(solution)/shard_map/ppermute | solution.py:547
  79.1 23.2 %all-to-all-start.1 = ((bf16[16,4,64,128]{3,2,1,0:T(8,128)(2,1)}), bf16[16,4,64,128]{3,2,1,0:T(8,128)(2,1)S(1)}, u32[]{:S(2)}, u32[]{:S(2)}) async-start(bf16[16,4,64,128]{3,2,1,0:T(8,128)(2,1)} %join.1), calls=%async_computation.1 | async-start | bytes 2097152 | tf_op jit(solution)/shard_map/all_to_all | solution.py:522
  88.0 10.2 %collective-permute-start.6 = (bf16[160,256]{1,0:T(8,128)(2,1)S(1)}, bf16[160,256]{1,0:T(8,128)(2,1)S(1)}, u32[]{:S(2)}, u32[]{:S(2)}) collective-permute-start(bf16[160,256]{1,0:T(8,128)(2,1)S(1)} %get-tuple-element.41), channel_id=1, source_target_pairs={{0,128},{128,0},{1,129},{129,1},{2,130},{130,2},{3,131},{131,3},{4... | collective-permute-start | bytes 245768 | tf_op jit(solution)/shard_map/ppermute | solution.py:394
  98.2 11.1 %copy-start.6 = (bf16[6144,128]{1,0:T(8,128)(2,1)S(1)}, bf16[6144,128]{1,0:T(8,128)(2,1)}, u32[]{:S(2)}) copy-start(bf16[6144,128]{1,0:T(8,128)(2,1)} %copy-done.5) | copy-start | bytes 4718596
  98.2 11.1 %copy-start.15 = (bf16[2048,128]{1,0:T(8,128)(2,1)S(1)}, bf16[2048,128]{1,0:T(8,128)(2,1)}, u32[]{:S(2)}) copy-start(bf16[2048,128]{1,0:T(8,128)(2,1)} %copy-done.14) | copy-start | bytes 1572868
  103.7 15.6 %all-to-all-start.2 = ((bf16[8,64,128]{2,1,0:T(8,128)(2,1)}), bf16[8,64,128]{2,1,0:T(8,128)(2,1)S(1)}, u32[]{:S(2)}, u32[]{:S(2)}) async-start(bf16[8,64,128]{2,1,0:T(8,128)(2,1)} %stage.1), calls=%async_computation.2 | async-start | bytes 262144 | tf_op jit(solution)/shard_map/all_to_all | solution.py:574
  120.1 17.5 %all-to-all-start.3 = ((bf16[32,64,128]{2,1,0:T(8,128)(2,1)}), bf16[32,64,128]{2,1,0:T(8,128)(2,1)S(1)}, u32[]{:S(2)}, u32[]{:S(2)}) async-start(bf16[32,64,128]{2,1,0:T(8,128)(2,1)} %last.1), calls=%async_computation.3 | async-start | bytes 1048576 | tf_op jit(solution)/shard_map/all_to_all | solution.py:578
  126.1 3.9 %collective-permute-start.7 = (bf16[128,256]{1,0:T(8,128)(2,1)S(1)}, bf16[128,256]{1,0:T(8,128)(2,1)S(1)}, u32[]{:S(2)}, u32[]{:S(2)}) collective-permute-start(bf16[128,256]{1,0:T(8,128)(2,1)S(1)} %get-tuple-element.43.refs_0_), channel_id=1, source_target_pairs={{0,1},{1,0},{2,3},{3,2},{4,5},{5,4},{6,7},{7,6},{8,9},{9,8},{10,11... | collective-permute-start | bytes 196616 | tf_op jit(solution)/shard_map/ppermute | solution.py:398
  127.8 4.5 %collective-permute-start.8 = (bf16[128,256]{1,0:T(8,128)(2,1)S(1)}, bf16[128,256]{1,0:T(8,128)(2,1)S(1)}, u32[]{:S(2)}, u32[]{:S(2)}) collective-permute-start(bf16[128,256]{1,0:T(8,128)(2,1)S(1)} %get-tuple-element.43.refs_0_), channel_id=1, source_target_pairs={{0,2},{1,3},{2,0},{3,1},{4,6},{5,7},{6,4},{7,5},{8,10},{9,11},{10,... | collective-permute-start | bytes 196616 | tf_op jit(solution)/shard_map/ppermute | solution.py:398
  129.9 5.2 %collective-permute-start.9 = (bf16[128,256]{1,0:T(8,128)(2,1)S(1)}, bf16[128,256]{1,0:T(8,128)(2,1)S(1)}, u32[]{:S(2)}, u32[]{:S(2)}) collective-permute-start(bf16[128,256]{1,0:T(8,128)(2,1)S(1)} %get-tuple-element.43.refs_0_), channel_id=1, source_target_pairs={{0,3},{1,2},{2,1},{3,0},{4,7},{5,6},{6,5},{7,4},{8,11},{9,10},{10,... | collective-permute-start | bytes 196616 | tf_op jit(solution)/shard_map/ppermute | solution.py:398
  (15 other events, 51.6 us)
